TPU v7x, 256 devices: a whole 4x4x8 slice. The times are simulated.
256 devices in a mesh: tile: 64 (over y, z, core), head: 4 (over x).
Axes of the slice: x: 4, y: 4, z: 8, core: 2. Of those that a mesh axis runs over, the one named last changes fastest.
Arguments:
- tokens: bfloat16 [256, 262144], P('head', 'tile'), may hold values from -6 to 6
- grad_in: bfloat16 [256, 262144], P('head', 'tile'), may hold values from -6 to 6
- w_qkv: bfloat16 [3, 256, 256], P(None, 'head'), may hold values from -0.375 to 0.375
- w_out: bfloat16 [256, 256], P('head'), may hold values from -0.375 to 0.375
- neighbors: int32 [9, 262144], P(None, 'tile'), may hold values from 0 to 4479, as said below
- send_rows: int32 [64, 3, 128], P('tile'), may hold values from 0 to 4096, as said below
Outputs:
- d_tokens: float32 [256, 262144], P('head', 'tile')
- grad_qkv: float32 [3, 256, 256], P(None, 'head')
- grad_out: float32 [256, 256], P('head')
Inputs may be any that keep to these rules, and one draw needn't show every extreme that they name: `send_rows`: entries of list p of index d are rows of index d, live entries first, the rest equal to 4096; list 2 of every index is full, and list 0 of index 0 is half full. `neighbors`: slot 0 of row r of an index is r itself; an entry below 4096 lies within 64 rows of r, counted around the index's 4096 rows; every entry at or above 4096 points to a live entry of the list it names.
All inputs are finite; a program needn't handle non-finite values.
Results may differ from a plain program's by a relative error of at most 0.0059.
Values may be sent and summed in bfloat16 or wider, within the bound.
No kernel may reach another device: no remote copies, remote signals or barrier semaphores. Data moves between devices by JAX's collectives and lax.ppermute only.
A program may use at most 64 MiB of HBM per device.

v0:
```python
import math

import jax
import jax.numpy as jnp
from jax import lax
from jax.sharding import PartitionSpec as P

C = 256
HEADS = 8
NBR = 9


def passed_along(value, axis, steps):
    count = lax.axis_size(axis)
    pairs = [(source, (source + steps) % count) for source in range(count)]
    return lax.ppermute(value, axis, pairs)


def attention(extended, picks_all, query, grad_att, block_rows):
    channels = query.shape[0]
    row_count = query.shape[1]
    head_dim = C // HEADS
    local_heads = channels // head_dim
    score_scale = 1.0 / math.sqrt(head_dim)
    block_count = row_count // block_rows
    pick_blocks = picks_all.reshape(NBR, block_count, block_rows).transpose(1, 0, 2)
    query_blocks = query.reshape(channels, block_count, block_rows).transpose(1, 0, 2)
    dout_blocks = grad_att.reshape(channels, block_count, block_rows).transpose(1, 0, 2)

    def attend_block(totals, inputs):
        picks, query_rows, dout_rows = inputs
        near = extended[picks].astype(jnp.float32)
        near_keys = near[:, :, :channels].reshape(NBR, block_rows, local_heads, head_dim)
        near_values = near[:, :, channels:].reshape(NBR, block_rows, local_heads, head_dim)
        query_heads = query_rows.astype(jnp.float32).T.reshape(block_rows, local_heads, head_dim)
        dout_heads = dout_rows.T.reshape(block_rows, local_heads, head_dim)
        scores = jnp.einsum("rhd,jrhd->jrh", query_heads, near_keys) * score_scale
        expon = jnp.exp(scores)
        probs = expon / jnp.sum(expon, axis=0)
        attended = jnp.einsum("jrh,jrhd->rhd", probs, near_values)
        dprob = jnp.einsum("rhd,jrhd->jrh", dout_heads, near_values)
        dscore = probs * (dprob - jnp.sum(probs * dprob, axis=0))
        grad_query = jnp.einsum("jrh,jrhd->rhd", dscore, near_keys) * score_scale
        grad_keys = dscore[..., None] * query_heads[None] * score_scale
        grad_values = probs[..., None] * dout_heads[None]
        grad_near = jnp.concatenate(
            [
                grad_keys.reshape(NBR, block_rows, channels),
                grad_values.reshape(NBR, block_rows, channels),
            ],
            axis=2,
        )
        totals = totals.at[picks.reshape(-1)].add(grad_near.reshape(NBR * block_rows, 2 * channels))
        attended_cols = attended.reshape(block_rows, channels).astype(jnp.bfloat16).T
        query_cols = grad_query.reshape(block_rows, channels).T
        return (totals, (attended_cols, query_cols))

    start_grad = jnp.zeros((extended.shape[0], 2 * channels), jnp.float32)
    grad_ext, (attended, grad_query) = lax.scan(
        attend_block, start_grad, (pick_blocks, query_blocks, dout_blocks)
    )
    attended = attended.transpose(1, 0, 2).reshape(channels, row_count)
    grad_query = grad_query.transpose(1, 0, 2).reshape(channels, row_count)
    return (grad_ext, attended, grad_query)


def local(tokens, grad_in, w_qkv, w_out, neighbors, send_rows):
    groups = lax.axis_size("tile")
    border = send_rows.shape[2]
    offsets = (1, groups - 1, groups // 2)
    lists = send_rows[0]
    full_x, full_dy = (
        lax.all_gather(tokens, "head", axis=0, tiled=True),
        lax.all_gather(grad_in, "head", axis=0, tiled=True),
    )
    row_count = tokens.shape[1]
    channels = tokens.shape[0]
    projected = jnp.einsum("tnc,cr->tnr", w_qkv, full_x, preferred_element_type=jnp.float32).astype(
        jnp.bfloat16
    )
    query = projected[0]
    packed = jnp.concatenate([projected[1].T, projected[2].T], axis=1)
    padded = jnp.concatenate([packed, jnp.zeros((1, 2 * channels), jnp.bfloat16)], axis=0)
    outgoing = padded[lists]
    pieces = []
    for peer in range(3):
        pieces.append(passed_along(outgoing[peer], "tile", offsets[peer]))
    halo = jnp.stack(pieces)
    extended = jnp.concatenate([packed, halo.reshape(3 * border, 2 * channels)], axis=0)
    grad_att = jnp.dot(w_out, full_dy, preferred_element_type=jnp.float32)
    grad_ext, attended, grad_query = attention(
        extended, neighbors, query, grad_att, min(1024, row_count)
    )
    grad_halo = grad_ext[row_count:].reshape(3, border, 2 * channels)
    answers = []
    for peer in range(3):
        answers.append(passed_along(grad_halo[peer], "tile", (groups - offsets[peer]) % groups))
    backward = jnp.stack(answers)
    own_grad = jnp.concatenate(
        [grad_ext[:row_count], jnp.zeros((1, 2 * channels), jnp.float32)], axis=0
    )
    own_grad = own_grad.at[lists.reshape(-1)].add(backward.reshape(3 * border, 2 * channels))[
        :row_count
    ]
    grad_proj = jnp.stack([grad_query, own_grad[:, :channels].T, own_grad[:, channels:].T]).astype(
        jnp.bfloat16
    )
    grad_scale = 1.0 / math.sqrt(row_count * groups)
    part_qkv = (
        jnp.einsum("tnr,cr->tnc", grad_proj, full_x, preferred_element_type=jnp.float32)
        * grad_scale
    )
    part_out = (
        lax.dot_general(
            attended, full_dy, (((1,), (1,)), ((), ())), preferred_element_type=jnp.float32
        )
        * grad_scale
    )
    grad_qkv, grad_out = lax.psum((part_qkv, part_out), "tile")
    partial_grad = jnp.einsum("tnc,tnr->cr", w_qkv, grad_proj, preferred_element_type=jnp.float32)
    mixed = lax.psum_scatter(partial_grad, "head", scatter_dimension=0, tiled=True)
    d_tokens = mixed + grad_in.astype(jnp.float32)
    return (d_tokens, grad_qkv, grad_out)


def solution(mesh):
    return jax.shard_map(
        local,
        mesh=mesh,
        in_specs=(
            P("head", "tile"),
            P("head", "tile"),
            P(None, "head", None),
            P("head", None),
            P(None, "tile"),
            P("tile", None, None),
        ),
        out_specs=(P("head", "tile"), P(None, "head", None), P("head", None)),
        check_vma=False,
    )
```

profile of v0, /device:TPU:1, one launch (start us, length us, event | category | flops | bytes accessed | tf_op | source)
XLA Modules:
  0.0 895.1 jit_solution(2888538529102410149)
XLA Ops:
  8.7 1.7 reshape.184
  12.4 34.6 %all-gather.3.cloned.1.call-done = bf16[256,4096]{1,0:T(8,128)(2,1)} async-done(((bf16[64,4096]{1,0:T(8,128)(2,1)}), bf16[256,4096]{1,0:T(8,128)(2,1)}) %all-gather.3.cloned.1.call-update) | async-done | bytes 2097168 | tf_op jit(solution)/shard_map/all_gather | solution.py:73
  47.0 2.2 convolution_convert_fusion
  52.5 1.9 collective-permute-start
  54.4 2.7 collective-permute-start.2
  57.1 25.2 %all-gather.5.cloned.1.call-done = bf16[256,4096]{1,0:T(8,128)(2,1)} async-done(((bf16[64,4096]{1,0:T(8,128)(2,1)}), bf16[256,4096]{1,0:T(8,128)(2,1)}) %all-gather.5.cloned.1.call-update) | async-done | bytes 2097168 | tf_op jit(solution)/shard_map/all_gather | solution.py:74
  82.3 2.1 fusion.36
  88.4 545.0 %while.14 = (s32[]{:T(128)}, f32[4480,128]{1,0:T(8,128)S(1)}, bf16[4,64,1024]{2,1,0:T(8,128)(2,1)}, bf16[4,64,1024]{2,1,0:T(8,128)(2,1)}, s32[4,9,1024]{2,0,1:T(...) while((s32[]{:T(128)}, f32[4480,128]{1,0:T(8,128)S(1)}, ...), condition=%wide.region_4.5_spmd, body=%wide.region_0.4_spmd.sunk | while | flops 11480082 | bytes 107651328 | solution.py:59
  93.7 1.7 fusion.50
  95.4 1.7 constant_dynamic-slice_fusion.7
  97.0 1.6 bitcast_convert_fusion.2
  99.4 35.9 %gather_fusion = bf16[9216,128]{1,0:T(8,128)(2,1)} fusion(bf16[4480,128]{1,0:T(8,128)(2,1)S(1)} %get-tuple-element.213, s32[9216]{0:T(1024)} %broadcast_clamp_fusion.2), kind=kCustom, calls=%fused_computation.clone.1 | custom fusion | bytes 4755456 | tf_op jit(solution)/shard_map/while/body/eval_jaxpr/gather | solution.py:32
  135.3 5.3 fusion.49
  140.6 3.8 copy.152
  144.4 1.8 multiply_reduce_fusion.8
  148.2 3.8 copy.155
  152.0 1.9 multiply_reduce_fusion.9
  165.6 2.5 pad_maximum_fusion.9
  168.1 6.0 copy.158
  174.2 50.6 %scatter_fusion = f32[4480,128]{1,0:T(8,128)S(1)} fusion(f32[4480,128]{1,0:T(8,128)S(1)} %get-tuple-element.200, s32[9216]{0:T(1024)} %bitcast.220, f32[9216,128]{1,0:T(8,128)} %copy.158), kind=kCustom, calls=%fused_computation.2.clone.1 | custom fusion | flops 1179648 | bytes 14192640 | tf_op jit(solution)/shard_map/while/body/eval_jaxpr/scatter-add | solution.py:53
  229.9 1.7 fusion.50
  231.5 1.7 constant_dynamic-slice_fusion.7
  235.6 35.9 %gather_fusion = bf16[9216,128]{1,0:T(8,128)(2,1)} fusion(bf16[4480,128]{1,0:T(8,128)(2,1)S(1)} %get-tuple-element.213, s32[9216]{0:T(1024)} %broadcast_clamp_fusion.2), kind=kCustom, calls=%fused_computation.clone.1 | custom fusion | bytes 4755456 | tf_op jit(solution)/shard_map/while/body/eval_jaxpr/gather | solution.py:32
  271.5 5.3 fusion.49
  276.8 3.8 copy.152
  280.6 1.8 multiply_reduce_fusion.8
  284.4 3.8 copy.155
  288.2 1.9 multiply_reduce_fusion.9
  301.8 2.5 pad_maximum_fusion.9
  304.3 6.0 copy.158
  310.3 50.6 %scatter_fusion = f32[4480,128]{1,0:T(8,128)S(1)} fusion(f32[4480,128]{1,0:T(8,128)S(1)} %get-tuple-element.200, s32[9216]{0:T(1024)} %bitcast.220, f32[9216,128]{1,0:T(8,128)} %copy.158), kind=kCustom, calls=%fused_computation.2.clone.1 | custom fusion | flops 1179648 | bytes 14192640 | tf_op jit(solution)/shard_map/while/body/eval_jaxpr/scatter-add | solution.py:53
  366.0 1.7 fusion.50
  367.7 1.7 constant_dynamic-slice_fusion.7
  371.7 35.9 %gather_fusion = bf16[9216,128]{1,0:T(8,128)(2,1)} fusion(bf16[4480,128]{1,0:T(8,128)(2,1)S(1)} %get-tuple-element.213, s32[9216]{0:T(1024)} %broadcast_clamp_fusion.2), kind=kCustom, calls=%fused_computation.clone.1 | custom fusion | bytes 4755456 | tf_op jit(solution)/shard_map/while/body/eval_jaxpr/gather | solution.py:32
  407.6 5.3 fusion.49
  412.9 3.8 copy.152
  416.7 1.8 multiply_reduce_fusion.8
  420.5 3.8 copy.155
  424.4 1.9 multiply_reduce_fusion.9
  437.9 2.5 pad_maximum_fusion.9
  440.4 6.0 copy.158
  446.5 50.6 %scatter_fusion = f32[4480,128]{1,0:T(8,128)S(1)} fusion(f32[4480,128]{1,0:T(8,128)S(1)} %get-tuple-element.200, s32[9216]{0:T(1024)} %bitcast.220, f32[9216,128]{1,0:T(8,128)} %copy.158), kind=kCustom, calls=%fused_computation.2.clone.1 | custom fusion | flops 1179648 | bytes 14192640 | tf_op jit(solution)/shard_map/while/body/eval_jaxpr/scatter-add | solution.py:53
  502.1 1.7 fusion.50
  503.8 1.7 constant_dynamic-slice_fusion.7
  507.8 35.9 %gather_fusion = bf16[9216,128]{1,0:T(8,128)(2,1)} fusion(bf16[4480,128]{1,0:T(8,128)(2,1)S(1)} %get-tuple-element.213, s32[9216]{0:T(1024)} %broadcast_clamp_fusion.2), kind=kCustom, calls=%fused_computation.clone.1 | custom fusion | bytes 4755456 | tf_op jit(solution)/shard_map/while/body/eval_jaxpr/gather | solution.py:32
  543.7 5.3 fusion.49
  549.1 3.8 copy.152
  552.9 1.8 multiply_reduce_fusion.8
  556.7 3.8 copy.155
  560.5 1.9 multiply_reduce_fusion.9
  574.0 2.5 pad_maximum_fusion.9
  576.6 6.0 copy.158
  582.6 50.6 %scatter_fusion = f32[4480,128]{1,0:T(8,128)S(1)} fusion(f32[4480,128]{1,0:T(8,128)S(1)} %get-tuple-element.200, s32[9216]{0:T(1024)} %bitcast.220, f32[9216,128]{1,0:T(8,128)} %copy.158), kind=kCustom, calls=%fused_computation.2.clone.1 | custom fusion | flops 1179648 | bytes 14192640 | tf_op jit(solution)/shard_map/while/body/eval_jaxpr/scatter-add | solution.py:53
  634.2 2.7 collective-permute-start.5
  638.5 3.1 slice_select_fusion
  643.2 3.4 scatter_fusion.1
  648.8 3.8 convolution_bitcast_fusion
  652.6 5.6 copy.88
  658.3 1.7 copy.57
  662.7 2.6 fusion.25
  665.3 40.3 %reduce-scatter.4.cloned.1.call-done = f32[64,4096]{1,0:T(8,128)} async-done(((f32[256,4096]{1,0:T(8,128)}), f32[64,4096]{1,0:T(8,128)}) %reduce-scatter.4.cloned.1.call-update) | async-done | bytes 1048592
  705.6 1.8 copy.89
  709.0 3.1 copy.59
  712.1 173.3 %all-reduce.4.cloned.1.call-done = (f32[3,64,256]{2,1,0:T(8,128)}, f32[64,256]{1,0:T(8,128)}) async-done(((f32[3,64,256]{2,1,0:T(8,128)}, f32[64,256]{1,0:T(8,128)}), (f32[3,64,256]{2,1,0:T(8,128)}, f32[64,256]{1,0:T(8,128)})) %all-reduce.4.cloned.1.call-update) | async-done | bytes 262160 | tf_op jit(solution)/shard_map/psum | solution.py:119
  (212 shorter events, 106.5 us)
Async XLA Ops:
  7.2 39.9 %copy-start = (bf16[3,64,256]{2,1,0:T(8,128)(2,1)S(1)}, bf16[3,64,256]{2,1,0:T(8,128)(2,1)}, u32[]{:S(2)}) copy-start(bf16[3,64,256]{2,1,0:T(8,128)(2,1)} %param.10) | copy-start | bytes 294916
  7.2 39.8 %all-gather.3.cloned.1.call-start = ((), (), s32[]{:S(2)}) async-start(), calls=%async_computation.1 | async-start | bytes 2621440 | tf_op jit(solution)/shard_map/all_gather | solution.py:73
  7.9 74.4 %all-gather.5.cloned.1.call-start = ((), (), s32[]{:S(2)}) async-start(), calls=%async_computation.2 | async-start | bytes 2621440 | tf_op jit(solution)/shard_map/all_gather | solution.py:74
  8.7 697.0 %reduce-scatter.4.cloned.1.call-start = ((), (), s32[]{:S(2)}) async-start(), calls=%async_computation.3 | async-start | bytes 5242880
  50.2 32.1 %copy-start.15 = (bf16[64,256]{1,0:T(8,128)(2,1)S(1)}, bf16[64,256]{1,0:T(8,128)(2,1)}, u32[]{:S(2)}) copy-start(bf16[64,256]{1,0:T(8,128)(2,1)} %param.11) | copy-start | bytes 98308
  52.5 34.3 %collective-permute-start = (bf16[128,128]{1,0:T(8,128)(2,1)S(1)}, bf16[128,128]{1,0:T(8,128)(2,1)S(1)}, u32[]{:S(2)}, u32[]{:S(2)}) collective-permute-start(bf16[128,128]{1,0:T(8,128)(2,1)S(1)} %get-tuple-element.126), channel_id=1, source_target_pairs={{0,4},{4,8},{8,12},{12,16},{16,20},{20,24},{24,28},{28,32},{32,36}... | collective-permute-start | bytes 98312 | tf_op jit(solution)/shard_map/ppermute | solution.py:16
  54.4 32.4 %collective-permute-start.1 = (bf16[128,128]{1,0:T(8,128)(2,1)S(1)}, bf16[128,128]{1,0:T(8,128)(2,1)S(1)}, u32[]{:S(2)}, u32[]{:S(2)}) collective-permute-start(bf16[128,128]{1,0:T(8,128)(2,1)S(1)} %get-tuple-element.127), channel_id=1, source_target_pairs={{0,252},{4,0},{8,4},{12,8},{16,12},{20,16},{24,20},{28,24},{32,28}... | collective-permute-start | bytes 98312 | tf_op jit(solution)/shard_map/ppermute | solution.py:16
  54.4 31.1 %copy-start.9 = (bf16[1,64,4096]{2,1,0:T(8,128)(2,1)S(1)}, bf16[1,64,4096]{2,1,0:T(8,128)(2,1)}, u32[]{:S(2)}) copy-start(bf16[1,64,4096]{2,1,0:T(8,128)(2,1)} %get-tuple-element.121) | copy-start | bytes 1572868
  54.4 32.4 %collective-permute-start.2 = (bf16[128,128]{1,0:T(8,128)(2,1)S(1)}, bf16[128,128]{1,0:T(8,128)(2,1)S(1)}, u32[]{:S(2)}, u32[]{:S(2)}) collective-permute-start(bf16[128,128]{1,0:T(8,128)(2,1)S(1)} %get-tuple-element.128), channel_id=1, source_target_pairs={{0,128},{4,132},{8,136},{12,140},{16,144},{20,148},{24,152},{28,15... | collective-permute-start | bytes 98312 | tf_op jit(solution)/shard_map/ppermute | solution.py:16
  88.4 550.1 %copy-start.17 = (pred[4097]{0:T(1024)(128)(4,1)S(1)}, pred[4097]{0:T(1024)(128)(4,1)}, u32[]{:S(2)}) copy-start(pred[4097]{0:T(1024)(128)(4,1)} %constant.6.clone.1) | copy-start | bytes 12295
  146.9 0.7 copy-start.2
  152.0 3.4 copy-start.3
  152.0 4.2 copy-start.1
  153.9 3.4 copy-start.5
  161.9 1.4 copy-start.4
  283.0 0.7 copy-start.2
  288.2 3.4 copy-start.3
  288.2 4.2 copy-start.1
  290.1 3.4 copy-start.5
  298.1 1.4 copy-start.4
  419.2 0.7 copy-start.2
  424.3 3.4 copy-start.3
  424.4 4.2 copy-start.1
  426.2 3.3 copy-start.5
  434.2 1.4 copy-start.4
  555.3 0.7 copy-start.2
  560.5 3.4 copy-start.3
  560.5 4.2 copy-start.1
  562.3 3.4 copy-start.5
  570.4 1.4 copy-start.4
  633.4 8.2 copy-start.10
  633.4 9.7 %collective-permute-start.3 = (f32[128,128]{1,0:T(8,128)S(1)}, f32[128,128]{1,0:T(8,128)S(1)}, u32[]{:S(2)}, u32[]{:S(2)}) collective-permute-start(f32[128,128]{1,0:T(8,128)S(1)} %get-tuple-element.118), channel_id=1, source_target_pairs={{0,252},{4,0},{8,4},{12,8},{16,12},{20,16},{24,20},{28,24},{32,28}... | collective-permute-start | bytes 196616 | tf_op jit(solution)/shard_map/ppermute | solution.py:16
  634.2 9.0 %collective-permute-start.5 = (f32[128,128]{1,0:T(8,128)S(1)}, f32[128,128]{1,0:T(8,128)S(1)}, u32[]{:S(2)}, u32[]{:S(2)}) collective-permute-start(f32[128,128]{1,0:T(8,128)S(1)} %get-tuple-element.119), channel_id=1, source_target_pairs={{0,128},{4,132},{8,136},{12,140},{16,144},{20,148},{24,152},{28,15... | collective-permute-start | bytes 196616 | tf_op jit(solution)/shard_map/ppermute | solution.py:16
  636.9 6.3 collective-permute-start.4
  641.6 1.6 copy-start.6
  641.6 1.6 copy-start.16
  647.8 0.8 copy-start.12
  647.9 1.0 copy-start.14
  658.3 3.0 copy-start.7
  658.3 227.1 %all-reduce.4.cloned.1.call-start = ((), (), s32[]{:S(2)}) async-start(), calls=%async_computation.4 | async-start | bytes 524288 | tf_op jit(solution)/shard_map/psum | solution.py:119
  660.0 2.7 copy-start.8
  660.0 2.7 copy-start.11
  660.0 2.7 copy-start.13
Sparse Core Ops, SparseCore 0:
  9.8 37.1 all-gather.2
  48.8 33.4 all-gather.4
  658.4 47.1 reduce-scatter.3
  710.2 175.2 all-reduce.3
where the time goes:
time: 900 us; the launch traced here: 895 us
  local copies, waits for them, and re-layouts  311 us (35%)
  waiting for transfers between devices  275 us (31%)
  other arithmetic  272 us (30%)
  between operations  14.1 us (2%)
  matrix products  12 us (1%)
  starting transfers between devices  9.82 us (1%)
    scatter-add x4, other arithmetic, attend_block(): totals.at[picks.reshape(-1)]  202 us
    psum x1, waiting for transfers between devices, local(): grad_qkv, grad_out = lax.psum((part_qkv, part_out), 'tile')  173 us
    gather x4, local copies, waits for them, and re-layouts, attend_block(): near = extended[picks].astype(jnp.float32)  144 us
    while x72, local copies, waits for them, and re-layouts  59 us
    unnamed x5, waiting for transfers between devices  41.7 us
    all_gather x1, waiting for transfers between devices, local(): lax.all_gather(tokens, 'head', axis=0, tiled=True)  34.6 us
    all_gather x1, waiting for transfers between devices, local(): lax.all_gather(grad_in, 'head', axis=0, tiled=True)  25.2 us
    concatenate x4, local copies, waits for them, and re-layouts, attend_block(): jnp.concatenate([grad_keys.reshape(NBR, block_rows, channels), grad_value...  24.2 us
  transfers between devices with their start and end apart: 10, of which 4 were waited for; matrix products, arithmetic and copies ran while one was open for 4% of the time, Pallas kernels for 0%

commit v1 on v0

v1 whole, which is shorter than its diff:
```python
import math

import jax
import jax.numpy as jnp
from jax import lax
from jax.experimental import pallas as pl
from jax.experimental.pallas import tpu as pltpu
from jax.sharding import PartitionSpec as P

C = 256
HEADS = 8
NBR = 9
HEAD_DIM = 32
BLOCK = 128
SIDE = 64
WINDOW = BLOCK + 2 * SIDE
LOG2E = math.log2(math.e)
F32 = jnp.float32
BF16 = jnp.bfloat16


def passed_along(value, axis, steps):
    count = lax.axis_size(axis)
    pairs = [(source, (source + steps) % count) for source in range(count)]
    return lax.ppermute(value, axis, pairs)


def grouped(value, groups):
    return lax.all_to_all(value, "tile", 0, 0, axis_index_groups=groups)


def vmem_spec():
    return pl.BlockSpec(memory_space=pltpu.VMEM)


def smem_spec():
    return pl.BlockSpec(memory_space=pltpu.SMEM)


def nt(a, b):
    return lax.dot_general(a, b, (((1,), (1,)), ((), ())), preferred_element_type=F32)


def tn(a, b):
    return lax.dot_general(a, b, (((0,), (0,)), ((), ())), preferred_element_type=F32)


def nn(a, b):
    return jnp.dot(a, b, preferred_element_type=F32)


def one_hot_rows(lists, start, count):
    rows = lax.broadcasted_iota(jnp.int32, (count, lists.shape[1]), 0) + start
    return jnp.where(rows == lists, 1.0, 0.0).astype(BF16)


def prepare(place, tokens, grad_in, w_qkv, w_out, lists, out0, out1, out2, out3, halo, padded):
    head = place[0]
    rows = tokens.shape[1]
    own = rows // 4
    ext = own + 2 * SIDE
    shifted = pltpu.roll(tokens[...].astype(F32), SIDE, 1).astype(BF16)
    padded[:, :rows] = shifted
    padded[:, rows:] = shifted[:, : 2 * SIDE]
    for step, out in enumerate((out0, out1, out2, out3)):
        target = (head + step) & 3
        first = pl.multiple_of(target * own, own)
        out[:, :ext] = padded[:, pl.ds(first, ext)]
        out[:, ext : ext + own] = grad_in[:, pl.ds(first, own)]
        base = ext + own
        for kind in range(3):
            out[:, base + kind * C : base + (kind + 1) * C] = w_qkv[kind]
        out[:, base + 3 * C :] = w_out[...]
    chosen = jnp.zeros(halo.shape, F32)
    for start in range(0, rows, 512):
        chosen = chosen + nn(tokens[:, start : start + 512], one_hot_rows(lists[...], start, 512))
    halo[...] = chosen.astype(BF16)


def attend(
    place, c0, c1, c2, c3, h0, h1, h2, h3, neighbors, o0, o1, o2, o3,
    xe, dy, wq, wkv, wo, qs, ds, kvt, kv, dkv, da, dkvt, grads, summed, bias,
):
    head = place[0]
    own = dy.shape[1]
    ext = own + 2 * SIDE
    full = xe.shape[1]
    border = full - ext
    cand = WINDOW + border
    rows_all = neighbors.shape[1]
    scale = 1.0 / math.sqrt(HEAD_DIM)
    wq[...] = jnp.zeros_like(wq)
    wo[...] = jnp.zeros_like(wo)
    for step, (chunk, far) in enumerate(((c0, h0), (c1, h1), (c2, h2), (c3, h3))):
        source = (head - step + 4) & 3
        row = pl.multiple_of(source * 64, 64)
        xe[pl.ds(row, 64), :ext] = chunk[:, :ext]
        xe[pl.ds(row, 64), ext:] = far[...]
        dy[pl.ds(row, 64), :] = chunk[:, ext : ext + own]
        base = ext + own
        for k in range(2):
            dest = pl.multiple_of(source * 128 + 64 * k, 64)
            part = slice(32 * k, 32 * k + 32)
            wq[pl.ds(dest, 32), :] = chunk[part, base : base + C]
            wkv[pl.ds(dest, 32), :] = chunk[part, base + C : base + 2 * C]
            wkv[pl.ds(dest + 32, 32), :] = chunk[part, base + 2 * C : base + 3 * C]
            wo[pl.ds(dest + 32, 32), :] = chunk[part, base + 3 * C :]
    for start in range(0, full, 128):
        cols = slice(start, start + 128)
        block = nn(wkv[...], xe[:, cols]).astype(BF16)
        kvt[:, cols] = block
        kv[cols, :] = block.T
    for start in range(0, ext, 128):
        cols = slice(start, start + 128)
        qs[cols, :] = nn(wq[...], xe[:, cols]).astype(BF16).T
    for start in range(0, own, 128):
        cols = slice(start, start + 128)
        ds[cols, :] = nn(wo[...], dy[:, cols]).astype(BF16).T
    dkv[...] = jnp.zeros_like(dkv)
    da[:, own:] = jnp.zeros((2 * C, 2 * SIDE), F32)
    lane_head = lax.broadcasted_iota(jnp.int32, (BLOCK, C), 1) // 64

    def step(b, carry):
        first = pl.multiple_of(b * BLOCK, BLOCK)
        near = neighbors[:, pl.ds(pl.multiple_of(head * own + b * BLOCK, BLOCK), BLOCK)]
        shifted = (near - (head * own + b * BLOCK - SIDE)) & (rows_all - 1)
        index = jnp.where(near < rows_all, shifted, near - rows_all + WINDOW)
        for start in range(0, cand, 128):
            rows = lax.broadcasted_iota(jnp.int32, (128, BLOCK), 0) + start
            count = jnp.zeros((128, BLOCK), F32)
            for slot in range(NBR):
                count = count + jnp.where(rows == index[slot : slot + 1, :], 1.0, 0.0)
            bias[start : start + 128, :] = jnp.where(count > 0.5, jnp.log(count) * LOG2E, -1e30)
        for g in range(2):
            cols = slice(C * g, C * g + C)
            query = qs[pl.ds(first + SIDE, BLOCK), cols]
            dout = ds[pl.ds(first, BLOCK), cols]
            both = jnp.concatenate([kv[pl.ds(first, WINDOW), cols], kv[ext:, cols]], axis=0)
            total = jnp.zeros((cand, C), F32)
            zero = jnp.zeros((BLOCK, C), BF16)
            for hh in range(4):
                mine = lane_head == hh
                stacked = jnp.concatenate(
                    [jnp.where(mine, query, zero), jnp.where(mine, dout, zero)], axis=0
                )
                products = nt(both, stacked)
                expon = jnp.exp2(products[:, :BLOCK] * (scale * LOG2E) + bias[...])
                dprob = products[:, BLOCK:]
                inverse = 1.0 / jnp.sum(expon, axis=0, keepdims=True)
                mean = jnp.sum(expon * dprob, axis=0, keepdims=True) * inverse
                prob = expon * inverse
                dscore = prob * (dprob - mean)
                weights = jnp.concatenate([dscore.astype(BF16), prob.astype(BF16)], axis=1)
                total = total + nn(weights, stacked)
                top = C * g + 64 * hh
                pair = jnp.concatenate(
                    [kvt[top : top + 64, pl.ds(first, WINDOW)], kvt[top : top + 64, ext:]], axis=1
                )
                result = nn(pair, weights)
                da[top : top + 32, pl.ds(first, BLOCK)] = result[:32, :BLOCK] * scale
                da[top + 32 : top + 64, pl.ds(first, BLOCK)] = result[32:, BLOCK:]
            dkv[pl.ds(first, WINDOW), cols] += total[:WINDOW]
            dkv[ext:, cols] += total[WINDOW:]
        return carry

    lax.fori_loop(0, own // BLOCK, step, 0)
    col_scale = jnp.where((lax.broadcasted_iota(jnp.int32, (128, 2 * C), 1) & 63) < 32, scale, 1.0)
    for start in range(0, full, 128):
        rows = slice(start, start + 128)
        dkvt[:, rows] = (dkv[rows, :] * col_scale).astype(BF16).T
    own_grads = pltpu.roll(da[...], SIDE, 1).astype(BF16)
    summed[:, :ext] = (tn(wkv[...], dkvt[:, :ext]) + tn(wq[...], own_grads)).astype(BF16)
    summed[:, ext:] = tn(wkv[...], dkvt[:, ext:]).astype(BF16)
    grads[0] = nt(own_grads, xe[:, :ext]).astype(BF16)
    grads[1] = nt(dkvt[...], xe[...]).astype(BF16)
    grads[2] = nt(da[:, :own].astype(BF16), dy[...]).astype(BF16)
    for step_out, out in enumerate((o0, o1, o2, o3)):
        target = (head + step_out) & 3
        out[:, :full] = summed[pl.ds(pl.multiple_of(target * 64, 64), 64), :]
        for k in range(2):
            top = pl.multiple_of(target * 128 + 64 * k, 64)
            part = slice(32 * k, 32 * k + 32)
            out[part, full : full + C] = grads[0, pl.ds(top, 32), :]
            out[part, full + C : full + 2 * C] = grads[1, pl.ds(top, 32), :]
            out[part, full + 2 * C : full + 3 * C] = grads[1, pl.ds(top + 32, 32), :]
            out[part, full + 3 * C :] = grads[2, pl.ds(top + 32, 32), :]


def add_up(r0, r1, r2, r3, b0, b1, b2, total):
    border = b0.shape[1]
    full = r0.shape[1] - 4 * C
    first = full - 3 * border
    parts = (r0, r1, r2, r3)
    for peer, out in enumerate((b0, b1, b2)):
        cols = slice(first + peer * border, first + (peer + 1) * border)
        out[...] = sum(part[:, cols].astype(F32) for part in parts).astype(BF16)
    for kind in range(4):
        cols = slice(full + kind * C, full + (kind + 1) * C)
        rows = slice(kind * 64, kind * 64 + 64)
        total[rows, :] = sum(part[:, cols].astype(F32) for part in parts).astype(BF16)


def finish(place, r0, r1, r2, r3, b0, b1, b2, grad_in, lists, out, padded):
    head = place[0]
    rows = grad_in.shape[1]
    own = rows // 4
    ext = own + 2 * SIDE
    padded[...] = jnp.zeros_like(padded)
    for step, part in enumerate((r0, r1, r2, r3)):
        source = (head - step + 4) & 3
        first = pl.multiple_of(source * own, own)
        padded[:, pl.ds(first, ext)] += part[:, :ext].astype(F32)
    padded[:, : 2 * SIDE] += padded[:, rows:]
    aligned = pltpu.roll(padded[:, :rows], rows - SIDE, 1)
    back = jnp.concatenate([b0[...], b1[...], b2[...]], axis=1)
    for start in range(0, rows, 512):
        cols = slice(start, start + 512)
        returned = nt(back, one_hot_rows(lists[...], start, 512))
        out[:, cols] = grad_in[:, cols].astype(F32) + aligned[:, cols] + returned


def kernel_call(body, out_shape, inputs, scratch=(), mib=48):
    specs = [smem_spec() if value.dtype == jnp.int32 and value.size == 1 else vmem_spec() for value in inputs]
    outs = [vmem_spec() for _ in out_shape] if isinstance(out_shape, (list, tuple)) else vmem_spec()
    return pl.pallas_call(
        body,
        out_shape=out_shape,
        in_specs=specs,
        out_specs=outs,
        scratch_shapes=list(scratch),
        compiler_params=pltpu.CompilerParams(vmem_limit_bytes=mib * 1024 * 1024),
    )(*inputs)


def sds(shape, dtype):
    return jax.ShapeDtypeStruct(shape, dtype)


def local(tokens, grad_in, w_qkv, w_out, neighbors, send_rows):
    groups = lax.axis_size("tile")
    border = send_rows.shape[2]
    offsets = (1, groups - 1, groups // 2)
    rows = tokens.shape[1]
    own = rows // 4
    ext = own + 2 * SIDE
    full = ext + 3 * border
    cand = WINDOW + 3 * border
    place = lax.axis_index("head").reshape(1).astype(jnp.int32)
    lists = send_rows.reshape(1, 3 * border)
    width = ext + own + 4 * C

    with jax.named_scope("prepare"):
        *chunks, halo = kernel_call(
            prepare,
            [sds((64, width), BF16)] * 4 + [sds((64, 3 * border), BF16)],
            (place, tokens, grad_in, w_qkv, w_out, lists),
            [pltpu.VMEM((64, rows + 2 * SIDE), BF16)],
        )
    with jax.named_scope("border_rows"):
        mine = jnp.concatenate(
            [
                passed_along(halo[:, peer * border : (peer + 1) * border], "tile", offsets[peer])
                for peer in range(3)
            ],
            axis=1,
        )
        far = [mine] + [passed_along(mine, "head", step) for step in (1, 2, 3)]
    with jax.named_scope("exchange"):
        chunks = [chunks[0]] + [passed_along(chunks[step], "head", step) for step in (1, 2, 3)]
    with jax.named_scope("attention"):
        parts = kernel_call(
            attend,
            [sds((64, full + 4 * C), BF16)] * 4,
            (place, *chunks, *far, neighbors),
            [
                pltpu.VMEM((C, full), BF16),
                pltpu.VMEM((C, own), BF16),
                pltpu.VMEM((2 * C, C), BF16),
                pltpu.VMEM((2 * C, C), BF16),
                pltpu.VMEM((2 * C, C), BF16),
                pltpu.VMEM((ext, 2 * C), BF16),
                pltpu.VMEM((own, 2 * C), BF16),
                pltpu.VMEM((2 * C, full), BF16),
                pltpu.VMEM((full, 2 * C), BF16),
                pltpu.VMEM((full, 2 * C), F32),
                pltpu.VMEM((2 * C, ext), F32),
                pltpu.VMEM((2 * C, full), BF16),
                pltpu.VMEM((3, 2 * C, C), BF16),
                pltpu.VMEM((C, full), BF16),
                pltpu.VMEM((cand, BLOCK), F32),
            ],
        )
    with jax.named_scope("return"):
        parts = [parts[0]] + [passed_along(parts[step], "head", step) for step in (1, 2, 3)]
        *back, total = kernel_call(
            add_up,
            [sds((64, border), BF16)] * 3 + [sds((C, C), BF16)],
            tuple(parts),
        )
        back = [
            passed_along(back[peer], "tile", (groups - offsets[peer]) % groups)
            for peer in range(3)
        ]
        d_tokens = kernel_call(
            finish,
            sds((64, rows), F32),
            (place, *parts, *back, grad_in, lists),
            [pltpu.VMEM((64, rows + 2 * SIDE), F32)],
        )
    with jax.named_scope("weight_sums"):
        near = [[16 * y + 2 * z + c for y in range(4) for c in range(2)] for z in range(8)]
        line = [[16 * y + 2 * z + c for z in range(8)] for y in range(4) for c in range(2)]
        piece = (8, C // 8, C)
        value = grouped(total.reshape(piece), near)
        value = value.astype(F32).sum(0).astype(BF16)
        value = grouped(jnp.broadcast_to(value[None], piece), line)
        value = value.astype(F32).sum(0).astype(BF16)
        value = grouped(jnp.broadcast_to(value[None], piece), near)
        grad_scale = 1.0 / math.sqrt(rows * groups)
        value = value.reshape(4, 64, C).astype(F32) * grad_scale
    return (d_tokens, value[:3], value[3])


def solution(mesh):
    return jax.shard_map(
        local,
        mesh=mesh,
        in_specs=(
            P("head", "tile"),
            P("head", "tile"),
            P(None, "head", None),
            P("head", None),
            P(None, "tile"),
            P("tile", None, None),
        ),
        out_specs=(P("head", "tile"), P(None, "head", None), P("head", None)),
        check_vma=False,
    )
```

time: 900 us -> 136 us (0.15)
  local copies, waits for them, and re-layouts: 311 us -> 6.45 us
  other arithmetic: 272 us -> 0.07 us
  waiting for transfers between devices: 275 us -> 28.6 us
  Pallas kernels: 0 us -> 39.9 us
  blocking collectives: 0 us -> 27.5 us
  starting transfers between devices: 9.82 us -> 30.5 us
  between operations: 14.1 us -> 0.73 us
  matrix products: 12 us -> 0 us
    scatter-add x5 -> x0, other arithmetic: 206 us -> none  [the longest x4 202 us: attend_block(): totals.at[picks.reshape(-1)]]
    psum x1 -> x0, waiting for transfers between devices: 173 us -> none  [local(): grad_qkv, grad_out = lax.psum((part_qkv, part_out), 'tile')]
    gather x5 -> x0, local copies, waits for them, and re-layouts: 145 us -> none  [the longest x4 144 us: attend_block(): near = extended[picks].astype(jnp.float32)]
    while x73 -> x0, local copies, waits for them, and re-layouts: 60.2 us -> none
    all_gather x2 -> x0, waiting for transfers between devices: 59.8 us -> none  [the longest x1 34.6 us: local(): lax.all_gather(tokens, 'head', axis=0, tiled=True)]
    unnamed x5 -> x0, waiting for transfers between devices: 41.7 us -> none
    pallas_call x0 -> x4, Pallas kernels: none -> 39.9 us  [kernel_call(): pl.pallas_call(body, out_shape=out_shape, in_specs=specs, out_specs=outs,...]
    ppermute x6 -> x15, waiting for transfers between devices: 0.02 us -> 28.6 us  [passed_along(): return lax.ppermute(value, axis, pairs)]
  transfers between devices with their start and end apart: 10 -> 16, of which waited for: 4 -> 6; matrix products, arithmetic and copies ran while one was open for 4% -> 0% of each run, Pallas kernels for 0% -> 2%
where the time goes in v1:
time: 136 us; the launch traced here: 134 us
  Pallas kernels  39.9 us (29%)
  starting transfers between devices  30.5 us (22%)
  waiting for transfers between devices  28.6 us (21%)
  blocking collectives  27.5 us (20%)
  local copies, waits for them, and re-layouts  6.45 us (5%)
    pallas_call x4, Pallas kernels, kernel_call(): pl.pallas_call(body, out_shape=out_shape, in_specs=specs, out_specs=outs,...  39.9 us
    ppermute x15, waiting for transfers between devices, passed_along(): return lax.ppermute(value, axis, pairs)  28.6 us
    all_to_all x2, blocking collectives, grouped(): return lax.all_to_all(value, 'tile', 0, 0, axis_index_groups=groups)  27.5 us
    ppermute x15, starting transfers between devices, passed_along(): return lax.ppermute(value, axis, pairs)  24.9 us
    all_to_all x1, starting transfers between devices, grouped(): return lax.all_to_all(value, 'tile', 0, 0, axis_index_groups=groups)  5.65 us
    unnamed x16, local copies, waits for them, and re-layouts  4.43 us
  transfers between devices with their start and end apart: 16, of which 6 were waited for; matrix products, arithmetic and copies ran while one was open for 0% of the time, Pallas kernels for 2%

profile of v1, /device:TPU:1, one launch (start us, length us, event | category | flops | bytes accessed | tf_op | source)
XLA Modules:
  0.0 133.8 jit_solution(2520803929964765494)
XLA Ops:
  0.6 0.0 copy-start.6
  0.6 0.7 copy-done.6
  1.3 0.0 copy-start
  1.3 1.0 copy-done
  2.4 0.0 copy-start.2
  2.4 1.0 copy-done.2
  3.4 0.0 copy-start.4
  3.4 0.9 copy-done.4
  4.3 0.0 copy-start.5
  4.3 0.8 copy-done.5
  5.1 0.0 copy-start.3
  5.1 0.9 prepare.1
  6.0 3.1 %collective-permute-start.3 = (bf16[64,128]{1,0:T(8,128)(2,1)S(1)}, bf16[64,128]{1,0:T(8,128)(2,1)S(1)}, u32[]{:S(2)}, u32[]{:S(2)}) collective-permute-start(bf16[64,128]{1,0:T(8,128)(2,1)S(1)} %get-tuple-element.31), channel_id=1, source_target_pairs={{0,4},{4,8},{8,12},{12,16},{16,20},{20,24},{24,28},{28,32},{32,36}... | collective-permute-start | bytes 49160 | tf_op jit(solution)/shard_map/border_rows/ppermute | solution.py:25
  9.1 2.9 %collective-permute-start.5 = (bf16[64,128]{1,0:T(8,128)(2,1)S(1)}, bf16[64,128]{1,0:T(8,128)(2,1)S(1)}, u32[]{:S(2)}, u32[]{:S(2)}) collective-permute-start(bf16[64,128]{1,0:T(8,128)(2,1)S(1)} %get-tuple-element.29), channel_id=1, source_target_pairs={{0,128},{4,132},{8,136},{12,140},{16,144},{20,148},{24,152},{28,15... | collective-permute-start | bytes 49160 | tf_op jit(solution)/shard_map/border_rows/ppermute | solution.py:25
  12.0 0.0 collective-permute-start.4
  12.0 1.2 collective-permute-start
  13.2 2.5 %collective-permute-start.1 = (bf16[64,3200]{1,0:T(8,128)(2,1)S(1)}, bf16[64,3200]{1,0:T(8,128)(2,1)S(1)}, u32[]{:S(2)}, u32[]{:S(2)}) collective-permute-start(bf16[64,3200]{1,0:T(8,128)(2,1)S(1)} %get-tuple-element.18), channel_id=1, source_target_pairs={{0,2},{1,3},{2,0},{3,1},{4,6},{5,7},{6,4},{7,5},{8,10},{9,11},{10,... | collective-permute-start | bytes 1228808 | tf_op jit(solution)/shard_map/exchange/ppermute | solution.py:25
  15.7 0.0 collective-permute-done.3
  15.7 1.1 collective-permute-start.2
  16.8 0.0 collective-permute-done.4
  16.8 0.0 collective-permute-done.5
  16.9 1.2 collective-permute-start.8
  18.0 1.0 collective-permute-start.7
  19.0 13.7 %collective-permute-done.8.h3 = bf16[64,384]{1,0:T(8,128)(2,1)S(1)} collective-permute-done((bf16[64,384]{1,0:T(8,128)(2,1)S(1)}, bf16[64,384]{1,0:T(8,128)(2,1)S(1)}, u32[]{:S(2)}, u32[]{:S(2)}) %collective-permute-start.8) | collective-permute-done | bytes 49184 | tf_op jit(solution)/shard_map/border_rows/ppermute | solution.py:25
  32.7 3.3 %collective-permute-start.6 = (bf16[64,384]{1,0:T(8,128)(2,1)S(1)}, bf16[64,384]{1,0:T(8,128)(2,1)S(1)}, u32[]{:S(2)}, u32[]{:S(2)}) collective-permute-start(bf16[64,384]{1,0:T(8,128)(2,1)S(1)} %constant_dynamic-update-slice_fusion.h0), channel_id=1, source_target_pairs={{0,1},{1,2},{2,3},{3,0},{4,5},{5,6},{6,7},{7,4},{8,9},{9,10},{10,1... | collective-permute-start | bytes 147464 | tf_op jit(solution)/shard_map/border_rows/ppermute | solution.py:25
  36.0 0.0 collective-permute-done.7.h2
  36.1 1.6 %collective-permute-done.6.h1 = bf16[64,384]{1,0:T(8,128)(2,1)S(1)} collective-permute-done((bf16[64,384]{1,0:T(8,128)(2,1)S(1)}, bf16[64,384]{1,0:T(8,128)(2,1)S(1)}, u32[]{:S(2)}, u32[]{:S(2)}) %collective-permute-start.6) | collective-permute-done | bytes 49184 | tf_op jit(solution)/shard_map/border_rows/ppermute | solution.py:25
  37.6 0.0 collective-permute-done.c1
  37.6 0.0 collective-permute-done.1.c2
  37.6 0.0 collective-permute-done.2.c3
  37.6 0.0 copy-done.3
  37.7 36.4 %attention.1 = (bf16[64,2560]{1,0:T(8,128)(2,1)S(1)}, bf16[64,2560]{1,0:T(8,128)(2,1)S(1)}, bf16[64,2560]{1,0:T(8,128)(2,1)S(1)}, bf16[64,2560]{1,0:T(8,128)(2,1)S(1)}) custom-call(s32[1]{0:T(128)} %bitcast.place, bf16[64,3200]{1,0:T(8,128)(2,1)S(1)} %get-tuple-element.16.c0, bf16[64,3200]{1,0:T(8,128)(2,1)S(1)} %collective-permute-done.c1, ...), custom_call_target="tpu_custom_call" | custom-call | tf_op jit(solution)/shard_map/attention/pallas_call | solution.py:225
  74.0 1.4 %collective-permute-start.9 = (bf16[64,2560]{1,0:T(8,128)(2,1)S(1)}, bf16[64,2560]{1,0:T(8,128)(2,1)S(1)}, u32[]{:S(2)}, u32[]{:S(2)}) collective-permute-start(bf16[64,2560]{1,0:T(8,128)(2,1)S(1)} %get-tuple-element.22), channel_id=1, source_target_pairs={{0,1},{1,2},{2,3},{3,0},{4,5},{5,6},{6,7},{7,4},{8,9},{9,10},{10,1... | collective-permute-start | bytes 983048 | tf_op jit(solution)/shard_map/return/ppermute | solution.py:25
  75.5 1.3 collective-permute-start.10
  76.8 1.2 collective-permute-start.11
  78.0 3.3 %collective-permute-done.9.r1 = bf16[64,2560]{1,0:T(8,128)(2,1)S(1)} collective-permute-done((bf16[64,2560]{1,0:T(8,128)(2,1)S(1)}, bf16[64,2560]{1,0:T(8,128)(2,1)S(1)}, u32[]{:S(2)}, u32[]{:S(2)}) %collective-permute-start.9) | collective-permute-done | bytes 327712 | tf_op jit(solution)/shard_map/return/ppermute | solution.py:25
  81.3 6.5 %collective-permute-done.10.r2 = bf16[64,2560]{1,0:T(8,128)(2,1)S(1)} collective-permute-done((bf16[64,2560]{1,0:T(8,128)(2,1)S(1)}, bf16[64,2560]{1,0:T(8,128)(2,1)S(1)}, u32[]{:S(2)}, u32[]{:S(2)}) %collective-permute-start.10) | collective-permute-done | bytes 327712 | tf_op jit(solution)/shard_map/return/ppermute | solution.py:25
  87.8 2.3 %collective-permute-done.11.r3 = bf16[64,2560]{1,0:T(8,128)(2,1)S(1)} collective-permute-done((bf16[64,2560]{1,0:T(8,128)(2,1)S(1)}, bf16[64,2560]{1,0:T(8,128)(2,1)S(1)}, u32[]{:S(2)}, u32[]{:S(2)}) %collective-permute-start.11) | collective-permute-done | bytes 327712 | tf_op jit(solution)/shard_map/return/ppermute | solution.py:25
  90.1 0.1 return.2
  90.2 11.6 %all_to_all.15 = bf16[8,32,256]{2,1,0:T(8,128)(2,1)S(1)} all-to-all(bf16[8,32,256]{2,1,0:T(8,128)(2,1)S(1)} %bitcast.5), channel_id=1, replica_groups={{0,4,64,68,128,132,192,196},{8,12,72,76,136,140,200,204},{16,20,80,84,1..., dimensions={0} | all-to-all | bytes 262144 | tf_op jit(solution)/shard_map/weight_sums/all_to_all | solution.py:29
  101.8 0.0 copy-start.1
  101.8 15.9 %all_to_all.16 = bf16[8,32,256]{2,1,0:T(8,128)(2,1)S(1)} all-to-all(bf16[8,32,256]{2,1,0:T(8,128)(2,1)S(1)} %broadcast_in_dim.4), channel_id=1, replica_groups={{0,8,16,24,32,40,48,56},{4,12,20,28,36,44,52,60},{64,72,80,88,96,104,11..., dimensions={0} | all-to-all | bytes 262144 | tf_op jit(solution)/shard_map/weight_sums/all_to_all | solution.py:29
  117.8 0.7 broadcast_in_dim.5
  118.4 5.6 %all-to-all-start.2 = ((bf16[8,32,256]{2,1,0:T(8,128)(2,1)}), bf16[8,32,256]{2,1,0:T(8,128)(2,1)S(1)}, u32[]{:S(2)}, u32[]{:S(2)}) async-start(bf16[8,32,256]{2,1,0:T(8,128)(2,1)} %broadcast_in_dim.5), calls=%async_computation.2 | async-start | bytes 262144 | tf_op jit(solution)/shard_map/weight_sums/all_to_all | solution.py:29
  124.1 0.2 collective-permute-start.12
  124.3 1.6 %collective-permute-start.13 = (bf16[64,128]{1,0:T(8,128)(2,1)S(1)}, bf16[64,128]{1,0:T(8,128)(2,1)S(1)}, u32[]{:S(2)}, u32[]{:S(2)}) collective-permute-start(bf16[64,128]{1,0:T(8,128)(2,1)S(1)} %get-tuple-element.26), channel_id=1, source_target_pairs={{0,4},{4,8},{8,12},{12,16},{16,20},{20,24},{24,28},{28,32},{32,36}... | collective-permute-start | bytes 49160 | tf_op jit(solution)/shard_map/return/ppermute | solution.py:25
  125.8 2.9 %collective-permute-start.14 = (bf16[64,128]{1,0:T(8,128)(2,1)S(1)}, bf16[64,128]{1,0:T(8,128)(2,1)S(1)}, u32[]{:S(2)}, u32[]{:S(2)}) collective-permute-start(bf16[64,128]{1,0:T(8,128)(2,1)S(1)} %get-tuple-element.27), channel_id=1, source_target_pairs={{0,128},{4,132},{8,136},{12,140},{16,144},{20,148},{24,152},{28,15... | collective-permute-start | bytes 49160 | tf_op jit(solution)/shard_map/return/ppermute | solution.py:25
  128.7 0.0 collective-permute-done.12.b0
  128.7 0.0 collective-permute-done.13.b1
  128.7 1.2 collective-permute-done.14.b2
  129.9 0.0 copy-done.1
  129.9 2.5 %return.3 = f32[64,4096]{1,0:T(8,128)} custom-call(s32[1]{0:T(128)} %bitcast.place, bf16[64,2560]{1,0:T(8,128)(2,1)S(1)} %get-tuple-element.21.r0, bf16[64,2560]{1,0:T(8,128)(2,1)S(1)} %collective-permute-done.9.r1, bf16[64,2560]{1,0:T(8,128)(2,1)S(1)} %collective-permute-done.10.r2, bf16[64,2560]{1,0:T(8,128)(2,1)S(1)} %collective-permute-done.11.r3, ...), custom_call_target="tpu_custom_call" | custom-call | tf_op jit(solution)/shard_map/return/pallas_call | solution.py:225
  132.4 0.0 all-to-all-done.2
  132.4 0.6 slice.26
  133.1 0.7 slice.25
  (8 shorter events, 0.1 us)
Async XLA Ops:
  0.6 0.7 copy-start.6
  1.3 1.0 copy-start
  2.4 1.0 copy-start.2
  3.4 0.9 copy-start.4
  4.3 0.8 copy-start.5
  5.1 32.6 %copy-start.3 = (s32[9,4096]{1,0:T(8,128)S(1)}, s32[9,4096]{1,0:T(8,128)}, u32[]{:S(2)}) copy-start(s32[9,4096]{1,0:T(8,128)} %neighbors.1) | copy-start | bytes 442372
  6.0 9.7 %collective-permute-start.3 = (bf16[64,128]{1,0:T(8,128)(2,1)S(1)}, bf16[64,128]{1,0:T(8,128)(2,1)S(1)}, u32[]{:S(2)}, u32[]{:S(2)}) collective-permute-start(bf16[64,128]{1,0:T(8,128)(2,1)S(1)} %get-tuple-element.31), channel_id=1, source_target_pairs={{0,4},{4,8},{8,12},{12,16},{16,20},{20,24},{24,28},{28,32},{32,36}... | collective-permute-start | bytes 49160 | tf_op jit(solution)/shard_map/border_rows/ppermute | solution.py:25
  9.1 7.8 %collective-permute-start.5 = (bf16[64,128]{1,0:T(8,128)(2,1)S(1)}, bf16[64,128]{1,0:T(8,128)(2,1)S(1)}, u32[]{:S(2)}, u32[]{:S(2)}) collective-permute-start(bf16[64,128]{1,0:T(8,128)(2,1)S(1)} %get-tuple-element.29), channel_id=1, source_target_pairs={{0,128},{4,132},{8,136},{12,140},{16,144},{20,148},{24,152},{28,15... | collective-permute-start | bytes 49160 | tf_op jit(solution)/shard_map/border_rows/ppermute | solution.py:25
  12.0 4.8 %collective-permute-start.4 = (bf16[64,128]{1,0:T(8,128)(2,1)S(1)}, bf16[64,128]{1,0:T(8,128)(2,1)S(1)}, u32[]{:S(2)}, u32[]{:S(2)}) collective-permute-start(bf16[64,128]{1,0:T(8,128)(2,1)S(1)} %get-tuple-element.30), channel_id=1, source_target_pairs={{0,252},{4,0},{8,4},{12,8},{16,12},{20,16},{24,20},{28,24},{32,28}... | collective-permute-start | bytes 49160 | tf_op jit(solution)/shard_map/border_rows/ppermute | solution.py:25
  12.0 25.6 %collective-permute-start = (bf16[64,3200]{1,0:T(8,128)(2,1)S(1)}, bf16[64,3200]{1,0:T(8,128)(2,1)S(1)}, u32[]{:S(2)}, u32[]{:S(2)}) collective-permute-start(bf16[64,3200]{1,0:T(8,128)(2,1)S(1)} %get-tuple-element.17), channel_id=1, source_target_pairs={{0,1},{1,2},{2,3},{3,0},{4,5},{5,6},{6,7},{7,4},{8,9},{9,10},{10,1... | collective-permute-start | bytes 1228808 | tf_op jit(solution)/shard_map/exchange/ppermute | solution.py:25
  13.2 24.4 %collective-permute-start.1 = (bf16[64,3200]{1,0:T(8,128)(2,1)S(1)}, bf16[64,3200]{1,0:T(8,128)(2,1)S(1)}, u32[]{:S(2)}, u32[]{:S(2)}) collective-permute-start(bf16[64,3200]{1,0:T(8,128)(2,1)S(1)} %get-tuple-element.18), channel_id=1, source_target_pairs={{0,2},{1,3},{2,0},{3,1},{4,6},{5,7},{6,4},{7,5},{8,10},{9,11},{10,... | collective-permute-start | bytes 1228808 | tf_op jit(solution)/shard_map/exchange/ppermute | solution.py:25
  15.7 22.0 %collective-permute-start.2 = (bf16[64,3200]{1,0:T(8,128)(2,1)S(1)}, bf16[64,3200]{1,0:T(8,128)(2,1)S(1)}, u32[]{:S(2)}, u32[]{:S(2)}) collective-permute-start(bf16[64,3200]{1,0:T(8,128)(2,1)S(1)} %get-tuple-element.19), channel_id=1, source_target_pairs={{0,3},{1,0},{2,1},{3,2},{4,7},{5,4},{6,5},{7,6},{8,11},{9,8},{10,9... | collective-permute-start | bytes 1228808 | tf_op jit(solution)/shard_map/exchange/ppermute | solution.py:25
  16.9 15.9 %collective-permute-start.8 = (bf16[64,384]{1,0:T(8,128)(2,1)S(1)}, bf16[64,384]{1,0:T(8,128)(2,1)S(1)}, u32[]{:S(2)}, u32[]{:S(2)}) collective-permute-start(bf16[64,384]{1,0:T(8,128)(2,1)S(1)} %constant_dynamic-update-slice_fusion.h0), channel_id=1, source_target_pairs={{0,3},{1,0},{2,1},{3,2},{4,7},{5,4},{6,5},{7,6},{8,11},{9,8},{10,9... | collective-permute-start | bytes 147464 | tf_op jit(solution)/shard_map/border_rows/ppermute | solution.py:25
  18.0 18.0 %collective-permute-start.7 = (bf16[64,384]{1,0:T(8,128)(2,1)S(1)}, bf16[64,384]{1,0:T(8,128)(2,1)S(1)}, u32[]{:S(2)}, u32[]{:S(2)}) collective-permute-start(bf16[64,384]{1,0:T(8,128)(2,1)S(1)} %constant_dynamic-update-slice_fusion.h0), channel_id=1, source_target_pairs={{0,2},{1,3},{2,0},{3,1},{4,6},{5,7},{6,4},{7,5},{8,10},{9,11},{10,... | collective-permute-start | bytes 147464 | tf_op jit(solution)/shard_map/border_rows/ppermute | solution.py:25
  32.7 4.9 %collective-permute-start.6 = (bf16[64,384]{1,0:T(8,128)(2,1)S(1)}, bf16[64,384]{1,0:T(8,128)(2,1)S(1)}, u32[]{:S(2)}, u32[]{:S(2)}) collective-permute-start(bf16[64,384]{1,0:T(8,128)(2,1)S(1)} %constant_dynamic-update-slice_fusion.h0), channel_id=1, source_target_pairs={{0,1},{1,2},{2,3},{3,0},{4,5},{5,6},{6,7},{7,4},{8,9},{9,10},{10,1... | collective-permute-start | bytes 147464 | tf_op jit(solution)/shard_map/border_rows/ppermute | solution.py:25
  74.0 7.2 %collective-permute-start.9 = (bf16[64,2560]{1,0:T(8,128)(2,1)S(1)}, bf16[64,2560]{1,0:T(8,128)(2,1)S(1)}, u32[]{:S(2)}, u32[]{:S(2)}) collective-permute-start(bf16[64,2560]{1,0:T(8,128)(2,1)S(1)} %get-tuple-element.22), channel_id=1, source_target_pairs={{0,1},{1,2},{2,3},{3,0},{4,5},{5,6},{6,7},{7,4},{8,9},{9,10},{10,1... | collective-permute-start | bytes 983048 | tf_op jit(solution)/shard_map/return/ppermute | solution.py:25
  75.5 12.3 %collective-permute-start.10 = (bf16[64,2560]{1,0:T(8,128)(2,1)S(1)}, bf16[64,2560]{1,0:T(8,128)(2,1)S(1)}, u32[]{:S(2)}, u32[]{:S(2)}) collective-permute-start(bf16[64,2560]{1,0:T(8,128)(2,1)S(1)} %get-tuple-element.23), channel_id=1, source_target_pairs={{0,2},{1,3},{2,0},{3,1},{4,6},{5,7},{6,4},{7,5},{8,10},{9,11},{10,... | collective-permute-start | bytes 983048 | tf_op jit(solution)/shard_map/return/ppermute | solution.py:25
  76.8 13.3 %collective-permute-start.11 = (bf16[64,2560]{1,0:T(8,128)(2,1)S(1)}, bf16[64,2560]{1,0:T(8,128)(2,1)S(1)}, u32[]{:S(2)}, u32[]{:S(2)}) collective-permute-start(bf16[64,2560]{1,0:T(8,128)(2,1)S(1)} %get-tuple-element.24), channel_id=1, source_target_pairs={{0,3},{1,0},{2,1},{3,2},{4,7},{5,4},{6,5},{7,6},{8,11},{9,8},{10,9... | collective-permute-start | bytes 983048 | tf_op jit(solution)/shard_map/return/ppermute | solution.py:25
  101.8 28.2 %copy-start.1 = (bf16[64,4096]{1,0:T(8,128)(2,1)S(1)}, bf16[64,4096]{1,0:T(8,128)(2,1)}, u32[]{:S(2)}) copy-start(bf16[64,4096]{1,0:T(8,128)(2,1)} %grad_in.3) | copy-start | bytes 1572868
  118.4 14.0 %all-to-all-start.2 = ((bf16[8,32,256]{2,1,0:T(8,128)(2,1)}), bf16[8,32,256]{2,1,0:T(8,128)(2,1)S(1)}, u32[]{:S(2)}, u32[]{:S(2)}) async-start(bf16[8,32,256]{2,1,0:T(8,128)(2,1)} %broadcast_in_dim.5), calls=%async_computation.2 | async-start | bytes 262144 | tf_op jit(solution)/shard_map/weight_sums/all_to_all | solution.py:29
  124.1 4.7 %collective-permute-start.12 = (bf16[64,128]{1,0:T(8,128)(2,1)S(1)}, bf16[64,128]{1,0:T(8,128)(2,1)S(1)}, u32[]{:S(2)}, u32[]{:S(2)}) collective-permute-start(bf16[64,128]{1,0:T(8,128)(2,1)S(1)} %get-tuple-element.25), channel_id=1, source_target_pairs={{0,252},{4,0},{8,4},{12,8},{16,12},{20,16},{24,20},{28,24},{32,28}... | collective-permute-start | bytes 49160 | tf_op jit(solution)/shard_map/return/ppermute | solution.py:25
  124.3 4.5 %collective-permute-start.13 = (bf16[64,128]{1,0:T(8,128)(2,1)S(1)}, bf16[64,128]{1,0:T(8,128)(2,1)S(1)}, u32[]{:S(2)}, u32[]{:S(2)}) collective-permute-start(bf16[64,128]{1,0:T(8,128)(2,1)S(1)} %get-tuple-element.26), channel_id=1, source_target_pairs={{0,4},{4,8},{8,12},{12,16},{16,20},{20,24},{24,28},{28,32},{32,36}... | collective-permute-start | bytes 49160 | tf_op jit(solution)/shard_map/return/ppermute | solution.py:25
  125.8 4.1 %collective-permute-start.14 = (bf16[64,128]{1,0:T(8,128)(2,1)S(1)}, bf16[64,128]{1,0:T(8,128)(2,1)S(1)}, u32[]{:S(2)}, u32[]{:S(2)}) collective-permute-start(bf16[64,128]{1,0:T(8,128)(2,1)S(1)} %get-tuple-element.27), channel_id=1, source_target_pairs={{0,128},{4,132},{8,136},{12,140},{16,144},{20,148},{24,152},{28,15... | collective-permute-start | bytes 49160 | tf_op jit(solution)/shard_map/return/ppermute | solution.py:25

commit v2 on v1

v2 whole, which is shorter than its diff:
```python
import math

import jax
import jax.numpy as jnp
from jax import lax
from jax.experimental import pallas as pl
from jax.experimental.pallas import tpu as pltpu
from jax.sharding import PartitionSpec as P

C = 256
HEADS = 8
NBR = 9
HEAD_DIM = 32
BLOCK = 128
SIDE = 64
CHUNK = 128
WINDOW = BLOCK + 2 * SIDE
LOG2E = math.log2(math.e)
F32 = jnp.float32
BF16 = jnp.bfloat16


def passed_along(value, axis, steps):
    count = lax.axis_size(axis)
    pairs = [(source, (source + steps) % count) for source in range(count)]
    return lax.ppermute(value, axis, pairs)


def grouped(value, groups):
    return lax.all_to_all(value, "tile", 0, 0, axis_index_groups=groups)


def plates(heads):
    return [
        [(16 * y + 2 * z + c) * heads + h for h in range(heads) for y in range(4) for c in range(2)]
        for z in range(8)
    ]


def vmem_spec():
    return pl.BlockSpec(memory_space=pltpu.VMEM)


def nt(a, b):
    return lax.dot_general(a, b, (((1,), (1,)), ((), ())), preferred_element_type=F32)


def tn(a, b):
    return lax.dot_general(a, b, (((0,), (0,)), ((), ())), preferred_element_type=F32)


def nn(a, b):
    return jnp.dot(a, b, preferred_element_type=F32)


def one_hot_rows(lists, start, count):
    rows = lax.broadcasted_iota(jnp.int32, (count, lists.shape[1]), 0) + start
    return jnp.where(rows == lists, 1.0, 0.0).astype(BF16)


def choose(tokens, lists, halo, x, sems):
    rows = tokens.shape[1]
    quarter = rows // 4
    fetches = [
        pltpu.make_async_copy(
            tokens.at[:, pl.ds(part * quarter, quarter)],
            x.at[:, pl.ds(part * quarter, quarter)],
            sems.at[part],
        )
        for part in range(4)
    ]
    for fetch in fetches:
        fetch.start()
    chosen = jnp.zeros(halo.shape, F32)
    for part, fetch in enumerate(fetches):
        fetch.wait()
        for start in range(part * quarter, (part + 1) * quarter, 512):
            chosen = chosen + nn(x[:, start : start + 512], one_hot_rows(lists[...], start, 512))
    halo[...] = chosen.astype(BF16)


def prepare(
    place, tokens, grad_in, w_qkv, w_out, halo, out0, out1, out2, out3, x, wv, wo, padded, sems
):
    head = place[0]
    rows = tokens.shape[1]
    own = rows // 4
    ext = own + 2 * SIDE
    base = ext + own
    outs = (out0, out1, out2, out3)
    fetch_x = pltpu.make_async_copy(tokens, x, sems.at[0])
    fetch_v = pltpu.make_async_copy(w_qkv, wv, sems.at[1])
    fetch_o = pltpu.make_async_copy(w_out, wo, sems.at[2])
    fetches = [
        pltpu.make_async_copy(
            grad_in.at[:, pl.ds(pl.multiple_of(((head + step) & 3) * own, own), own)],
            out.at[:, pl.ds(ext, own)],
            sems.at[3 + step],
        )
        for step, out in enumerate(outs)
    ]
    fetch_x.start()
    fetch_v.start()
    fetch_o.start()
    for fetch in fetches:
        fetch.start()
    fetch_x.wait()
    shifted = pltpu.roll(x[...].astype(F32), SIDE, 1).astype(BF16)
    padded[:, :rows] = shifted
    padded[:, rows:] = shifted[:, : 2 * SIDE]
    for step, out in enumerate(outs):
        first = pl.multiple_of(((head + step) & 3) * own, own)
        out[:, :ext] = padded[:, pl.ds(first, ext)]
    fetch_v.wait()
    fetch_o.wait()
    for out in outs:
        for kind in range(3):
            out[:, base + kind * C : base + (kind + 1) * C] = wv[kind]
        out[:, base + 3 * C :] = wo[...]
    for fetch in fetches:
        fetch.wait()


def attend(
    place, c0, c1, c2, c3, far, neighbors, o0, o1, o2, o3, sums,
    xe, dy, wq, wkv, wo, qs, ds, kvt, kv, dkv, da, dkvt, grads, summed, bias,
    products0, products1, weights0, weights1,
):
    head = place[0]
    own = dy.shape[1]
    ext = own + 2 * SIDE
    full = xe.shape[1]
    border = full - ext
    cand = WINDOW + border
    rows_all = neighbors.shape[1]
    scale = 1.0 / math.sqrt(HEAD_DIM)
    wq[...] = jnp.zeros_like(wq)
    wo[...] = jnp.zeros_like(wo)
    xe[:, ext:] = far[...].reshape(C, border)
    for step, chunk in enumerate((c0, c1, c2, c3)):
        source = (head - step + 4) & 3
        row = pl.multiple_of(source * 64, 64)
        xe[pl.ds(row, 64), :ext] = chunk[:, :ext]
        dy[pl.ds(row, 64), :] = chunk[:, ext : ext + own]
        base = ext + own
        for k in range(2):
            dest = pl.multiple_of(source * 128 + 64 * k, 64)
            part = slice(32 * k, 32 * k + 32)
            wq[pl.ds(dest, 32), :] = chunk[part, base : base + C]
            wkv[pl.ds(dest, 32), :] = chunk[part, base + C : base + 2 * C]
            wkv[pl.ds(dest + 32, 32), :] = chunk[part, base + 2 * C : base + 3 * C]
            wo[pl.ds(dest + 32, 32), :] = chunk[part, base + 3 * C :]
    for start in range(0, full, 128):
        cols = slice(start, start + 128)
        block = nn(wkv[...], xe[:, cols]).astype(BF16)
        kvt[:, cols] = block
        kv[cols, :] = block.T
    for start in range(0, ext, 128):
        cols = slice(start, start + 128)
        qs[cols, :] = nn(wq[...], xe[:, cols]).astype(BF16).T
    for start in range(0, own, 128):
        cols = slice(start, start + 128)
        ds[cols, :] = nn(wo[...], dy[:, cols]).astype(BF16).T
    dkv[...] = jnp.zeros_like(dkv)
    da[:, own:] = jnp.zeros((2 * C, 2 * SIDE), F32)
    lane_head = lax.broadcasted_iota(jnp.int32, (BLOCK, C), 1) // 64

    zero = jnp.zeros((BLOCK, C), BF16)
    last = own // BLOCK - 1

    def operands(b, g, hh):
        first = pl.multiple_of(b * BLOCK, BLOCK)
        cols = slice(C * g, C * g + C)
        mine = lane_head == hh
        query = jnp.where(mine, qs[pl.ds(first + SIDE, BLOCK), cols], zero)
        dout = jnp.where(mine, ds[pl.ds(first, BLOCK), cols], zero)
        return jnp.concatenate([query, dout], axis=0)

    def multiply(b, g, hh, products):
        first = pl.multiple_of(b * BLOCK, BLOCK)
        cols = slice(C * g, C * g + C)
        out = slice(C * hh, C * hh + C)
        both = jnp.concatenate([kv[pl.ds(first, WINDOW), cols], kv[ext:, cols]], axis=0)
        products[:, out] = nt(both, operands(b, g, hh))

    def weigh(hh, products, weights):
        left = slice(C * hh, C * hh + BLOCK)
        right = slice(C * hh + BLOCK, C * hh + C)
        acc = jnp.zeros((8, BLOCK), F32)
        for start in range(0, cand, CHUNK):
            rows = slice(start, start + CHUNK)
            expon = jnp.exp2(products[rows, left] * (scale * LOG2E) + bias[rows, :])
            products[rows, left] = expon
            acc = acc + expon.reshape(CHUNK // 8, 8, BLOCK).sum(0)
        inverse = 1.0 / jnp.sum(acc, axis=0, keepdims=True)
        acc = jnp.zeros((8, BLOCK), F32)
        for start in range(0, cand, CHUNK):
            rows = slice(start, start + CHUNK)
            term = (products[rows, left] * inverse) * products[rows, right]
            acc = acc + term.reshape(CHUNK // 8, 8, BLOCK).sum(0)
        mean = jnp.sum(acc, axis=0, keepdims=True)
        for start in range(0, cand, CHUNK):
            rows = slice(start, start + CHUNK)
            prob = products[rows, left] * inverse
            weights[rows, left] = (prob * (products[rows, right] - mean)).astype(BF16)
            weights[rows, right] = prob.astype(BF16)

    def gather_rows(b, g, hh, weights):
        first = pl.multiple_of(b * BLOCK, BLOCK)
        top = C * g + 64 * hh
        pair = jnp.concatenate(
            [kvt[top : top + 64, pl.ds(first, WINDOW)], kvt[top : top + 64, ext:]], axis=1
        )
        result = nn(pair, weights[:, C * hh : C * hh + C])
        da[top : top + 32, pl.ds(first, BLOCK)] = result[:32, :BLOCK] * scale
        da[top + 32 : top + 64, pl.ds(first, BLOCK)] = result[32:, BLOCK:]

    def spread(b, g, weights):
        first = pl.multiple_of(b * BLOCK, BLOCK)
        cols = slice(C * g, C * g + C)
        stack = jnp.concatenate([operands(b, g, hh) for hh in range(4)], axis=0)
        total = nn(weights[...], stack)
        dkv[pl.ds(first, WINDOW), cols] += total[:WINDOW]
        dkv[ext:, cols] += total[WINDOW:]

    def step(b, carry):
        near = neighbors[:, pl.ds(pl.multiple_of(head * own + b * BLOCK, BLOCK), BLOCK)]
        shifted = (near - (head * own + b * BLOCK - SIDE)) & (rows_all - 1)
        index = jnp.where(near < rows_all, shifted, near - rows_all + WINDOW)
        for start in range(0, cand, CHUNK):
            rows = lax.broadcasted_iota(jnp.int32, (CHUNK, BLOCK), 0) + start
            count = jnp.zeros((CHUNK, BLOCK), F32)
            for slot in range(NBR):
                count = count + jnp.where(rows == index[slot : slot + 1, :], 1.0, 0.0)
            bias[start : start + CHUNK, :] = jnp.where(count > 0.5, jnp.log(count) * LOG2E, -1e30)
        before = jnp.maximum(b - 1, 0)
        after = jnp.minimum(b + 1, last)
        for hh in range(4):
            multiply(b, 1, hh, products1)
            weigh(hh, products0, weights0)
            gather_rows(before, 1, hh, weights1)
        spread(before, 1, weights1)
        for hh in range(4):
            multiply(after, 0, hh, products0)
            weigh(hh, products1, weights1)
            gather_rows(b, 0, hh, weights0)
        spread(b, 0, weights0)
        return carry

    weights1[...] = jnp.zeros_like(weights1)
    for hh in range(4):
        multiply(0, 0, hh, products0)
    lax.fori_loop(0, own // BLOCK, step, 0)
    for hh in range(4):
        gather_rows(last, 1, hh, weights1)
    spread(last, 1, weights1)
    col_scale = jnp.where((lax.broadcasted_iota(jnp.int32, (128, 2 * C), 1) & 63) < 32, scale, 1.0)
    for start in range(0, full, 128):
        rows = slice(start, start + 128)
        dkvt[:, rows] = (dkv[rows, :] * col_scale).astype(BF16).T
    own_grads = pltpu.roll(da[...], SIDE, 1).astype(BF16)
    summed[:, :ext] = (tn(wkv[...], dkvt[:, :ext]) + tn(wq[...], own_grads)).astype(BF16)
    summed[:, ext:] = tn(wkv[...], dkvt[:, ext:]).astype(BF16)
    grads[0] = nt(own_grads, xe[:, :ext]).astype(BF16)
    grads[1] = nt(dkvt[...], xe[...]).astype(BF16)
    grads[2] = nt(da[:, :own].astype(BF16), dy[...]).astype(BF16)
    for step_out, out in enumerate((o0, o1, o2, o3)):
        target = (head + step_out) & 3
        out[...] = summed[pl.ds(pl.multiple_of(target * 64, 64), 64), :]
    for target in range(4):
        for k in range(2):
            top = 128 * target + 64 * k
            for kind, (which, low) in enumerate(((0, 0), (1, 0), (1, 32), (2, 32))):
                sums[target, 64 * kind + 32 * k : 64 * kind + 32 * k + 32, :] = grads[
                    which, top + low : top + low + 32, :
                ]


def add_up(r0, r1, r2, r3, b0, b1, b2):
    border = b0.shape[1]
    first = r0.shape[1] - 3 * border
    for peer, out in enumerate((b0, b1, b2)):
        cols = slice(first + peer * border, first + (peer + 1) * border)
        out[...] = sum(part[:, cols].astype(F32) for part in (r0, r1, r2, r3)).astype(BF16)


def finish(place, r0, r1, r2, r3, b0, b1, b2, grad_in, lists, out, padded):
    head = place[0]
    rows = grad_in.shape[1]
    own = rows // 4
    ext = own + 2 * SIDE
    padded[...] = jnp.zeros_like(padded)
    for step, part in enumerate((r0, r1, r2, r3)):
        source = (head - step + 4) & 3
        first = pl.multiple_of(source * own, own)
        padded[:, pl.ds(first, ext)] += part[:, :ext].astype(F32)
    padded[:, : 2 * SIDE] += padded[:, rows:]
    aligned = pltpu.roll(padded[:, :rows], rows - SIDE, 1)
    back = jnp.concatenate([b0[...], b1[...], b2[...]], axis=1)
    for start in range(0, rows, 512):
        cols = slice(start, start + 512)
        returned = nt(back, one_hot_rows(lists[...], start, 512))
        out[:, cols] = grad_in[:, cols].astype(F32) + aligned[:, cols] + returned


def kernel_call(body, out_shape, inputs, scratch=(), mib=48, loose=()):
    specs = []
    for place, value in enumerate(inputs):
        if value.dtype == jnp.int32 and value.size == 1:
            specs.append(pl.BlockSpec(memory_space=pltpu.SMEM))
        elif place in loose:
            specs.append(pl.BlockSpec(memory_space=pltpu.HBM))
        else:
            specs.append(vmem_spec())
    outs = [vmem_spec() for _ in out_shape] if isinstance(out_shape, (list, tuple)) else vmem_spec()
    return pl.pallas_call(
        body,
        out_shape=out_shape,
        in_specs=specs,
        out_specs=outs,
        scratch_shapes=list(scratch),
        compiler_params=pltpu.CompilerParams(vmem_limit_bytes=mib * 1024 * 1024),
    )(*inputs)


def sds(shape, dtype):
    return jax.ShapeDtypeStruct(shape, dtype)


def attend_call(place, *args):
    *inputs, own, ext, full, cand = args
    return kernel_call(
        attend,
        [sds((64, full), BF16)] * 4 + [sds((4, C, C), BF16)],
        (place, *inputs),
        [
            pltpu.VMEM((C, full), BF16),
            pltpu.VMEM((C, own), BF16),
            pltpu.VMEM((2 * C, C), BF16),
            pltpu.VMEM((2 * C, C), BF16),
            pltpu.VMEM((2 * C, C), BF16),
            pltpu.VMEM((ext, 2 * C), BF16),
            pltpu.VMEM((own, 2 * C), BF16),
            pltpu.VMEM((2 * C, full), BF16),
            pltpu.VMEM((full, 2 * C), BF16),
            pltpu.VMEM((full, 2 * C), F32),
            pltpu.VMEM((2 * C, ext), F32),
            pltpu.VMEM((2 * C, full), BF16),
            pltpu.VMEM((3, 2 * C, C), BF16),
            pltpu.VMEM((C, full), BF16),
            pltpu.VMEM((cand, BLOCK), F32),
            pltpu.VMEM((cand, 4 * C), F32),
            pltpu.VMEM((cand, 4 * C), F32),
            pltpu.VMEM((cand, 4 * C), BF16),
            pltpu.VMEM((cand, 4 * C), BF16),
        ],
    )


def local(tokens, grad_in, w_qkv, w_out, neighbors, send_rows):
    groups = lax.axis_size("tile")
    border = send_rows.shape[2]
    offsets = (1, groups - 1, groups // 2)
    rows = tokens.shape[1]
    own = rows // 4
    ext = own + 2 * SIDE
    full = ext + 3 * border
    cand = WINDOW + 3 * border
    place = lax.axis_index("head").reshape(1).astype(jnp.int32)
    lists = send_rows.reshape(1, 3 * border)
    width = ext + own + 4 * C

    with jax.named_scope("border_rows"):
        halo = kernel_call(
            choose,
            sds((64, 3 * border), BF16),
            (tokens, lists),
            [pltpu.VMEM((64, rows), BF16), pltpu.SemaphoreType.DMA((4,))],
            loose=(0,),
        )
    with jax.named_scope("prepare"):
        chunks = kernel_call(
            prepare,
            [sds((64, width), BF16)] * 4,
            (place, tokens, grad_in, w_qkv, w_out, halo),
            [
                pltpu.VMEM((64, rows), BF16),
                pltpu.VMEM((3, 64, C), BF16),
                pltpu.VMEM((64, C), BF16),
                pltpu.VMEM((64, rows + 2 * SIDE), BF16),
                pltpu.SemaphoreType.DMA((7,)),
            ],
            loose=(1, 2, 3, 4),
        )
    with jax.named_scope("border_rows"):
        mine = jnp.concatenate(
            [
                passed_along(halo[:, peer * border : (peer + 1) * border], "tile", offsets[peer])
                for peer in range(3)
            ],
            axis=1,
        )
        spread = lax.all_to_all(
            jnp.broadcast_to(mine[None], (4, 64, 3 * border)), "head", 0, 0
        )
    with jax.named_scope("exchange"):
        chunks = [chunks[0]] + [passed_along(chunks[step], "head", step) for step in (1, 2, 3)]
    with jax.named_scope("attention"):
        *parts, sums = attend_call(place, *chunks, spread, neighbors, own, ext, full, cand)
    with jax.named_scope("return"):
        parts = [parts[0]] + [passed_along(parts[step], "head", step) for step in (1, 2, 3)]
    with jax.named_scope("weight_sums"):
        value = lax.all_to_all(
            sums.reshape(32, C // 8, C), ("tile", "head"), 0, 0, axis_index_groups=plates(4)
        )
        value = value.astype(F32).sum(0).astype(BF16)
        *parts, value = lax.optimization_barrier((*parts, value))
    with jax.named_scope("return"):
        back = kernel_call(add_up, [sds((64, border), BF16)] * 3, tuple(parts))
        back = [
            passed_along(back[peer], "tile", (groups - offsets[peer]) % groups)
            for peer in range(3)
        ]
    with jax.named_scope("weight_sums"):
        line = [[16 * y + 2 * z + c for z in range(8)] for y in range(4) for c in range(2)]
        piece = (8, C // 8, C)
        value = grouped(jnp.broadcast_to(value[None], piece), line)
        value = value.astype(F32).sum(0)
        *back, value = lax.optimization_barrier((*back, value))
        value = grouped(jnp.broadcast_to(value[None], piece), plates(1))
        grad_scale = 1.0 / math.sqrt(rows * groups)
        value = value.reshape(4, 64, C) * grad_scale
    with jax.named_scope("return"):
        d_tokens = kernel_call(
            finish,
            sds((64, rows), F32),
            (place, *parts, *back, grad_in, lists),
            [pltpu.VMEM((64, rows + 2 * SIDE), F32)],
        )
    return (d_tokens, value[:3], value[3])


def solution(mesh):
    return jax.shard_map(
        local,
        mesh=mesh,
        in_specs=(
            P("head", "tile"),
            P("head", "tile"),
            P(None, "head", None),
            P("head", None),
            P(None, "tile"),
            P("tile", None, None),
        ),
        out_specs=(P("head", "tile"), P(None, "head", None), P("head", None)),
        check_vma=False,
    )
```

time: 136 us -> 120 us (0.88); the launches traced: 134 us -> 119 us
  blocking collectives: 27.5 us -> 7.68 us
  starting transfers between devices: 30.5 us -> 50.1 us
  waiting for transfers between devices: 28.6 us -> 19.5 us
  Pallas kernels: 39.9 us -> 35.8 us
    ppermute x15 -> x12, waiting for transfers between devices: 28.6 us -> 6.83 us  [passed_along(): return lax.ppermute(value, axis, pairs)]
    all_to_all x2 -> x1, blocking collectives: 27.5 us -> 7.68 us  [local(): lax.all_to_all(jnp.broadcast_to(mine[None], (4, 64, 3 * border)), 'head',...]
    all_to_all x1 -> x2, starting transfers between devices: 5.65 us -> 15.4 us  [grouped(): return lax.all_to_all(value, 'tile', 0, 0, axis_index_groups=groups)]
    all_to_all x0 -> x1, starting transfers between devices: none -> 8.2 us  [local(): lax.all_to_all(sums.reshape(32, C // 8, C), ('tile', 'head'), 0, 0, axis_...]
    all_to_all x0 -> x1, waiting for transfers between devices: none -> 6.7 us  [local(): lax.all_to_all(sums.reshape(32, C // 8, C), ('tile', 'head'), 0, 0, axis_...]
    all_to_all x1 -> x2, waiting for transfers between devices: 0.01 us -> 6 us  [grouped(): return lax.all_to_all(value, 'tile', 0, 0, axis_index_groups=groups)]
    pallas_call x4 -> x5, Pallas kernels: 39.9 us -> 35.8 us  [kernel_call(): pl.pallas_call(body, out_shape=out_shape, in_specs=specs, out_specs=outs,...]
    unnamed x16 -> x12, local copies, waits for them, and re-layouts: 4.43 us -> 2.61 us
  transfers between devices with their start and end apart: 16 -> 15, of which waited for: 6 -> 6; matrix products, arithmetic and copies ran while one was open for 0% -> 0% of each run, Pallas kernels for 2% -> 2%
where the time goes in v2:
time: 120 us; the launch traced here: 119 us
  starting transfers between devices  50.1 us (42%)
  Pallas kernels  35.8 us (30%)
  waiting for transfers between devices  19.5 us (16%)
  blocking collectives  7.68 us (6%)
  local copies, waits for them, and re-layouts  5.35 us (4%)
    pallas_call x5, Pallas kernels, kernel_call(): pl.pallas_call(body, out_shape=out_shape, in_specs=specs, out_specs=outs,...  35.8 us
    ppermute x12, starting transfers between devices, passed_along(): return lax.ppermute(value, axis, pairs)  26.5 us
    all_to_all x2, starting transfers between devices, grouped(): return lax.all_to_all(value, 'tile', 0, 0, axis_index_groups=groups)  15.4 us
    all_to_all x1, starting transfers between devices, local(): lax.all_to_all(sums.reshape(32, C // 8, C), ('tile', 'head'), 0, 0, axis_...  8.2 us
    all_to_all x1, blocking collectives, local(): lax.all_to_all(jnp.broadcast_to(mine[None], (4, 64, 3 * border)), 'head',...  7.68 us
    ppermute x12, waiting for transfers between devices, passed_along(): return lax.ppermute(value, axis, pairs)  6.83 us
    all_to_all x1, waiting for transfers between devices, local(): lax.all_to_all(sums.reshape(32, C // 8, C), ('tile', 'head'), 0, 0, axis_...  6.7 us
    all_to_all x2, waiting for transfers between devices, grouped(): return lax.all_to_all(value, 'tile', 0, 0, axis_index_groups=groups)  6 us
  transfers between devices with their start and end apart: 15, of which 6 were waited for; matrix products, arithmetic and copies ran while one was open for 0% of the time, Pallas kernels for 2%

profile of v2, /device:TPU:1, one launch (start us, length us, event | category | flops | bytes accessed | tf_op | source)
XLA Modules:
  0.0 119.4 jit_solution(3476928440254747798)
XLA Ops:
  0.6 0.0 copy-start.5
  0.6 0.7 copy-done.5
  1.3 0.0 copy-start
  1.3 1.0 copy-done
  2.4 0.0 copy-start.1
  2.4 0.0 copy-start.4
  2.4 1.2 border_rows.1.halo
  3.6 0.0 copy-done.1
  3.6 0.0 copy-done.4
  3.6 0.0 copy-start.3
  3.6 0.9 copy-done.3
  4.5 0.7 prepare.1
  5.1 2.1 %collective-permute-start = (bf16[64,3200]{1,0:T(8,128)(2,1)S(1)}, bf16[64,3200]{1,0:T(8,128)(2,1)S(1)}, u32[]{:S(2)}, u32[]{:S(2)}) collective-permute-start(bf16[64,3200]{1,0:T(8,128)(2,1)S(1)} %get-tuple-element.25), channel_id=1, source_target_pairs={{0,1},{1,2},{2,3},{3,0},{4,5},{5,6},{6,7},{7,4},{8,9},{9,10},{10,1... | collective-permute-start | bytes 1228808 | tf_op jit(solution)/shard_map/exchange/ppermute | solution.py:26
  7.3 2.5 %collective-permute-start.1 = (bf16[64,3200]{1,0:T(8,128)(2,1)S(1)}, bf16[64,3200]{1,0:T(8,128)(2,1)S(1)}, u32[]{:S(2)}, u32[]{:S(2)}) collective-permute-start(bf16[64,3200]{1,0:T(8,128)(2,1)S(1)} %get-tuple-element.26), channel_id=1, source_target_pairs={{0,2},{1,3},{2,0},{3,1},{4,6},{5,7},{6,4},{7,5},{8,10},{9,11},{10,... | collective-permute-start | bytes 1228808 | tf_op jit(solution)/shard_map/exchange/ppermute | solution.py:26
  9.7 1.1 collective-permute-start.2
  10.9 3.1 %collective-permute-start.3 = (bf16[64,128]{1,0:T(8,128)(2,1)S(1)}, bf16[64,128]{1,0:T(8,128)(2,1)S(1)}, u32[]{:S(2)}, u32[]{:S(2)}) collective-permute-start(bf16[64,128]{1,0:T(8,128)(2,1)S(1)} %get-tuple-element.45), channel_id=1, source_target_pairs={{0,4},{4,8},{8,12},{12,16},{16,20},{20,24},{24,28},{28,32},{32,36}... | collective-permute-start | bytes 49160 | tf_op jit(solution)/shard_map/border_rows/ppermute | solution.py:26
  14.0 2.9 %collective-permute-start.5 = (bf16[64,128]{1,0:T(8,128)(2,1)S(1)}, bf16[64,128]{1,0:T(8,128)(2,1)S(1)}, u32[]{:S(2)}, u32[]{:S(2)}) collective-permute-start(bf16[64,128]{1,0:T(8,128)(2,1)S(1)} %get-tuple-element.46), channel_id=1, source_target_pairs={{0,128},{4,132},{8,136},{12,140},{16,144},{20,148},{24,152},{28,15... | collective-permute-start | bytes 49160 | tf_op jit(solution)/shard_map/border_rows/ppermute | solution.py:26
  16.9 0.0 collective-permute-done.3
  16.9 3.9 %collective-permute-start.4 = (bf16[64,128]{1,0:T(8,128)(2,1)S(1)}, bf16[64,128]{1,0:T(8,128)(2,1)S(1)}, u32[]{:S(2)}, u32[]{:S(2)}) collective-permute-start(bf16[64,128]{1,0:T(8,128)(2,1)S(1)} %get-tuple-element.47), channel_id=1, source_target_pairs={{0,252},{4,0},{8,4},{12,8},{16,12},{20,16},{24,20},{28,24},{32,28}... | collective-permute-start | bytes 49160 | tf_op jit(solution)/shard_map/border_rows/ppermute | solution.py:26
  20.8 0.0 collective-permute-done.5
  20.8 0.8 collective-permute-done.4
  21.6 0.0 copy-start.2
  21.7 7.7 %all_to_all.20.far = bf16[4,64,384]{2,1,0:T(8,128)(2,1)S(1)} all-to-all(bf16[4,64,384]{2,1,0:T(8,128)(2,1)S(1)} %broadcast_in_dim.6), channel_id=1, replica_groups=mesh['tile'=64,'head'=4] {'head'}, dimensions={0} | all-to-all | bytes 393216 | tf_op jit(solution)/shard_map/border_rows/all_to_all | solution.py:403
  29.4 0.0 collective-permute-done.c1
  29.4 0.0 collective-permute-done.1.c2
  29.4 0.0 collective-permute-done.2.c3
  29.4 0.0 copy-done.2
  29.4 31.5 %attention.1 = (bf16[64,1536]{1,0:T(8,128)(2,1)S(1)}, bf16[64,1536]{1,0:T(8,128)(2,1)S(1)}, bf16[64,1536]{1,0:T(8,128)(2,1)S(1)}, bf16[64,1536]{1,0:T(8,128)(2,1)S(1)}, bf16[4,256,256]{2,1,0:T(8,128)(2,1)}) custom-call(s32[1]{0:T(128)} %bitcast.place, bf16[64,3200]{1,0:T(8,128)(2,1)S(1)} %get-tuple-element.24.c0, ...), custom_call_target="tpu_custom_call" | custom-call | tf_op jit(solution)/shard_map/attention/pallas_call | solution.py:316
  60.8 8.2 %all-to-all-start.1 = ((bf16[32,32,256]{2,1,0:T(8,128)(2,1)}), bf16[32,32,256]{2,1,0:T(8,128)(2,1)S(1)}, u32[]{:S(2)}, u32[]{:S(2)}) async-start(bf16[32,32,256]{2,1,0:T(8,128)(2,1)} %bitcast.2), calls=%async_computation.1 | async-start | bytes 1048576 | tf_op jit(solution)/shard_map/weight_sums/all_to_all | solution.py:413
  69.1 1.5 %collective-permute-start.6 = (bf16[64,1536]{1,0:T(8,128)(2,1)S(1)}, bf16[64,1536]{1,0:T(8,128)(2,1)S(1)}, u32[]{:S(2)}, u32[]{:S(2)}) collective-permute-start(bf16[64,1536]{1,0:T(8,128)(2,1)S(1)} %get-tuple-element.29), channel_id=1, source_target_pairs={{0,1},{1,2},{2,3},{3,0},{4,5},{5,6},{6,7},{7,4},{8,9},{9,10},{10,1... | collective-permute-start | bytes 589832 | tf_op jit(solution)/shard_map/return/ppermute | solution.py:26
  70.5 2.4 %collective-permute-start.7 = (bf16[64,1536]{1,0:T(8,128)(2,1)S(1)}, bf16[64,1536]{1,0:T(8,128)(2,1)S(1)}, u32[]{:S(2)}, u32[]{:S(2)}) collective-permute-start(bf16[64,1536]{1,0:T(8,128)(2,1)S(1)} %get-tuple-element.30), channel_id=1, source_target_pairs={{0,2},{1,3},{2,0},{3,1},{4,6},{5,7},{6,4},{7,5},{8,10},{9,11},{10,... | collective-permute-start | bytes 589832 | tf_op jit(solution)/shard_map/return/ppermute | solution.py:26
  73.0 1.1 collective-permute-start.8
  74.1 6.7 %all-to-all-done.1 = bf16[32,32,256]{2,1,0:T(8,128)(2,1)S(1)} async-done(((bf16[32,32,256]{2,1,0:T(8,128)(2,1)}), bf16[32,32,256]{2,1,0:T(8,128)(2,1)S(1)}, u32[]{:S(2)}, u32[]{:S(2)}) %all-to-all-start.1) | async-done | bytes 524320 | tf_op jit(solution)/shard_map/weight_sums/all_to_all | solution.py:413
  80.8 0.1 reduce_sum.21
  80.9 1.5 %collective-permute-done.6.r1 = bf16[64,1536]{1,0:T(8,128)(2,1)S(1)} collective-permute-done((bf16[64,1536]{1,0:T(8,128)(2,1)S(1)}, bf16[64,1536]{1,0:T(8,128)(2,1)S(1)}, u32[]{:S(2)}, u32[]{:S(2)}) %collective-permute-start.6) | collective-permute-done | bytes 196640 | tf_op jit(solution)/shard_map/return/ppermute | solution.py:26
  82.4 4.5 %collective-permute-done.7.r2 = bf16[64,1536]{1,0:T(8,128)(2,1)S(1)} collective-permute-done((bf16[64,1536]{1,0:T(8,128)(2,1)S(1)}, bf16[64,1536]{1,0:T(8,128)(2,1)S(1)}, u32[]{:S(2)}, u32[]{:S(2)}) %collective-permute-start.7) | collective-permute-done | bytes 196640 | tf_op jit(solution)/shard_map/return/ppermute | solution.py:26
  86.9 0.0 collective-permute-done.8.r3
  86.9 0.7 broadcast_in_dim.7
  87.5 8.2 %all-to-all-start.2 = ((bf16[8,32,256]{2,1,0:T(8,128)(2,1)}), bf16[8,32,256]{2,1,0:T(8,128)(2,1)S(1)}, u32[]{:S(2)}, u32[]{:S(2)}) async-start(bf16[8,32,256]{2,1,0:T(8,128)(2,1)} %broadcast_in_dim.7), calls=%async_computation.2 | async-start | bytes 262144 | tf_op jit(solution)/shard_map/weight_sums/all_to_all | solution.py:30
  95.7 1.2 %collective-permute-start.9 = (bf16[64,128]{1,0:T(8,128)(2,1)S(1)}, bf16[64,128]{1,0:T(8,128)(2,1)S(1)}, u32[]{:S(2)}, u32[]{:S(2)}) collective-permute-start(bf16[64,128]{1,0:T(8,128)(2,1)S(1)} %get-tuple-element.37), channel_id=1, source_target_pairs={{0,252},{4,0},{8,4},{12,8},{16,12},{20,16},{24,20},{28,24},{32,28}... | collective-permute-start | bytes 49160 | tf_op jit(solution)/shard_map/return/ppermute | solution.py:26
  97.0 1.9 %collective-permute-start.10 = (bf16[64,128]{1,0:T(8,128)(2,1)S(1)}, bf16[64,128]{1,0:T(8,128)(2,1)S(1)}, u32[]{:S(2)}, u32[]{:S(2)}) collective-permute-start(bf16[64,128]{1,0:T(8,128)(2,1)S(1)} %get-tuple-element.38), channel_id=1, source_target_pairs={{0,4},{4,8},{8,12},{12,16},{16,20},{20,24},{24,28},{28,32},{32,36}... | collective-permute-start | bytes 49160 | tf_op jit(solution)/shard_map/return/ppermute | solution.py:26
  98.9 2.7 %collective-permute-start.11 = (bf16[64,128]{1,0:T(8,128)(2,1)S(1)}, bf16[64,128]{1,0:T(8,128)(2,1)S(1)}, u32[]{:S(2)}, u32[]{:S(2)}) collective-permute-start(bf16[64,128]{1,0:T(8,128)(2,1)S(1)} %get-tuple-element.39), channel_id=1, source_target_pairs={{0,128},{4,132},{8,136},{12,140},{16,144},{20,148},{24,152},{28,15... | collective-permute-start | bytes 49160 | tf_op jit(solution)/shard_map/return/ppermute | solution.py:26
  101.6 2.0 %all-to-all-done.2 = bf16[8,32,256]{2,1,0:T(8,128)(2,1)S(1)} async-done(((bf16[8,32,256]{2,1,0:T(8,128)(2,1)}), bf16[8,32,256]{2,1,0:T(8,128)(2,1)S(1)}, u32[]{:S(2)}, u32[]{:S(2)}) %all-to-all-start.2) | async-done | bytes 131104 | tf_op jit(solution)/shard_map/weight_sums/all_to_all | solution.py:30
  103.6 0.0 collective-permute-done.9.b0
  103.6 0.0 collective-permute-done.10.b1
  103.6 0.0 collective-permute-done.11.b2
  103.6 0.7 broadcast_in_dim.8
  104.3 7.2 %all-to-all-start.3 = ((f32[8,32,256]{2,1,0:T(8,128)}), f32[8,32,256]{2,1,0:T(8,128)S(1)}, u32[]{:S(2)}, u32[]{:S(2)}) async-start(f32[8,32,256]{2,1,0:T(8,128)} %broadcast_in_dim.8), calls=%async_computation.3 | async-start | bytes 524288 | tf_op jit(solution)/shard_map/weight_sums/all_to_all | solution.py:30
  111.5 2.5 %return.3 = f32[64,4096]{1,0:T(8,128)} custom-call(s32[1]{0:T(128)} %bitcast.place, bf16[64,1536]{1,0:T(8,128)(2,1)S(1)} %get-tuple-element.33.r0, bf16[64,1536]{1,0:T(8,128)(2,1)S(1)} %collective-permute-done.6.r1, bf16[64,1536]{1,0:T(8,128)(2,1)S(1)} %collective-permute-done.7.r2, bf16[64,1536]{1,0:T(8,128)(2,1)S(1)} %collective-permute-done.8.r3, ...), custom_call_target="tpu_custom_call" | custom-call | tf_op jit(solution)/shard_map/return/pallas_call | solution.py:316
  114.0 4.0 %all-to-all-done.3 = f32[8,32,256]{2,1,0:T(8,128)S(1)} async-done(((f32[8,32,256]{2,1,0:T(8,128)}), f32[8,32,256]{2,1,0:T(8,128)S(1)}, u32[]{:S(2)}, u32[]{:S(2)}) %all-to-all-start.3) | async-done | bytes 262176 | tf_op jit(solution)/shard_map/weight_sums/all_to_all | solution.py:30
  118.1 0.6 slice.29
  118.7 0.7 slice.28
  (6 shorter events, 0.1 us)
Async XLA Ops:
  0.6 0.7 copy-start.5
  1.3 1.0 copy-start
  2.4 1.2 %copy-start.1 = (bf16[64,4096]{1,0:T(8,128)(2,1)S(1)}, bf16[64,4096]{1,0:T(8,128)(2,1)}, u32[]{:S(2)}) copy-start(bf16[64,4096]{1,0:T(8,128)(2,1)} %grad_in.3) | copy-start | bytes 1572868
  2.4 1.2 %copy-start.4 = (bf16[64,256]{1,0:T(8,128)(2,1)S(1)}, bf16[64,256]{1,0:T(8,128)(2,1)}, u32[]{:S(2)}) copy-start(bf16[64,256]{1,0:T(8,128)(2,1)} %w_out.1) | copy-start | bytes 98308
  3.6 0.9 copy-start.3
  5.1 24.2 %collective-permute-start = (bf16[64,3200]{1,0:T(8,128)(2,1)S(1)}, bf16[64,3200]{1,0:T(8,128)(2,1)S(1)}, u32[]{:S(2)}, u32[]{:S(2)}) collective-permute-start(bf16[64,3200]{1,0:T(8,128)(2,1)S(1)} %get-tuple-element.25), channel_id=1, source_target_pairs={{0,1},{1,2},{2,3},{3,0},{4,5},{5,6},{6,7},{7,4},{8,9},{9,10},{10,1... | collective-permute-start | bytes 1228808 | tf_op jit(solution)/shard_map/exchange/ppermute | solution.py:26
  7.3 22.1 %collective-permute-start.1 = (bf16[64,3200]{1,0:T(8,128)(2,1)S(1)}, bf16[64,3200]{1,0:T(8,128)(2,1)S(1)}, u32[]{:S(2)}, u32[]{:S(2)}) collective-permute-start(bf16[64,3200]{1,0:T(8,128)(2,1)S(1)} %get-tuple-element.26), channel_id=1, source_target_pairs={{0,2},{1,3},{2,0},{3,1},{4,6},{5,7},{6,4},{7,5},{8,10},{9,11},{10,... | collective-permute-start | bytes 1228808 | tf_op jit(solution)/shard_map/exchange/ppermute | solution.py:26
  9.7 19.7 %collective-permute-start.2 = (bf16[64,3200]{1,0:T(8,128)(2,1)S(1)}, bf16[64,3200]{1,0:T(8,128)(2,1)S(1)}, u32[]{:S(2)}, u32[]{:S(2)}) collective-permute-start(bf16[64,3200]{1,0:T(8,128)(2,1)S(1)} %get-tuple-element.27), channel_id=1, source_target_pairs={{0,3},{1,0},{2,1},{3,2},{4,7},{5,4},{6,5},{7,6},{8,11},{9,8},{10,9... | collective-permute-start | bytes 1228808 | tf_op jit(solution)/shard_map/exchange/ppermute | solution.py:26
  10.9 6.0 %collective-permute-start.3 = (bf16[64,128]{1,0:T(8,128)(2,1)S(1)}, bf16[64,128]{1,0:T(8,128)(2,1)S(1)}, u32[]{:S(2)}, u32[]{:S(2)}) collective-permute-start(bf16[64,128]{1,0:T(8,128)(2,1)S(1)} %get-tuple-element.45), channel_id=1, source_target_pairs={{0,4},{4,8},{8,12},{12,16},{16,20},{20,24},{24,28},{28,32},{32,36}... | collective-permute-start | bytes 49160 | tf_op jit(solution)/shard_map/border_rows/ppermute | solution.py:26
  14.0 6.8 %collective-permute-start.5 = (bf16[64,128]{1,0:T(8,128)(2,1)S(1)}, bf16[64,128]{1,0:T(8,128)(2,1)S(1)}, u32[]{:S(2)}, u32[]{:S(2)}) collective-permute-start(bf16[64,128]{1,0:T(8,128)(2,1)S(1)} %get-tuple-element.46), channel_id=1, source_target_pairs={{0,128},{4,132},{8,136},{12,140},{16,144},{20,148},{24,152},{28,15... | collective-permute-start | bytes 49160 | tf_op jit(solution)/shard_map/border_rows/ppermute | solution.py:26
  16.9 4.7 %collective-permute-start.4 = (bf16[64,128]{1,0:T(8,128)(2,1)S(1)}, bf16[64,128]{1,0:T(8,128)(2,1)S(1)}, u32[]{:S(2)}, u32[]{:S(2)}) collective-permute-start(bf16[64,128]{1,0:T(8,128)(2,1)S(1)} %get-tuple-element.47), channel_id=1, source_target_pairs={{0,252},{4,0},{8,4},{12,8},{16,12},{20,16},{24,20},{28,24},{32,28}... | collective-permute-start | bytes 49160 | tf_op jit(solution)/shard_map/border_rows/ppermute | solution.py:26
  21.6 7.7 %copy-start.2 = (s32[9,4096]{1,0:T(8,128)S(1)}, s32[9,4096]{1,0:T(8,128)}, u32[]{:S(2)}) copy-start(s32[9,4096]{1,0:T(8,128)} %neighbors.1) | copy-start | bytes 442372
  60.8 20.0 %all-to-all-start.1 = ((bf16[32,32,256]{2,1,0:T(8,128)(2,1)}), bf16[32,32,256]{2,1,0:T(8,128)(2,1)S(1)}, u32[]{:S(2)}, u32[]{:S(2)}) async-start(bf16[32,32,256]{2,1,0:T(8,128)(2,1)} %bitcast.2), calls=%async_computation.1 | async-start | bytes 1048576 | tf_op jit(solution)/shard_map/weight_sums/all_to_all | solution.py:413
  69.1 13.3 %collective-permute-start.6 = (bf16[64,1536]{1,0:T(8,128)(2,1)S(1)}, bf16[64,1536]{1,0:T(8,128)(2,1)S(1)}, u32[]{:S(2)}, u32[]{:S(2)}) collective-permute-start(bf16[64,1536]{1,0:T(8,128)(2,1)S(1)} %get-tuple-element.29), channel_id=1, source_target_pairs={{0,1},{1,2},{2,3},{3,0},{4,5},{5,6},{6,7},{7,4},{8,9},{9,10},{10,1... | collective-permute-start | bytes 589832 | tf_op jit(solution)/shard_map/return/ppermute | solution.py:26
  70.5 16.3 %collective-permute-start.7 = (bf16[64,1536]{1,0:T(8,128)(2,1)S(1)}, bf16[64,1536]{1,0:T(8,128)(2,1)S(1)}, u32[]{:S(2)}, u32[]{:S(2)}) collective-permute-start(bf16[64,1536]{1,0:T(8,128)(2,1)S(1)} %get-tuple-element.30), channel_id=1, source_target_pairs={{0,2},{1,3},{2,0},{3,1},{4,6},{5,7},{6,4},{7,5},{8,10},{9,11},{10,... | collective-permute-start | bytes 589832 | tf_op jit(solution)/shard_map/return/ppermute | solution.py:26
  73.0 13.9 %collective-permute-start.8 = (bf16[64,1536]{1,0:T(8,128)(2,1)S(1)}, bf16[64,1536]{1,0:T(8,128)(2,1)S(1)}, u32[]{:S(2)}, u32[]{:S(2)}) collective-permute-start(bf16[64,1536]{1,0:T(8,128)(2,1)S(1)} %get-tuple-element.31), channel_id=1, source_target_pairs={{0,3},{1,0},{2,1},{3,2},{4,7},{5,4},{6,5},{7,6},{8,11},{9,8},{10,9... | collective-permute-start | bytes 589832 | tf_op jit(solution)/shard_map/return/ppermute | solution.py:26
  87.5 16.0 %all-to-all-start.2 = ((bf16[8,32,256]{2,1,0:T(8,128)(2,1)}), bf16[8,32,256]{2,1,0:T(8,128)(2,1)S(1)}, u32[]{:S(2)}, u32[]{:S(2)}) async-start(bf16[8,32,256]{2,1,0:T(8,128)(2,1)} %broadcast_in_dim.7), calls=%async_computation.2 | async-start | bytes 262144 | tf_op jit(solution)/shard_map/weight_sums/all_to_all | solution.py:30
  95.7 7.9 %collective-permute-start.9 = (bf16[64,128]{1,0:T(8,128)(2,1)S(1)}, bf16[64,128]{1,0:T(8,128)(2,1)S(1)}, u32[]{:S(2)}, u32[]{:S(2)}) collective-permute-start(bf16[64,128]{1,0:T(8,128)(2,1)S(1)} %get-tuple-element.37), channel_id=1, source_target_pairs={{0,252},{4,0},{8,4},{12,8},{16,12},{20,16},{24,20},{28,24},{32,28}... | collective-permute-start | bytes 49160 | tf_op jit(solution)/shard_map/return/ppermute | solution.py:26
  97.0 6.6 %collective-permute-start.10 = (bf16[64,128]{1,0:T(8,128)(2,1)S(1)}, bf16[64,128]{1,0:T(8,128)(2,1)S(1)}, u32[]{:S(2)}, u32[]{:S(2)}) collective-permute-start(bf16[64,128]{1,0:T(8,128)(2,1)S(1)} %get-tuple-element.38), channel_id=1, source_target_pairs={{0,4},{4,8},{8,12},{12,16},{16,20},{20,24},{24,28},{28,32},{32,36}... | collective-permute-start | bytes 49160 | tf_op jit(solution)/shard_map/return/ppermute | solution.py:26
  98.9 4.7 %collective-permute-start.11 = (bf16[64,128]{1,0:T(8,128)(2,1)S(1)}, bf16[64,128]{1,0:T(8,128)(2,1)S(1)}, u32[]{:S(2)}, u32[]{:S(2)}) collective-permute-start(bf16[64,128]{1,0:T(8,128)(2,1)S(1)} %get-tuple-element.39), channel_id=1, source_target_pairs={{0,128},{4,132},{8,136},{12,140},{16,144},{20,148},{24,152},{28,15... | collective-permute-start | bytes 49160 | tf_op jit(solution)/shard_map/return/ppermute | solution.py:26
  104.3 13.7 %all-to-all-start.3 = ((f32[8,32,256]{2,1,0:T(8,128)}), f32[8,32,256]{2,1,0:T(8,128)S(1)}, u32[]{:S(2)}, u32[]{:S(2)}) async-start(f32[8,32,256]{2,1,0:T(8,128)} %broadcast_in_dim.8), calls=%async_computation.3 | async-start | bytes 524288 | tf_op jit(solution)/shard_map/weight_sums/all_to_all | solution.py:30

commit v3 on v2

--- a/solution.py
+++ b/solution.py
@@ -14,6 +14,7 @@
 BLOCK = 128
 SIDE = 64
 CHUNK = 128
+PARTS = 32
 WINDOW = BLOCK + 2 * SIDE
 LOG2E = math.log2(math.e)
 F32 = jnp.float32
@@ -26,15 +27,16 @@
     return lax.ppermute(value, axis, pairs)
 
 
-def grouped(value, groups):
-    return lax.all_to_all(value, "tile", 0, 0, axis_index_groups=groups)
-
-
-def plates(heads):
-    return [
-        [(16 * y + 2 * z + c) * heads + h for h in range(heads) for y in range(4) for c in range(2)]
-        for z in range(8)
-    ]
+def rank(y, z, core):
+    return 16 * y + 2 * z + core
+
+
+PLATES = [[rank(y, z, core) for y in range(4) for core in range(2)] for z in range(8)]
+SHEETS = [
+    [rank(y, z, core) * 4 + head for z in range(8) for head in range(4)]
+    for y in range(4)
+    for core in range(2)
+]
 
 
 def vmem_spec():
@@ -121,10 +123,33 @@
         fetch.wait()
 
 
+def masks(place, neighbors, bias):
+    head = place[0]
+    rows_all = neighbors.shape[1]
+    blocks, cand, _ = bias.shape
+
+    def step(b, carry):
+        first = head * (rows_all // 4) + b * BLOCK
+        near = neighbors[:, pl.ds(pl.multiple_of(first, BLOCK), BLOCK)]
+        shifted = (near - (first - SIDE)) & (rows_all - 1)
+        index = jnp.where(near < rows_all, shifted, near - rows_all + WINDOW)
+        for start in range(0, cand, CHUNK):
+            rows = lax.broadcasted_iota(jnp.int32, (CHUNK, BLOCK), 0) + start
+            count = jnp.zeros((CHUNK, BLOCK), F32)
+            for slot in range(NBR):
+                count = count + jnp.where(rows == index[slot : slot + 1, :], 1.0, 0.0)
+            bias[b, start : start + CHUNK, :] = jnp.where(
+                count > 0.5, jnp.log(count) * LOG2E, -1e30
+            )
+        return carry
+
+    lax.fori_loop(0, blocks, step, 0)
+
+
 def attend(
-    place, c0, c1, c2, c3, far, neighbors, o0, o1, o2, o3, sums,
-    xe, dy, wq, wkv, wo, qs, ds, kvt, kv, dkv, da, dkvt, grads, summed, bias,
-    products0, products1, weights0, weights1,
+    place, c0, c1, c2, c3, far, bias, o0, o1, o2, o3, sums,
+    xe, dy, wq, wkv, wo, qs, ds, kvt, kv, dkv, da, dkvt, grads, summed,
+    products0, products1, weights0, weights1, means0, means1, qt, dt,
 ):
     head = place[0]
     own = dy.shape[1]
@@ -132,7 +157,6 @@
     full = xe.shape[1]
     border = full - ext
     cand = WINDOW + border
-    rows_all = neighbors.shape[1]
     scale = 1.0 / math.sqrt(HEAD_DIM)
     wq[...] = jnp.zeros_like(wq)
     wo[...] = jnp.zeros_like(wo)
@@ -150,17 +174,20 @@
             wkv[pl.ds(dest, 32), :] = chunk[part, base + C : base + 2 * C]
             wkv[pl.ds(dest + 32, 32), :] = chunk[part, base + 2 * C : base + 3 * C]
             wo[pl.ds(dest + 32, 32), :] = chunk[part, base + 3 * C :]
-    for start in range(0, full, 128):
-        cols = slice(start, start + 128)
+    for start in range(0, full, 256):
+        cols = slice(start, start + 256)
         block = nn(wkv[...], xe[:, cols]).astype(BF16)
         kvt[:, cols] = block
         kv[cols, :] = block.T
-    for start in range(0, ext, 128):
-        cols = slice(start, start + 128)
+    for start in range(0, ext, 384):
+        cols = slice(start, start + 384)
         qs[cols, :] = nn(wq[...], xe[:, cols]).astype(BF16).T
-    for start in range(0, own, 128):
-        cols = slice(start, start + 128)
-        ds[cols, :] = nn(wo[...], dy[:, cols]).astype(BF16).T
+    for start in range(0, own, 256):
+        cols = slice(start, start + 256)
+        block = nn(wo[...], dy[:, cols]).astype(BF16)
+        dt[:, cols] = block
+        ds[cols, :] = block.T
+        qt[:, cols] = qs[start + SIDE : start + SIDE + 256, :].T
     dkv[...] = jnp.zeros_like(dkv)
     da[:, own:] = jnp.zeros((2 * C, 2 * SIDE), F32)
     lane_head = lax.broadcasted_iota(jnp.int32, (BLOCK, C), 1) // 64
@@ -179,85 +206,96 @@
     def multiply(b, g, hh, products):
         first = pl.multiple_of(b * BLOCK, BLOCK)
         cols = slice(C * g, C * g + C)
-        out = slice(C * hh, C * hh + C)
-        both = jnp.concatenate([kv[pl.ds(first, WINDOW), cols], kv[ext:, cols]], axis=0)
-        products[:, out] = nt(both, operands(b, g, hh))
-
-    def weigh(hh, products, weights):
+        out = slice(C * hh, C * hh + 2 * C)
+        stack = jnp.concatenate([operands(b, g, hh), operands(b, g, hh + 1)], axis=0)
+        products[:WINDOW, out] = nt(kv[pl.ds(first, WINDOW), cols], stack)
+        products[WINDOW:, out] = nt(kv[ext:, cols], stack)
+
+    def first_pass(block, hh, products):
+        left = slice(C * hh, C * hh + BLOCK)
+        acc = jnp.zeros((PARTS, BLOCK), F32)
+        for start in range(0, cand, CHUNK):
+            rows = slice(start, start + CHUNK)
+            expon = jnp.exp2(products[rows, left] * (scale * LOG2E) + bias[block, rows, :])
+            products[rows, left] = expon
+            acc = acc + expon.reshape(CHUNK // PARTS, PARTS, BLOCK).sum(0)
+        return 1.0 / jnp.sum(acc, axis=0, keepdims=True)
+
+    def second_pass(hh, products, weights, means, inverse):
         left = slice(C * hh, C * hh + BLOCK)
         right = slice(C * hh + BLOCK, C * hh + C)
-        acc = jnp.zeros((8, BLOCK), F32)
-        for start in range(0, cand, CHUNK):
-            rows = slice(start, start + CHUNK)
-            expon = jnp.exp2(products[rows, left] * (scale * LOG2E) + bias[rows, :])
-            products[rows, left] = expon
-            acc = acc + expon.reshape(CHUNK // 8, 8, BLOCK).sum(0)
-        inverse = 1.0 / jnp.sum(acc, axis=0, keepdims=True)
-        acc = jnp.zeros((8, BLOCK), F32)
-        for start in range(0, cand, CHUNK):
-            rows = slice(start, start + CHUNK)
-            term = (products[rows, left] * inverse) * products[rows, right]
-            acc = acc + term.reshape(CHUNK // 8, 8, BLOCK).sum(0)
-        mean = jnp.sum(acc, axis=0, keepdims=True)
+        acc = jnp.zeros((PARTS, BLOCK), F32)
         for start in range(0, cand, CHUNK):
             rows = slice(start, start + CHUNK)
             prob = products[rows, left] * inverse
-            weights[rows, left] = (prob * (products[rows, right] - mean)).astype(BF16)
+            term = prob * products[rows, right]
+            weights[rows, left] = term.astype(BF16)
             weights[rows, right] = prob.astype(BF16)
-
-    def gather_rows(b, g, hh, weights):
+            acc = acc + term.reshape(CHUNK // PARTS, PARTS, BLOCK).sum(0)
+        means[hh : hh + 1, :] = jnp.sum(acc, axis=0, keepdims=True)
+
+    def gather_rows(b, g, hh, weights, means):
         first = pl.multiple_of(b * BLOCK, BLOCK)
         top = C * g + 64 * hh
         pair = jnp.concatenate(
             [kvt[top : top + 64, pl.ds(first, WINDOW)], kvt[top : top + 64, ext:]], axis=1
         )
         result = nn(pair, weights[:, C * hh : C * hh + C])
-        da[top : top + 32, pl.ds(first, BLOCK)] = result[:32, :BLOCK] * scale
+        grad_query = result[:32, :BLOCK] - result[:32, BLOCK:] * means[hh : hh + 1, :]
+        da[top : top + 32, pl.ds(first, BLOCK)] = grad_query * scale
         da[top + 32 : top + 64, pl.ds(first, BLOCK)] = result[32:, BLOCK:]
 
-    def spread(b, g, weights):
+    def spread(b, g, hh, weights, means):
         first = pl.multiple_of(b * BLOCK, BLOCK)
-        cols = slice(C * g, C * g + C)
-        stack = jnp.concatenate([operands(b, g, hh) for hh in range(4)], axis=0)
-        total = nn(weights[...], stack)
-        dkv[pl.ds(first, WINDOW), cols] += total[:WINDOW]
-        dkv[ext:, cols] += total[WINDOW:]
+        top = C * g + 64 * hh
+        query = qt[top : top + 64, pl.ds(first, BLOCK)]
+        dout = dt[top : top + 64, pl.ds(first, BLOCK)]
+        second = dout - (query.astype(F32) * means[hh : hh + 1, :]).astype(BF16)
+        both = jnp.concatenate([query, second], axis=1)
+        cols = slice(C * hh, C * hh + C)
+        dkv[top : top + 64, pl.ds(first, WINDOW)] += nt(both, weights[:WINDOW, cols])
+        dkv[top : top + 64, ext:] += nt(both, weights[WINDOW:, cols])
+
+    def phase(block, ahead, group, behind, products, weights, means, products_next, weights_done, means_done):
+        inv0 = first_pass(block, 0, products)
+        multiply(*ahead, 0, products_next)
+        second_pass(0, products, weights, means, inv0)
+        gather_rows(*behind, 0, weights_done, means_done)
+        spread(*behind, 0, weights_done, means_done)
+        inv1 = first_pass(block, 1, products)
+        second_pass(1, products, weights, means, inv1)
+        gather_rows(*behind, 1, weights_done, means_done)
+        spread(*behind, 1, weights_done, means_done)
+        inv2 = first_pass(block, 2, products)
+        multiply(*ahead, 2, products_next)
+        second_pass(2, products, weights, means, inv2)
+        gather_rows(*behind, 2, weights_done, means_done)
+        spread(*behind, 2, weights_done, means_done)
+        inv3 = first_pass(block, 3, products)
+        second_pass(3, products, weights, means, inv3)
+        gather_rows(*behind, 3, weights_done, means_done)
+        spread(*behind, 3, weights_done, means_done)
 
     def step(b, carry):
-        near = neighbors[:, pl.ds(pl.multiple_of(head * own + b * BLOCK, BLOCK), BLOCK)]
-        shifted = (near - (head * own + b * BLOCK - SIDE)) & (rows_all - 1)
-        index = jnp.where(near < rows_all, shifted, near - rows_all + WINDOW)
-        for start in range(0, cand, CHUNK):
-            rows = lax.broadcasted_iota(jnp.int32, (CHUNK, BLOCK), 0) + start
-            count = jnp.zeros((CHUNK, BLOCK), F32)
-            for slot in range(NBR):
-                count = count + jnp.where(rows == index[slot : slot + 1, :], 1.0, 0.0)
-            bias[start : start + CHUNK, :] = jnp.where(count > 0.5, jnp.log(count) * LOG2E, -1e30)
         before = jnp.maximum(b - 1, 0)
         after = jnp.minimum(b + 1, last)
-        for hh in range(4):
-            multiply(b, 1, hh, products1)
-            weigh(hh, products0, weights0)
-            gather_rows(before, 1, hh, weights1)
-        spread(before, 1, weights1)
-        for hh in range(4):
-            multiply(after, 0, hh, products0)
-            weigh(hh, products1, weights1)
-            gather_rows(b, 0, hh, weights0)
-        spread(b, 0, weights0)
+        phase(b, (b, 1), 0, (before, 1), products0, weights0, means0, products1, weights1, means1)
+        phase(b, (after, 0), 1, (b, 0), products1, weights1, means1, products0, weights0, means0)
         return carry
 
     weights1[...] = jnp.zeros_like(weights1)
-    for hh in range(4):
+    means0[...] = jnp.zeros_like(means0)
+    means1[...] = jnp.zeros_like(means1)
+    for hh in (0, 2):
         multiply(0, 0, hh, products0)
     lax.fori_loop(0, own // BLOCK, step, 0)
     for hh in range(4):
-        gather_rows(last, 1, hh, weights1)
-    spread(last, 1, weights1)
-    col_scale = jnp.where((lax.broadcasted_iota(jnp.int32, (128, 2 * C), 1) & 63) < 32, scale, 1.0)
+        gather_rows(last, 1, hh, weights1, means1)
+        spread(last, 1, hh, weights1, means1)
+    row_scale = jnp.where((lax.broadcasted_iota(jnp.int32, (2 * C, 128), 0) & 63) < 32, scale, 1.0)
     for start in range(0, full, 128):
-        rows = slice(start, start + 128)
-        dkvt[:, rows] = (dkv[rows, :] * col_scale).astype(BF16).T
+        cols = slice(start, start + 128)
+        dkvt[:, cols] = (dkv[:, cols] * row_scale).astype(BF16)
     own_grads = pltpu.roll(da[...], SIDE, 1).astype(BF16)
     summed[:, :ext] = (tn(wkv[...], dkvt[:, :ext]) + tn(wq[...], own_grads)).astype(BF16)
     summed[:, ext:] = tn(wkv[...], dkvt[:, ext:]).astype(BF16)
@@ -271,9 +309,7 @@
         for k in range(2):
             top = 128 * target + 64 * k
             for kind, (which, low) in enumerate(((0, 0), (1, 0), (1, 32), (2, 32))):
-                sums[target, 64 * kind + 32 * k : 64 * kind + 32 * k + 32, :] = grads[
-                    which, top + low : top + low + 32, :
-                ]
+                sums[2 * kind + k, target] = grads[which, top + low : top + low + 32, :]
 
 
 def add_up(r0, r1, r2, r3, b0, b1, b2):
@@ -303,7 +339,7 @@
         out[:, cols] = grad_in[:, cols].astype(F32) + aligned[:, cols] + returned
 
 
-def kernel_call(body, out_shape, inputs, scratch=(), mib=48, loose=()):
+def kernel_call(body, out_shape, inputs, scratch=(), mib=12, loose=()):
     specs = []
     for place, value in enumerate(inputs):
         if value.dtype == jnp.int32 and value.size == 1:
@@ -328,11 +364,13 @@
 
 
 def attend_call(place, *args):
-    *inputs, own, ext, full, cand = args
+    *inputs, neighbors, own, ext, full, cand = args
+    with jax.named_scope("masks"):
+        bias = kernel_call(masks, sds((own // BLOCK, cand, BLOCK), F32), (place, neighbors))
     return kernel_call(
         attend,
-        [sds((64, full), BF16)] * 4 + [sds((4, C, C), BF16)],
-        (place, *inputs),
+        [sds((64, full), BF16)] * 4 + [sds((8, 4, C // 8, C), BF16)],
+        (place, *inputs, bias),
         [
             pltpu.VMEM((C, full), BF16),
             pltpu.VMEM((C, own), BF16),
@@ -343,17 +381,21 @@
             pltpu.VMEM((own, 2 * C), BF16),
             pltpu.VMEM((2 * C, full), BF16),
             pltpu.VMEM((full, 2 * C), BF16),
-            pltpu.VMEM((full, 2 * C), F32),
+            pltpu.VMEM((2 * C, full), F32),
             pltpu.VMEM((2 * C, ext), F32),
             pltpu.VMEM((2 * C, full), BF16),
             pltpu.VMEM((3, 2 * C, C), BF16),
             pltpu.VMEM((C, full), BF16),
-            pltpu.VMEM((cand, BLOCK), F32),
             pltpu.VMEM((cand, 4 * C), F32),
             pltpu.VMEM((cand, 4 * C), F32),
             pltpu.VMEM((cand, 4 * C), BF16),
             pltpu.VMEM((cand, 4 * C), BF16),
+            pltpu.VMEM((8, BLOCK), F32),
+            pltpu.VMEM((8, BLOCK), F32),
+            pltpu.VMEM((2 * C, own), BF16),
+            pltpu.VMEM((2 * C, own), BF16),
         ],
+        mib=36,
     )
 
 
@@ -410,9 +452,7 @@
     with jax.named_scope("return"):
         parts = [parts[0]] + [passed_along(parts[step], "head", step) for step in (1, 2, 3)]
     with jax.named_scope("weight_sums"):
-        value = lax.all_to_all(
-            sums.reshape(32, C // 8, C), ("tile", "head"), 0, 0, axis_index_groups=plates(4)
-        )
+        value = lax.all_to_all(sums, "tile", 0, 0, axis_index_groups=PLATES)
         value = value.astype(F32).sum(0).astype(BF16)
         *parts, value = lax.optimization_barrier((*parts, value))
     with jax.named_scope("return"):
@@ -422,14 +462,13 @@
             for peer in range(3)
         ]
     with jax.named_scope("weight_sums"):
-        line = [[16 * y + 2 * z + c for z in range(8)] for y in range(4) for c in range(2)]
-        piece = (8, C // 8, C)
-        value = grouped(jnp.broadcast_to(value[None], piece), line)
-        value = value.astype(F32).sum(0)
+        value = jnp.broadcast_to(value[None], (8, 4, C // 8, C)).reshape(32, C // 8, C)
+        value = lax.all_to_all(value, ("tile", "head"), 0, 0, axis_index_groups=SHEETS)
+        value = value.astype(F32).sum(0) * (1.0 / math.sqrt(rows * groups))
         *back, value = lax.optimization_barrier((*back, value))
-        value = grouped(jnp.broadcast_to(value[None], piece), plates(1))
-        grad_scale = 1.0 / math.sqrt(rows * groups)
-        value = value.reshape(4, 64, C) * grad_scale
+        value = jnp.broadcast_to(value[None], (8, C // 8, C))
+        value = lax.all_to_all(value, "tile", 0, 0, axis_index_groups=PLATES)
+        value = value.reshape(4, 64, C)
     with jax.named_scope("return"):
         d_tokens = kernel_call(
             finish,

time: 120 us -> 126 us (1.050)
  blocking collectives: 7.68 us -> 0 us
  waiting for transfers between devices: 19.5 us -> 26.6 us
  local copies, waits for them, and re-layouts: 5.35 us -> 11 us
    all_to_all x3 -> x4, waiting for transfers between devices: 12.7 us -> 23.1 us  [the longest x1 11.5 us: local(): lax.all_to_all(value, ('tile', 'head'), 0, 0, axis_index_groups=SHEETS)]
    all_to_all x1 -> x0, blocking collectives: 7.68 us -> none  [local(): lax.all_to_all(jnp.broadcast_to(mine[None], (4, 64, 3 * border)), 'head',...]
    unnamed x12 -> x22, local copies, waits for them, and re-layouts: 2.61 us -> 7.38 us
    ppermute x12, waiting for transfers between devices: 6.83 us -> 3.53 us  [passed_along(): return lax.ppermute(value, axis, pairs)]
    all_to_all x3 -> x4, starting transfers between devices: 23.6 us -> 26.5 us  [the longest x1 10.4 us: local(): lax.all_to_all(value, ('tile', 'head'), 0, 0, axis_index_groups=SHEETS)]
    ppermute x12, starting transfers between devices: 26.5 us -> 23.9 us  [passed_along(): return lax.ppermute(value, axis, pairs)]
    pallas_call x5 -> x6, Pallas kernels: 35.8 us -> 36.3 us  [kernel_call(): pl.pallas_call(body, out_shape=out_shape, in_specs=specs, out_specs=outs,...]
  transfers between devices with their start and end apart: 15 -> 16, of which waited for: 6 -> 7; matrix products, arithmetic and copies ran while one was open for 0% -> 1% of each run, Pallas kernels for 2% -> 4%
where the time goes in v3:
time: 126 us; the launch traced here: 125 us
  starting transfers between devices  50.4 us (40%)
  Pallas kernels  36.3 us (29%)
  waiting for transfers between devices  26.6 us (21%)
  local copies, waits for them, and re-layouts  11 us (9%)
    pallas_call x6, Pallas kernels, kernel_call(): pl.pallas_call(body, out_shape=out_shape, in_specs=specs, out_specs=outs,...  36.3 us
    ppermute x12, starting transfers between devices, passed_along(): return lax.ppermute(value, axis, pairs)  23.9 us
    all_to_all x1, waiting for transfers between devices, local(): lax.all_to_all(value, ('tile', 'head'), 0, 0, axis_index_groups=SHEETS)  11.5 us
    all_to_all x1, starting transfers between devices, local(): lax.all_to_all(value, ('tile', 'head'), 0, 0, axis_index_groups=SHEETS)  10.4 us
    unnamed x22, local copies, waits for them, and re-layouts  7.38 us
    all_to_all x1, starting transfers between devices, local(): value = lax.all_to_all(value, 'tile', 0, 0, axis_index_groups=PLATES)  6.54 us
    all_to_all x1, waiting for transfers between devices, local(): value = lax.all_to_all(sums, 'tile', 0, 0, axis_index_groups=PLATES)  6.43 us
    all_to_all x1, starting transfers between devices, local(): value = lax.all_to_all(sums, 'tile', 0, 0, axis_index_groups=PLATES)  6.06 us
  transfers between devices with their start and end apart: 16, of which 7 were waited for; matrix products, arithmetic and copies ran while one was open for 1% of the time, Pallas kernels for 4%

profile of v3, /device:TPU:1, one launch (start us, length us, event | category | flops | bytes accessed | tf_op | source)
XLA Modules:
  0.0 125.3 jit_solution(7382376993454447379)
XLA Ops:
  0.6 0.0 copy-start
  0.6 1.0 copy-done
  1.7 0.0 copy-start.6
  1.7 0.7 copy-done.6
  2.4 1.2 border_rows.1.halo
  3.6 0.0 copy-start.1
  3.6 1.0 copy-done.1
  4.6 0.0 copy-start.4
  4.6 0.9 copy-done.4
  5.5 0.8 copy-done.5
  6.3 1.7 %prepare.1 = (bf16[64,3200]{1,0:T(8,128)(2,1)S(1)}, bf16[64,3200]{1,0:T(8,128)(2,1)}, bf16[64,3200]{1,0:T(8,128)(2,1)}, bf16[64,3200]{1,0:T(8,128)(2,1)}) custom-call(s32[1]{0:T(128)} %bitcast.place, bf16[64,4096]{1,0:T(8,128)(2,1)S(1)} %copy-done, bf16[64,4096]{1,0:T(8,128)(2,1)S(1)} %copy-done.1, bf16[3,64,256]{2,1,0:T(8,128)(2,1)S(1)} %copy-done.4, ...), custom_call_target="tpu_custom_call" | custom-call | tf_op jit(solution)/shard_map/prepare/pallas_call | solution.py:352
  8.0 2.1 %collective-permute-start = (bf16[64,3200]{1,0:T(8,128)(2,1)}, bf16[64,3200]{1,0:T(8,128)(2,1)}, u32[]{:S(2)}, u32[]{:S(2)}) collective-permute-start(bf16[64,3200]{1,0:T(8,128)(2,1)} %get-tuple-element.25), channel_id=1, source_target_pairs={{0,1},{1,2},{2,3},{3,0},{4,5},{5,6},{6,7},{7,4},{8,9},{9,10},{10,1... | collective-permute-start | bytes 1228808 | tf_op jit(solution)/shard_map/exchange/ppermute | solution.py:27
  10.1 2.5 %collective-permute-start.1 = (bf16[64,3200]{1,0:T(8,128)(2,1)}, bf16[64,3200]{1,0:T(8,128)(2,1)}, u32[]{:S(2)}, u32[]{:S(2)}) collective-permute-start(bf16[64,3200]{1,0:T(8,128)(2,1)} %get-tuple-element.26), channel_id=1, source_target_pairs={{0,2},{1,3},{2,0},{3,1},{4,6},{5,7},{6,4},{7,5},{8,10},{9,11},{10,... | collective-permute-start | bytes 1228808 | tf_op jit(solution)/shard_map/exchange/ppermute | solution.py:27
  12.5 1.2 collective-permute-start.2
  13.7 3.1 %collective-permute-start.3 = (bf16[64,128]{1,0:T(8,128)(2,1)S(1)}, bf16[64,128]{1,0:T(8,128)(2,1)S(1)}, u32[]{:S(2)}, u32[]{:S(2)}) collective-permute-start(bf16[64,128]{1,0:T(8,128)(2,1)S(1)} %get-tuple-element.45), channel_id=1, source_target_pairs={{0,4},{4,8},{8,12},{12,16},{16,20},{20,24},{24,28},{28,32},{32,36}... | collective-permute-start | bytes 49160 | tf_op jit(solution)/shard_map/border_rows/ppermute | solution.py:27
  16.8 2.9 %collective-permute-start.5 = (bf16[64,128]{1,0:T(8,128)(2,1)S(1)}, bf16[64,128]{1,0:T(8,128)(2,1)S(1)}, u32[]{:S(2)}, u32[]{:S(2)}) collective-permute-start(bf16[64,128]{1,0:T(8,128)(2,1)S(1)} %get-tuple-element.46), channel_id=1, source_target_pairs={{0,128},{4,132},{8,136},{12,140},{16,144},{20,148},{24,152},{28,15... | collective-permute-start | bytes 49160 | tf_op jit(solution)/shard_map/border_rows/ppermute | solution.py:27
  19.7 0.0 collective-permute-done.3
  19.7 3.9 %collective-permute-start.4 = (bf16[64,128]{1,0:T(8,128)(2,1)S(1)}, bf16[64,128]{1,0:T(8,128)(2,1)S(1)}, u32[]{:S(2)}, u32[]{:S(2)}) collective-permute-start(bf16[64,128]{1,0:T(8,128)(2,1)S(1)} %get-tuple-element.47), channel_id=1, source_target_pairs={{0,252},{4,0},{8,4},{12,8},{16,12},{20,16},{24,20},{28,24},{32,28}... | collective-permute-start | bytes 49160 | tf_op jit(solution)/shard_map/border_rows/ppermute | solution.py:27
  23.6 0.0 collective-permute-done.5
  23.6 0.8 collective-permute-done.4
  24.5 0.7 broadcast_in_dim.6
  25.2 3.5 %all-to-all-start = ((bf16[4,64,384]{2,1,0:T(8,128)(2,1)}), bf16[4,64,384]{2,1,0:T(8,128)(2,1)S(1)}, u32[]{:S(2)}, u32[]{:S(2)}) async-start(bf16[4,64,384]{2,1,0:T(8,128)(2,1)} %broadcast_in_dim.6), calls=%async_computation | async-start | bytes 393216 | tf_op jit(solution)/shard_map/border_rows/all_to_all | solution.py:445
  28.7 0.0 copy-start.3
  28.7 0.9 copy-done.3
  29.7 2.8 %masks.1.bias = f32[8,640,128]{2,1,0:T(8,128)S(1)} custom-call(s32[1]{0:T(128)} %bitcast.place, s32[9,4096]{1,0:T(8,128)S(1)} %copy-done.3), custom_call_target="tpu_custom_call" | custom-call | tf_op jit(solution)/shard_map/attention/masks/pallas_call | solution.py:352
  32.5 1.2 all-to-all-done.far
  33.7 0.0 collective-permute-done.c1
  33.7 0.0 collective-permute-done.1.c2
  33.7 0.0 collective-permute-done.2.c3
  33.7 28.1 %attention.1 = (bf16[64,1536]{1,0:T(8,128)(2,1)S(1)}, bf16[64,1536]{1,0:T(8,128)(2,1)S(1)}, bf16[64,1536]{1,0:T(8,128)(2,1)S(1)}, bf16[64,1536]{1,0:T(8,128)(2,1)S(1)}, bf16[8,4,32,256]{3,2,1,0:T(8,128)(2,1)}) custom-call(s32[1]{0:T(128)} %bitcast.place, bf16[64,3200]{1,0:T(8,128)(2,1)S(1)} %get-tuple-element.24.c0, ...), custom_call_target="tpu_custom_call" | custom-call | tf_op jit(solution)/shard_map/attention/pallas_call | solution.py:352
  61.8 0.0 copy-start.8
  61.8 0.7 copy-done.8
  62.4 0.0 copy-start.9
  62.4 0.7 copy-done.9
  63.1 0.0 copy-start.10
  63.1 0.7 copy-done.10
  63.8 0.0 copy-start.2
  63.8 6.1 %all-to-all-start.1 = ((bf16[8,4,32,256]{3,2,1,0:T(8,128)(2,1)}), bf16[8,4,32,256]{3,2,1,0:T(8,128)(2,1)S(1)}, u32[]{:S(2)}, u32[]{:S(2)}) async-start(bf16[8,4,32,256]{3,2,1,0:T(8,128)(2,1)} %get-tuple-element.32), calls=%async_computation.1 | async-start | bytes 1048576 | tf_op jit(solution)/shard_map/weight_sums/all_to_all | solution.py:455
  69.8 0.7 collective-permute-start.6
  70.5 1.4 %collective-permute-start.7 = (bf16[64,1536]{1,0:T(8,128)(2,1)}, bf16[64,1536]{1,0:T(8,128)(2,1)S(1)}, u32[]{:S(2)}, u32[]{:S(2)}) collective-permute-start(bf16[64,1536]{1,0:T(8,128)(2,1)} %copy-done.9), channel_id=1, source_target_pairs={{0,2},{1,3},{2,0},{3,1},{4,6},{5,7},{6,4},{7,5},{8,10},{9,11},{10,... | collective-permute-start | bytes 589832 | tf_op jit(solution)/shard_map/return/ppermute | solution.py:27
  72.0 1.0 collective-permute-start.8
  72.9 6.4 %all-to-all-done.1 = bf16[8,4,32,256]{3,2,1,0:T(8,128)(2,1)S(1)} async-done(((bf16[8,4,32,256]{3,2,1,0:T(8,128)(2,1)}), bf16[8,4,32,256]{3,2,1,0:T(8,128)(2,1)S(1)}, u32[]{:S(2)}, u32[]{:S(2)}) %all-to-all-start.1) | async-done | bytes 524320 | tf_op jit(solution)/shard_map/weight_sums/all_to_all | solution.py:455
  79.3 0.1 reduce_sum.21
  79.4 0.0 collective-permute-done.6.r1
  79.4 1.9 %collective-permute-done.7.r2 = bf16[64,1536]{1,0:T(8,128)(2,1)S(1)} collective-permute-done((bf16[64,1536]{1,0:T(8,128)(2,1)}, bf16[64,1536]{1,0:T(8,128)(2,1)S(1)}, u32[]{:S(2)}, u32[]{:S(2)}) %collective-permute-start.7) | collective-permute-done | bytes 196640 | tf_op jit(solution)/shard_map/return/ppermute | solution.py:27
  81.3 0.8 collective-permute-done.8.r3
  82.1 0.9 broadcast_in_dim.7
  83.0 10.4 %all-to-all-start.2 = ((bf16[32,32,256]{2,1,0:T(8,128)(2,1)}), bf16[32,32,256]{2,1,0:T(8,128)(2,1)S(1)}, u32[]{:S(2)}, u32[]{:S(2)}) async-start(bf16[32,32,256]{2,1,0:T(8,128)(2,1)} %bitcast.2), calls=%async_computation.2 | async-start | bytes 1048576 | tf_op jit(solution)/shard_map/weight_sums/all_to_all | solution.py:466
  93.4 0.8 collective-permute-start.9
  94.2 1.5 %collective-permute-start.10 = (bf16[64,128]{1,0:T(8,128)(2,1)S(1)}, bf16[64,128]{1,0:T(8,128)(2,1)S(1)}, u32[]{:S(2)}, u32[]{:S(2)}) collective-permute-start(bf16[64,128]{1,0:T(8,128)(2,1)S(1)} %get-tuple-element.38), channel_id=1, source_target_pairs={{0,4},{4,8},{8,12},{12,16},{16,20},{20,24},{24,28},{28,32},{32,36}... | collective-permute-start | bytes 49160 | tf_op jit(solution)/shard_map/return/ppermute | solution.py:27
  95.7 2.9 %collective-permute-start.11 = (bf16[64,128]{1,0:T(8,128)(2,1)S(1)}, bf16[64,128]{1,0:T(8,128)(2,1)S(1)}, u32[]{:S(2)}, u32[]{:S(2)}) collective-permute-start(bf16[64,128]{1,0:T(8,128)(2,1)S(1)} %get-tuple-element.39), channel_id=1, source_target_pairs={{0,128},{4,132},{8,136},{12,140},{16,144},{20,148},{24,152},{28,15... | collective-permute-start | bytes 49160 | tf_op jit(solution)/shard_map/return/ppermute | solution.py:27
  98.6 11.5 %all-to-all-done.2 = bf16[32,32,256]{2,1,0:T(8,128)(2,1)S(1)} async-done(((bf16[32,32,256]{2,1,0:T(8,128)(2,1)}), bf16[32,32,256]{2,1,0:T(8,128)(2,1)S(1)}, u32[]{:S(2)}, u32[]{:S(2)}) %all-to-all-start.2) | async-done | bytes 524320 | tf_op jit(solution)/shard_map/weight_sums/all_to_all | solution.py:466
  110.1 0.1 convert_reduce_fusion
  110.1 0.0 collective-permute-done.9.b0
  110.2 0.0 collective-permute-done.10.b1
  110.2 0.0 collective-permute-done.11.b2
  110.2 0.7 broadcast_in_dim.8
  110.9 6.5 %all-to-all-start.3 = ((f32[8,32,256]{2,1,0:T(8,128)}), f32[8,32,256]{2,1,0:T(8,128)S(1)}, u32[]{:S(2)}, u32[]{:S(2)}) async-start(f32[8,32,256]{2,1,0:T(8,128)} %broadcast_in_dim.8), calls=%async_computation.3 | async-start | bytes 524288 | tf_op jit(solution)/shard_map/weight_sums/all_to_all | solution.py:470
  117.4 0.0 copy-done.2
  117.4 0.0 copy-done.7
  117.5 2.5 %return.3 = f32[64,4096]{1,0:T(8,128)} custom-call(s32[1]{0:T(128)} %bitcast.place, bf16[64,1536]{1,0:T(8,128)(2,1)S(1)} %get-tuple-element.33.r0, bf16[64,1536]{1,0:T(8,128)(2,1)S(1)} %collective-permute-done.6.r1, bf16[64,1536]{1,0:T(8,128)(2,1)S(1)} %collective-permute-done.7.r2, bf16[64,1536]{1,0:T(8,128)(2,1)S(1)} %collective-permute-done.8.r3, ...), custom_call_target="tpu_custom_call" | custom-call | tf_op jit(solution)/shard_map/return/pallas_call | solution.py:352
  119.9 4.0 %all-to-all-done.3 = f32[8,32,256]{2,1,0:T(8,128)S(1)} async-done(((f32[8,32,256]{2,1,0:T(8,128)}), f32[8,32,256]{2,1,0:T(8,128)S(1)}, u32[]{:S(2)}, u32[]{:S(2)}) %all-to-all-start.3) | async-done | bytes 262176 | tf_op jit(solution)/shard_map/weight_sums/all_to_all | solution.py:470
  123.9 0.6 slice.29
  124.6 0.7 slice.28
  (6 shorter events, 0.1 us)
Async XLA Ops:
  0.6 1.0 copy-start
  1.7 0.7 copy-start.6
  3.6 1.0 copy-start.1
  4.6 0.9 copy-start.4
  5.5 0.8 copy-start.5
  8.0 25.7 %collective-permute-start = (bf16[64,3200]{1,0:T(8,128)(2,1)}, bf16[64,3200]{1,0:T(8,128)(2,1)}, u32[]{:S(2)}, u32[]{:S(2)}) collective-permute-start(bf16[64,3200]{1,0:T(8,128)(2,1)} %get-tuple-element.25), channel_id=1, source_target_pairs={{0,1},{1,2},{2,3},{3,0},{4,5},{5,6},{6,7},{7,4},{8,9},{9,10},{10,1... | collective-permute-start | bytes 1228808 | tf_op jit(solution)/shard_map/exchange/ppermute | solution.py:27
  10.1 23.6 %collective-permute-start.1 = (bf16[64,3200]{1,0:T(8,128)(2,1)}, bf16[64,3200]{1,0:T(8,128)(2,1)}, u32[]{:S(2)}, u32[]{:S(2)}) collective-permute-start(bf16[64,3200]{1,0:T(8,128)(2,1)} %get-tuple-element.26), channel_id=1, source_target_pairs={{0,2},{1,3},{2,0},{3,1},{4,6},{5,7},{6,4},{7,5},{8,10},{9,11},{10,... | collective-permute-start | bytes 1228808 | tf_op jit(solution)/shard_map/exchange/ppermute | solution.py:27
  12.5 21.2 %collective-permute-start.2 = (bf16[64,3200]{1,0:T(8,128)(2,1)}, bf16[64,3200]{1,0:T(8,128)(2,1)}, u32[]{:S(2)}, u32[]{:S(2)}) collective-permute-start(bf16[64,3200]{1,0:T(8,128)(2,1)} %get-tuple-element.27), channel_id=1, source_target_pairs={{0,3},{1,0},{2,1},{3,2},{4,7},{5,4},{6,5},{7,6},{8,11},{9,8},{10,9... | collective-permute-start | bytes 1228808 | tf_op jit(solution)/shard_map/exchange/ppermute | solution.py:27
  13.7 6.0 %collective-permute-start.3 = (bf16[64,128]{1,0:T(8,128)(2,1)S(1)}, bf16[64,128]{1,0:T(8,128)(2,1)S(1)}, u32[]{:S(2)}, u32[]{:S(2)}) collective-permute-start(bf16[64,128]{1,0:T(8,128)(2,1)S(1)} %get-tuple-element.45), channel_id=1, source_target_pairs={{0,4},{4,8},{8,12},{12,16},{16,20},{20,24},{24,28},{28,32},{32,36}... | collective-permute-start | bytes 49160 | tf_op jit(solution)/shard_map/border_rows/ppermute | solution.py:27
  16.8 6.8 %collective-permute-start.5 = (bf16[64,128]{1,0:T(8,128)(2,1)S(1)}, bf16[64,128]{1,0:T(8,128)(2,1)S(1)}, u32[]{:S(2)}, u32[]{:S(2)}) collective-permute-start(bf16[64,128]{1,0:T(8,128)(2,1)S(1)} %get-tuple-element.46), channel_id=1, source_target_pairs={{0,128},{4,132},{8,136},{12,140},{16,144},{20,148},{24,152},{28,15... | collective-permute-start | bytes 49160 | tf_op jit(solution)/shard_map/border_rows/ppermute | solution.py:27
  19.7 4.7 %collective-permute-start.4 = (bf16[64,128]{1,0:T(8,128)(2,1)S(1)}, bf16[64,128]{1,0:T(8,128)(2,1)S(1)}, u32[]{:S(2)}, u32[]{:S(2)}) collective-permute-start(bf16[64,128]{1,0:T(8,128)(2,1)S(1)} %get-tuple-element.47), channel_id=1, source_target_pairs={{0,252},{4,0},{8,4},{12,8},{16,12},{20,16},{24,20},{28,24},{32,28}... | collective-permute-start | bytes 49160 | tf_op jit(solution)/shard_map/border_rows/ppermute | solution.py:27
  25.2 8.5 %all-to-all-start = ((bf16[4,64,384]{2,1,0:T(8,128)(2,1)}), bf16[4,64,384]{2,1,0:T(8,128)(2,1)S(1)}, u32[]{:S(2)}, u32[]{:S(2)}) async-start(bf16[4,64,384]{2,1,0:T(8,128)(2,1)} %broadcast_in_dim.6), calls=%async_computation | async-start | bytes 393216 | tf_op jit(solution)/shard_map/border_rows/all_to_all | solution.py:445
  28.7 1.0 copy-start.3
  61.8 0.7 copy-start.8
  62.4 0.7 copy-start.9
  63.1 0.7 copy-start.10
  63.8 53.7 %copy-start.2 = (bf16[64,4096]{1,0:T(8,128)(2,1)S(1)}, bf16[64,4096]{1,0:T(8,128)(2,1)}, u32[]{:S(2)}) copy-start(bf16[64,4096]{1,0:T(8,128)(2,1)} %grad_in.3) | copy-start | bytes 1572868
  63.8 53.7 %copy-start.7 = (s32[1,3,128]{2,0,1:T(1,128)S(1)}, s32[1,3,128]{2,0,1:T(1,128)}, u32[]{:S(2)}) copy-start(s32[1,3,128]{2,0,1:T(1,128)} %param.11) | copy-start | bytes 4612
  63.8 15.6 %all-to-all-start.1 = ((bf16[8,4,32,256]{3,2,1,0:T(8,128)(2,1)}), bf16[8,4,32,256]{3,2,1,0:T(8,128)(2,1)S(1)}, u32[]{:S(2)}, u32[]{:S(2)}) async-start(bf16[8,4,32,256]{3,2,1,0:T(8,128)(2,1)} %get-tuple-element.32), calls=%async_computation.1 | async-start | bytes 1048576 | tf_op jit(solution)/shard_map/weight_sums/all_to_all | solution.py:455
  69.8 9.6 %collective-permute-start.6 = (bf16[64,1536]{1,0:T(8,128)(2,1)}, bf16[64,1536]{1,0:T(8,128)(2,1)S(1)}, u32[]{:S(2)}, u32[]{:S(2)}) collective-permute-start(bf16[64,1536]{1,0:T(8,128)(2,1)} %copy-done.10), channel_id=1, source_target_pairs={{0,1},{1,2},{2,3},{3,0},{4,5},{5,6},{6,7},{7,4},{8,9},{9,10},{10,1... | collective-permute-start | bytes 589832 | tf_op jit(solution)/shard_map/return/ppermute | solution.py:27
  70.5 10.8 %collective-permute-start.7 = (bf16[64,1536]{1,0:T(8,128)(2,1)}, bf16[64,1536]{1,0:T(8,128)(2,1)S(1)}, u32[]{:S(2)}, u32[]{:S(2)}) collective-permute-start(bf16[64,1536]{1,0:T(8,128)(2,1)} %copy-done.9), channel_id=1, source_target_pairs={{0,2},{1,3},{2,0},{3,1},{4,6},{5,7},{6,4},{7,5},{8,10},{9,11},{10,... | collective-permute-start | bytes 589832 | tf_op jit(solution)/shard_map/return/ppermute | solution.py:27
  72.0 10.1 %collective-permute-start.8 = (bf16[64,1536]{1,0:T(8,128)(2,1)}, bf16[64,1536]{1,0:T(8,128)(2,1)S(1)}, u32[]{:S(2)}, u32[]{:S(2)}) collective-permute-start(bf16[64,1536]{1,0:T(8,128)(2,1)} %copy-done.8), channel_id=1, source_target_pairs={{0,3},{1,0},{2,1},{3,2},{4,7},{5,4},{6,5},{7,6},{8,11},{9,8},{10,9... | collective-permute-start | bytes 589832 | tf_op jit(solution)/shard_map/return/ppermute | solution.py:27
  83.0 27.1 %all-to-all-start.2 = ((bf16[32,32,256]{2,1,0:T(8,128)(2,1)}), bf16[32,32,256]{2,1,0:T(8,128)(2,1)S(1)}, u32[]{:S(2)}, u32[]{:S(2)}) async-start(bf16[32,32,256]{2,1,0:T(8,128)(2,1)} %bitcast.2), calls=%async_computation.2 | async-start | bytes 1048576 | tf_op jit(solution)/shard_map/weight_sums/all_to_all | solution.py:466
  93.4 16.8 %collective-permute-start.9 = (bf16[64,128]{1,0:T(8,128)(2,1)S(1)}, bf16[64,128]{1,0:T(8,128)(2,1)S(1)}, u32[]{:S(2)}, u32[]{:S(2)}) collective-permute-start(bf16[64,128]{1,0:T(8,128)(2,1)S(1)} %get-tuple-element.37), channel_id=1, source_target_pairs={{0,252},{4,0},{8,4},{12,8},{16,12},{20,16},{24,20},{28,24},{32,28}... | collective-permute-start | bytes 49160 | tf_op jit(solution)/shard_map/return/ppermute | solution.py:27
  94.2 15.9 %collective-permute-start.10 = (bf16[64,128]{1,0:T(8,128)(2,1)S(1)}, bf16[64,128]{1,0:T(8,128)(2,1)S(1)}, u32[]{:S(2)}, u32[]{:S(2)}) collective-permute-start(bf16[64,128]{1,0:T(8,128)(2,1)S(1)} %get-tuple-element.38), channel_id=1, source_target_pairs={{0,4},{4,8},{8,12},{12,16},{16,20},{20,24},{24,28},{28,32},{32,36}... | collective-permute-start | bytes 49160 | tf_op jit(solution)/shard_map/return/ppermute | solution.py:27
  95.7 14.5 %collective-permute-start.11 = (bf16[64,128]{1,0:T(8,128)(2,1)S(1)}, bf16[64,128]{1,0:T(8,128)(2,1)S(1)}, u32[]{:S(2)}, u32[]{:S(2)}) collective-permute-start(bf16[64,128]{1,0:T(8,128)(2,1)S(1)} %get-tuple-element.39), channel_id=1, source_target_pairs={{0,128},{4,132},{8,136},{12,140},{16,144},{20,148},{24,152},{28,15... | collective-permute-start | bytes 49160 | tf_op jit(solution)/shard_map/return/ppermute | solution.py:27
  110.9 13.0 %all-to-all-start.3 = ((f32[8,32,256]{2,1,0:T(8,128)}), f32[8,32,256]{2,1,0:T(8,128)S(1)}, u32[]{:S(2)}, u32[]{:S(2)}) async-start(f32[8,32,256]{2,1,0:T(8,128)} %broadcast_in_dim.8), calls=%async_computation.3 | async-start | bytes 524288 | tf_op jit(solution)/shard_map/weight_sums/all_to_all | solution.py:470

commit v4 on v3

--- a/solution.py
+++ b/solution.py
@@ -13,7 +13,7 @@
 HEAD_DIM = 32
 BLOCK = 128
 SIDE = 64
-CHUNK = 128
+CHUNK = 64
 PARTS = 32
 WINDOW = BLOCK + 2 * SIDE
 LOG2E = math.log2(math.e)
@@ -27,16 +27,15 @@
     return lax.ppermute(value, axis, pairs)
 
 
-def rank(y, z, core):
-    return 16 * y + 2 * z + core
-
-
-PLATES = [[rank(y, z, core) for y in range(4) for core in range(2)] for z in range(8)]
-SHEETS = [
-    [rank(y, z, core) * 4 + head for z in range(8) for head in range(4)]
-    for y in range(4)
-    for core in range(2)
-]
+def grouped(value, groups):
+    return lax.all_to_all(value, "tile", 0, 0, axis_index_groups=groups)
+
+
+def plates(heads):
+    return [
+        [(16 * y + 2 * z + c) * heads + h for h in range(heads) for y in range(4) for c in range(2)]
+        for z in range(8)
+    ]
 
 
 def vmem_spec():
@@ -123,32 +122,9 @@
         fetch.wait()
 
 
-def masks(place, neighbors, bias):
-    head = place[0]
-    rows_all = neighbors.shape[1]
-    blocks, cand, _ = bias.shape
-
-    def step(b, carry):
-        first = head * (rows_all // 4) + b * BLOCK
-        near = neighbors[:, pl.ds(pl.multiple_of(first, BLOCK), BLOCK)]
-        shifted = (near - (first - SIDE)) & (rows_all - 1)
-        index = jnp.where(near < rows_all, shifted, near - rows_all + WINDOW)
-        for start in range(0, cand, CHUNK):
-            rows = lax.broadcasted_iota(jnp.int32, (CHUNK, BLOCK), 0) + start
-            count = jnp.zeros((CHUNK, BLOCK), F32)
-            for slot in range(NBR):
-                count = count + jnp.where(rows == index[slot : slot + 1, :], 1.0, 0.0)
-            bias[b, start : start + CHUNK, :] = jnp.where(
-                count > 0.5, jnp.log(count) * LOG2E, -1e30
-            )
-        return carry
-
-    lax.fori_loop(0, blocks, step, 0)
-
-
 def attend(
-    place, c0, c1, c2, c3, far, bias, o0, o1, o2, o3, sums,
-    xe, dy, wq, wkv, wo, qs, ds, kvt, kv, dkv, da, dkvt, grads, summed,
+    place, c0, c1, c2, c3, far, neighbors, o0, o1, o2, o3, sums,
+    bias, xe, dy, wq, wkv, wo, qs, ds, kvt, kv, dkv, da, dkvt, grads, summed,
     products0, products1, weights0, weights1, means0, means1, qt, dt,
 ):
     head = place[0]
@@ -216,7 +192,7 @@
         acc = jnp.zeros((PARTS, BLOCK), F32)
         for start in range(0, cand, CHUNK):
             rows = slice(start, start + CHUNK)
-            expon = jnp.exp2(products[rows, left] * (scale * LOG2E) + bias[block, rows, :])
+            expon = jnp.exp2(products[rows, left] * (scale * LOG2E) + bias[rows, :])
             products[rows, left] = expon
             acc = acc + expon.reshape(CHUNK // PARTS, PARTS, BLOCK).sum(0)
         return 1.0 / jnp.sum(acc, axis=0, keepdims=True)
@@ -253,8 +229,9 @@
         second = dout - (query.astype(F32) * means[hh : hh + 1, :]).astype(BF16)
         both = jnp.concatenate([query, second], axis=1)
         cols = slice(C * hh, C * hh + C)
-        dkv[top : top + 64, pl.ds(first, WINDOW)] += nt(both, weights[:WINDOW, cols])
-        dkv[top : top + 64, ext:] += nt(both, weights[WINDOW:, cols])
+        out = nt(both, weights[:, cols])
+        dkv[top : top + 64, pl.ds(first, WINDOW)] += out[:, :WINDOW]
+        dkv[top : top + 64, ext:] += out[:, WINDOW:]
 
     def phase(block, ahead, group, behind, products, weights, means, products_next, weights_done, means_done):
         inv0 = first_pass(block, 0, products)
@@ -277,6 +254,15 @@
         spread(*behind, 3, weights_done, means_done)
 
     def step(b, carry):
+        near = neighbors[:, pl.ds(pl.multiple_of(head * own + b * BLOCK, BLOCK), BLOCK)]
+        shifted = (near - (head * own + b * BLOCK - SIDE)) & (neighbors.shape[1] - 1)
+        index = jnp.where(near < neighbors.shape[1], shifted, near - neighbors.shape[1] + WINDOW)
+        for start in range(0, cand, CHUNK):
+            rows = lax.broadcasted_iota(jnp.int32, (CHUNK, BLOCK), 0) + start
+            count = jnp.zeros((CHUNK, BLOCK), F32)
+            for slot in range(NBR):
+                count = count + jnp.where(rows == index[slot : slot + 1, :], 1.0, 0.0)
+            bias[start : start + CHUNK, :] = jnp.where(count > 0.5, jnp.log(count) * LOG2E, -1e30)
         before = jnp.maximum(b - 1, 0)
         after = jnp.minimum(b + 1, last)
         phase(b, (b, 1), 0, (before, 1), products0, weights0, means0, products1, weights1, means1)
@@ -309,7 +295,9 @@
         for k in range(2):
             top = 128 * target + 64 * k
             for kind, (which, low) in enumerate(((0, 0), (1, 0), (1, 32), (2, 32))):
-                sums[2 * kind + k, target] = grads[which, top + low : top + low + 32, :]
+                sums[target, 64 * kind + 32 * k : 64 * kind + 32 * k + 32, :] = grads[
+                    which, top + low : top + low + 32, :
+                ]
 
 
 def add_up(r0, r1, r2, r3, b0, b1, b2):
@@ -339,7 +327,7 @@
         out[:, cols] = grad_in[:, cols].astype(F32) + aligned[:, cols] + returned
 
 
-def kernel_call(body, out_shape, inputs, scratch=(), mib=12, loose=()):
+def kernel_call(body, out_shape, inputs, scratch=(), mib=48, loose=()):
     specs = []
     for place, value in enumerate(inputs):
         if value.dtype == jnp.int32 and value.size == 1:
@@ -364,14 +352,13 @@
 
 
 def attend_call(place, *args):
-    *inputs, neighbors, own, ext, full, cand = args
-    with jax.named_scope("masks"):
-        bias = kernel_call(masks, sds((own // BLOCK, cand, BLOCK), F32), (place, neighbors))
+    *inputs, own, ext, full, cand = args
     return kernel_call(
         attend,
-        [sds((64, full), BF16)] * 4 + [sds((8, 4, C // 8, C), BF16)],
-        (place, *inputs, bias),
+        [sds((64, full), BF16)] * 4 + [sds((4, C, C), BF16)],
+        (place, *inputs),
         [
+            pltpu.VMEM((cand, BLOCK), F32),
             pltpu.VMEM((C, full), BF16),
             pltpu.VMEM((C, own), BF16),
             pltpu.VMEM((2 * C, C), BF16),
@@ -395,7 +382,6 @@
             pltpu.VMEM((2 * C, own), BF16),
             pltpu.VMEM((2 * C, own), BF16),
         ],
-        mib=36,
     )
 
 
@@ -452,7 +438,9 @@
     with jax.named_scope("return"):
         parts = [parts[0]] + [passed_along(parts[step], "head", step) for step in (1, 2, 3)]
     with jax.named_scope("weight_sums"):
-        value = lax.all_to_all(sums, "tile", 0, 0, axis_index_groups=PLATES)
+        value = lax.all_to_all(
+            sums.reshape(32, C // 8, C), ("tile", "head"), 0, 0, axis_index_groups=plates(4)
+        )
         value = value.astype(F32).sum(0).astype(BF16)
         *parts, value = lax.optimization_barrier((*parts, value))
     with jax.named_scope("return"):
@@ -462,12 +450,13 @@
             for peer in range(3)
         ]
     with jax.named_scope("weight_sums"):
-        value = jnp.broadcast_to(value[None], (8, 4, C // 8, C)).reshape(32, C // 8, C)
-        value = lax.all_to_all(value, ("tile", "head"), 0, 0, axis_index_groups=SHEETS)
-        value = value.astype(F32).sum(0) * (1.0 / math.sqrt(rows * groups))
+        line = [[16 * y + 2 * z + c for z in range(8)] for y in range(4) for c in range(2)]
+        piece = (8, C // 8, C)
+        value = grouped(jnp.broadcast_to(value[None], piece), line)
+        grad_scale = 1.0 / math.sqrt(rows * groups)
+        value = value.astype(F32).sum(0) * grad_scale
         *back, value = lax.optimization_barrier((*back, value))
-        value = jnp.broadcast_to(value[None], (8, C // 8, C))
-        value = lax.all_to_all(value, "tile", 0, 0, axis_index_groups=PLATES)
+        value = grouped(jnp.broadcast_to(value[None], piece), plates(1))
         value = value.reshape(4, 64, C)
     with jax.named_scope("return"):
         d_tokens = kernel_call(

time: 126 us -> 117 us (0.929)
  blocking collectives: 0 us -> 7.68 us
  waiting for transfers between devices: 26.6 us -> 19.7 us
  local copies, waits for them, and re-layouts: 11 us -> 5.35 us
  Pallas kernels: 36.3 us -> 32.8 us
    all_to_all x4 -> x3, waiting for transfers between devices: 23.1 us -> 12.9 us  [the longest x1 6.7 us: local(): lax.all_to_all(sums.reshape(32, C // 8, C), ('tile', 'head'), 0, 0, axis_...]
    all_to_all x0 -> x1, blocking collectives: none -> 7.68 us  [local(): lax.all_to_all(jnp.broadcast_to(mine[None], (4, 64, 3 * border)), 'head',...]
    unnamed x22 -> x12, local copies, waits for them, and re-layouts: 7.38 us -> 2.61 us
    pallas_call x6 -> x5, Pallas kernels: 36.3 us -> 32.8 us  [kernel_call(): pl.pallas_call(body, out_shape=out_shape, in_specs=specs, out_specs=outs,...]
    ppermute x12, waiting for transfers between devices: 3.53 us -> 6.83 us  [passed_along(): return lax.ppermute(value, axis, pairs)]
    all_to_all x4 -> x3, starting transfers between devices: 26.5 us -> 23.5 us  [the longest x2 15.4 us: grouped(): return lax.all_to_all(value, 'tile', 0, 0, axis_index_groups=groups)]
    ppermute x12, starting transfers between devices: 23.9 us -> 26.3 us  [passed_along(): return lax.ppermute(value, axis, pairs)]
  transfers between devices with their start and end apart: 16 -> 15, of which waited for: 7 -> 6; matrix products, arithmetic and copies ran while one was open for 1% -> 0% of each run, Pallas kernels for 4% -> 2%
where the time goes in v4:
time: 117 us; the launch traced here: 116 us
  starting transfers between devices  49.9 us (43%)
  Pallas kernels  32.8 us (28%)
  waiting for transfers between devices  19.7 us (17%)
  blocking collectives  7.68 us (7%)
  local copies, waits for them, and re-layouts  5.35 us (5%)
    pallas_call x5, Pallas kernels, kernel_call(): pl.pallas_call(body, out_shape=out_shape, in_specs=specs, out_specs=outs,...  32.8 us
    ppermute x12, starting transfers between devices, passed_along(): return lax.ppermute(value, axis, pairs)  26.3 us
    all_to_all x2, starting transfers between devices, grouped(): return lax.all_to_all(value, 'tile', 0, 0, axis_index_groups=groups)  15.4 us
    all_to_all x1, starting transfers between devices, local(): lax.all_to_all(sums.reshape(32, C // 8, C), ('tile', 'head'), 0, 0, axis_...  8.19 us
    all_to_all x1, blocking collectives, local(): lax.all_to_all(jnp.broadcast_to(mine[None], (4, 64, 3 * border)), 'head',...  7.68 us
    ppermute x12, waiting for transfers between devices, passed_along(): return lax.ppermute(value, axis, pairs)  6.83 us
    all_to_all x1, waiting for transfers between devices, local(): lax.all_to_all(sums.reshape(32, C // 8, C), ('tile', 'head'), 0, 0, axis_...  6.7 us
    all_to_all x2, waiting for transfers between devices, grouped(): return lax.all_to_all(value, 'tile', 0, 0, axis_index_groups=groups)  6.22 us
  transfers between devices with their start and end apart: 15, of which 6 were waited for; matrix products, arithmetic and copies ran while one was open for 0% of the time, Pallas kernels for 2%

profile of v4, /device:TPU:1, one launch (start us, length us, event | category | flops | bytes accessed | tf_op | source)
XLA Modules:
  0.0 116.3 jit_solution(5172756620983278791)
XLA Ops:
  0.6 0.0 copy-start.5
  0.6 0.7 copy-done.5
  1.3 0.0 copy-start
  1.3 1.0 copy-done
  2.4 0.0 copy-start.1
  2.4 0.0 copy-start.4
  2.4 1.2 %border_rows.1.halo = bf16[64,384]{1,0:T(8,128)(2,1)S(1)} custom-call(bf16[64,4096]{1,0:T(8,128)(2,1)S(1)} %copy-done, s32[1,384]{1,0:T(1,128)S(1)} %bitcast.5), custom_call_target="tpu_custom_call" | custom-call | tf_op jit(solution)/shard_map/border_rows/pallas_call | solution.py:340
  3.6 0.0 copy-done.1
  3.6 0.0 copy-done.4
  3.6 0.0 copy-start.3
  3.6 0.9 copy-done.3
  4.5 0.7 prepare.1
  5.1 2.1 %collective-permute-start = (bf16[64,3200]{1,0:T(8,128)(2,1)S(1)}, bf16[64,3200]{1,0:T(8,128)(2,1)S(1)}, u32[]{:S(2)}, u32[]{:S(2)}) collective-permute-start(bf16[64,3200]{1,0:T(8,128)(2,1)S(1)} %get-tuple-element.25), channel_id=1, source_target_pairs={{0,1},{1,2},{2,3},{3,0},{4,5},{5,6},{6,7},{7,4},{8,9},{9,10},{10,1... | collective-permute-start | bytes 1228808 | tf_op jit(solution)/shard_map/exchange/ppermute | solution.py:27
  7.3 2.5 %collective-permute-start.1 = (bf16[64,3200]{1,0:T(8,128)(2,1)S(1)}, bf16[64,3200]{1,0:T(8,128)(2,1)S(1)}, u32[]{:S(2)}, u32[]{:S(2)}) collective-permute-start(bf16[64,3200]{1,0:T(8,128)(2,1)S(1)} %get-tuple-element.26), channel_id=1, source_target_pairs={{0,2},{1,3},{2,0},{3,1},{4,6},{5,7},{6,4},{7,5},{8,10},{9,11},{10,... | collective-permute-start | bytes 1228808 | tf_op jit(solution)/shard_map/exchange/ppermute | solution.py:27
  9.7 1.1 collective-permute-start.2
  10.9 3.1 %collective-permute-start.3 = (bf16[64,128]{1,0:T(8,128)(2,1)S(1)}, bf16[64,128]{1,0:T(8,128)(2,1)S(1)}, u32[]{:S(2)}, u32[]{:S(2)}) collective-permute-start(bf16[64,128]{1,0:T(8,128)(2,1)S(1)} %get-tuple-element.45), channel_id=1, source_target_pairs={{0,4},{4,8},{8,12},{12,16},{16,20},{20,24},{24,28},{28,32},{32,36}... | collective-permute-start | bytes 49160 | tf_op jit(solution)/shard_map/border_rows/ppermute | solution.py:27
  14.0 2.9 %collective-permute-start.5 = (bf16[64,128]{1,0:T(8,128)(2,1)S(1)}, bf16[64,128]{1,0:T(8,128)(2,1)S(1)}, u32[]{:S(2)}, u32[]{:S(2)}) collective-permute-start(bf16[64,128]{1,0:T(8,128)(2,1)S(1)} %get-tuple-element.46), channel_id=1, source_target_pairs={{0,128},{4,132},{8,136},{12,140},{16,144},{20,148},{24,152},{28,15... | collective-permute-start | bytes 49160 | tf_op jit(solution)/shard_map/border_rows/ppermute | solution.py:27
  16.9 0.0 collective-permute-done.3
  16.9 3.9 %collective-permute-start.4 = (bf16[64,128]{1,0:T(8,128)(2,1)S(1)}, bf16[64,128]{1,0:T(8,128)(2,1)S(1)}, u32[]{:S(2)}, u32[]{:S(2)}) collective-permute-start(bf16[64,128]{1,0:T(8,128)(2,1)S(1)} %get-tuple-element.47), channel_id=1, source_target_pairs={{0,252},{4,0},{8,4},{12,8},{16,12},{20,16},{24,20},{28,24},{32,28}... | collective-permute-start | bytes 49160 | tf_op jit(solution)/shard_map/border_rows/ppermute | solution.py:27
  20.8 0.0 collective-permute-done.5
  20.8 0.8 collective-permute-done.4
  21.6 0.0 copy-start.2
  21.7 7.7 %all_to_all.20.far = bf16[4,64,384]{2,1,0:T(8,128)(2,1)S(1)} all-to-all(bf16[4,64,384]{2,1,0:T(8,128)(2,1)S(1)} %broadcast_in_dim.6), channel_id=1, replica_groups=mesh['tile'=64,'head'=4] {'head'}, dimensions={0} | all-to-all | bytes 393216 | tf_op jit(solution)/shard_map/border_rows/all_to_all | solution.py:431
  29.4 0.0 collective-permute-done.c1
  29.4 0.0 collective-permute-done.1.c2
  29.4 0.0 collective-permute-done.2.c3
  29.4 0.0 copy-done.2
  29.4 28.4 %attention.1 = (bf16[64,1536]{1,0:T(8,128)(2,1)S(1)}, bf16[64,1536]{1,0:T(8,128)(2,1)S(1)}, bf16[64,1536]{1,0:T(8,128)(2,1)S(1)}, bf16[64,1536]{1,0:T(8,128)(2,1)S(1)}, bf16[4,256,256]{2,1,0:T(8,128)(2,1)}) custom-call(s32[1]{0:T(128)} %bitcast.place, bf16[64,3200]{1,0:T(8,128)(2,1)S(1)} %get-tuple-element.24.c0, ...), custom_call_target="tpu_custom_call" | custom-call | tf_op jit(solution)/shard_map/attention/pallas_call | solution.py:340
  57.8 8.2 %all-to-all-start.1 = ((bf16[32,32,256]{2,1,0:T(8,128)(2,1)}), bf16[32,32,256]{2,1,0:T(8,128)(2,1)S(1)}, u32[]{:S(2)}, u32[]{:S(2)}) async-start(bf16[32,32,256]{2,1,0:T(8,128)(2,1)} %bitcast.2), calls=%async_computation.1 | async-start | bytes 1048576 | tf_op jit(solution)/shard_map/weight_sums/all_to_all | solution.py:441
  66.0 1.5 %collective-permute-start.6 = (bf16[64,1536]{1,0:T(8,128)(2,1)S(1)}, bf16[64,1536]{1,0:T(8,128)(2,1)S(1)}, u32[]{:S(2)}, u32[]{:S(2)}) collective-permute-start(bf16[64,1536]{1,0:T(8,128)(2,1)S(1)} %get-tuple-element.29), channel_id=1, source_target_pairs={{0,1},{1,2},{2,3},{3,0},{4,5},{5,6},{6,7},{7,4},{8,9},{9,10},{10,1... | collective-permute-start | bytes 589832 | tf_op jit(solution)/shard_map/return/ppermute | solution.py:27
  67.5 2.4 %collective-permute-start.7 = (bf16[64,1536]{1,0:T(8,128)(2,1)S(1)}, bf16[64,1536]{1,0:T(8,128)(2,1)S(1)}, u32[]{:S(2)}, u32[]{:S(2)}) collective-permute-start(bf16[64,1536]{1,0:T(8,128)(2,1)S(1)} %get-tuple-element.30), channel_id=1, source_target_pairs={{0,2},{1,3},{2,0},{3,1},{4,6},{5,7},{6,4},{7,5},{8,10},{9,11},{10,... | collective-permute-start | bytes 589832 | tf_op jit(solution)/shard_map/return/ppermute | solution.py:27
  69.9 1.1 collective-permute-start.8
  71.0 6.7 %all-to-all-done.1 = bf16[32,32,256]{2,1,0:T(8,128)(2,1)S(1)} async-done(((bf16[32,32,256]{2,1,0:T(8,128)(2,1)}), bf16[32,32,256]{2,1,0:T(8,128)(2,1)S(1)}, u32[]{:S(2)}, u32[]{:S(2)}) %all-to-all-start.1) | async-done | bytes 524320 | tf_op jit(solution)/shard_map/weight_sums/all_to_all | solution.py:441
  77.7 0.1 reduce_sum.21
  77.8 1.5 %collective-permute-done.6.r1 = bf16[64,1536]{1,0:T(8,128)(2,1)S(1)} collective-permute-done((bf16[64,1536]{1,0:T(8,128)(2,1)S(1)}, bf16[64,1536]{1,0:T(8,128)(2,1)S(1)}, u32[]{:S(2)}, u32[]{:S(2)}) %collective-permute-start.6) | collective-permute-done | bytes 196640 | tf_op jit(solution)/shard_map/return/ppermute | solution.py:27
  79.3 4.5 %collective-permute-done.7.r2 = bf16[64,1536]{1,0:T(8,128)(2,1)S(1)} collective-permute-done((bf16[64,1536]{1,0:T(8,128)(2,1)S(1)}, bf16[64,1536]{1,0:T(8,128)(2,1)S(1)}, u32[]{:S(2)}, u32[]{:S(2)}) %collective-permute-start.7) | collective-permute-done | bytes 196640 | tf_op jit(solution)/shard_map/return/ppermute | solution.py:27
  83.8 0.0 collective-permute-done.8.r3
  83.8 0.7 broadcast_in_dim.7
  84.5 8.2 %all-to-all-start.2 = ((bf16[8,32,256]{2,1,0:T(8,128)(2,1)}), bf16[8,32,256]{2,1,0:T(8,128)(2,1)S(1)}, u32[]{:S(2)}, u32[]{:S(2)}) async-start(bf16[8,32,256]{2,1,0:T(8,128)(2,1)} %broadcast_in_dim.7), calls=%async_computation.2 | async-start | bytes 262144 | tf_op jit(solution)/shard_map/weight_sums/all_to_all | solution.py:31
  92.7 1.2 %collective-permute-start.9 = (bf16[64,128]{1,0:T(8,128)(2,1)S(1)}, bf16[64,128]{1,0:T(8,128)(2,1)S(1)}, u32[]{:S(2)}, u32[]{:S(2)}) collective-permute-start(bf16[64,128]{1,0:T(8,128)(2,1)S(1)} %get-tuple-element.37), channel_id=1, source_target_pairs={{0,252},{4,0},{8,4},{12,8},{16,12},{20,16},{24,20},{28,24},{32,28}... | collective-permute-start | bytes 49160 | tf_op jit(solution)/shard_map/return/ppermute | solution.py:27
  93.9 1.7 %collective-permute-start.10 = (bf16[64,128]{1,0:T(8,128)(2,1)S(1)}, bf16[64,128]{1,0:T(8,128)(2,1)S(1)}, u32[]{:S(2)}, u32[]{:S(2)}) collective-permute-start(bf16[64,128]{1,0:T(8,128)(2,1)S(1)} %get-tuple-element.38), channel_id=1, source_target_pairs={{0,4},{4,8},{8,12},{12,16},{16,20},{20,24},{24,28},{28,32},{32,36}... | collective-permute-start | bytes 49160 | tf_op jit(solution)/shard_map/return/ppermute | solution.py:27
  95.6 2.7 %collective-permute-start.11 = (bf16[64,128]{1,0:T(8,128)(2,1)S(1)}, bf16[64,128]{1,0:T(8,128)(2,1)S(1)}, u32[]{:S(2)}, u32[]{:S(2)}) collective-permute-start(bf16[64,128]{1,0:T(8,128)(2,1)S(1)} %get-tuple-element.39), channel_id=1, source_target_pairs={{0,128},{4,132},{8,136},{12,140},{16,144},{20,148},{24,152},{28,15... | collective-permute-start | bytes 49160 | tf_op jit(solution)/shard_map/return/ppermute | solution.py:27
  98.3 2.2 %all-to-all-done.2 = bf16[8,32,256]{2,1,0:T(8,128)(2,1)S(1)} async-done(((bf16[8,32,256]{2,1,0:T(8,128)(2,1)}), bf16[8,32,256]{2,1,0:T(8,128)(2,1)S(1)}, u32[]{:S(2)}, u32[]{:S(2)}) %all-to-all-start.2) | async-done | bytes 131104 | tf_op jit(solution)/shard_map/weight_sums/all_to_all | solution.py:31
  100.5 0.0 collective-permute-done.9.b0
  100.5 0.0 collective-permute-done.10.b1
  100.6 0.0 collective-permute-done.11.b2
  100.6 0.7 broadcast_in_dim.8
  101.3 7.2 %all-to-all-start.3 = ((f32[8,32,256]{2,1,0:T(8,128)}), f32[8,32,256]{2,1,0:T(8,128)S(1)}, u32[]{:S(2)}, u32[]{:S(2)}) async-start(f32[8,32,256]{2,1,0:T(8,128)} %broadcast_in_dim.8), calls=%async_computation.3 | async-start | bytes 524288 | tf_op jit(solution)/shard_map/weight_sums/all_to_all | solution.py:31
  108.5 2.5 %return.3 = f32[64,4096]{1,0:T(8,128)} custom-call(s32[1]{0:T(128)} %bitcast.place, bf16[64,1536]{1,0:T(8,128)(2,1)S(1)} %get-tuple-element.33.r0, bf16[64,1536]{1,0:T(8,128)(2,1)S(1)} %collective-permute-done.6.r1, bf16[64,1536]{1,0:T(8,128)(2,1)S(1)} %collective-permute-done.7.r2, bf16[64,1536]{1,0:T(8,128)(2,1)S(1)} %collective-permute-done.8.r3, ...), custom_call_target="tpu_custom_call" | custom-call | tf_op jit(solution)/shard_map/return/pallas_call | solution.py:340
  111.0 4.0 %all-to-all-done.3 = f32[8,32,256]{2,1,0:T(8,128)S(1)} async-done(((f32[8,32,256]{2,1,0:T(8,128)}), f32[8,32,256]{2,1,0:T(8,128)S(1)}, u32[]{:S(2)}, u32[]{:S(2)}) %all-to-all-start.3) | async-done | bytes 262176 | tf_op jit(solution)/shard_map/weight_sums/all_to_all | solution.py:31
  115.0 0.6 slice.29
  115.6 0.7 slice.28
  (6 shorter events, 0.1 us)
Async XLA Ops:
  0.6 0.7 copy-start.5
  1.3 1.0 copy-start
  2.4 1.2 %copy-start.1 = (bf16[64,4096]{1,0:T(8,128)(2,1)S(1)}, bf16[64,4096]{1,0:T(8,128)(2,1)}, u32[]{:S(2)}) copy-start(bf16[64,4096]{1,0:T(8,128)(2,1)} %grad_in.3) | copy-start | bytes 1572868
  2.4 1.2 %copy-start.4 = (bf16[64,256]{1,0:T(8,128)(2,1)S(1)}, bf16[64,256]{1,0:T(8,128)(2,1)}, u32[]{:S(2)}) copy-start(bf16[64,256]{1,0:T(8,128)(2,1)} %w_out.1) | copy-start | bytes 98308
  3.6 0.9 copy-start.3
  5.1 24.2 %collective-permute-start = (bf16[64,3200]{1,0:T(8,128)(2,1)S(1)}, bf16[64,3200]{1,0:T(8,128)(2,1)S(1)}, u32[]{:S(2)}, u32[]{:S(2)}) collective-permute-start(bf16[64,3200]{1,0:T(8,128)(2,1)S(1)} %get-tuple-element.25), channel_id=1, source_target_pairs={{0,1},{1,2},{2,3},{3,0},{4,5},{5,6},{6,7},{7,4},{8,9},{9,10},{10,1... | collective-permute-start | bytes 1228808 | tf_op jit(solution)/shard_map/exchange/ppermute | solution.py:27
  7.3 22.1 %collective-permute-start.1 = (bf16[64,3200]{1,0:T(8,128)(2,1)S(1)}, bf16[64,3200]{1,0:T(8,128)(2,1)S(1)}, u32[]{:S(2)}, u32[]{:S(2)}) collective-permute-start(bf16[64,3200]{1,0:T(8,128)(2,1)S(1)} %get-tuple-element.26), channel_id=1, source_target_pairs={{0,2},{1,3},{2,0},{3,1},{4,6},{5,7},{6,4},{7,5},{8,10},{9,11},{10,... | collective-permute-start | bytes 1228808 | tf_op jit(solution)/shard_map/exchange/ppermute | solution.py:27
  9.7 19.7 %collective-permute-start.2 = (bf16[64,3200]{1,0:T(8,128)(2,1)S(1)}, bf16[64,3200]{1,0:T(8,128)(2,1)S(1)}, u32[]{:S(2)}, u32[]{:S(2)}) collective-permute-start(bf16[64,3200]{1,0:T(8,128)(2,1)S(1)} %get-tuple-element.27), channel_id=1, source_target_pairs={{0,3},{1,0},{2,1},{3,2},{4,7},{5,4},{6,5},{7,6},{8,11},{9,8},{10,9... | collective-permute-start | bytes 1228808 | tf_op jit(solution)/shard_map/exchange/ppermute | solution.py:27
  10.9 6.0 %collective-permute-start.3 = (bf16[64,128]{1,0:T(8,128)(2,1)S(1)}, bf16[64,128]{1,0:T(8,128)(2,1)S(1)}, u32[]{:S(2)}, u32[]{:S(2)}) collective-permute-start(bf16[64,128]{1,0:T(8,128)(2,1)S(1)} %get-tuple-element.45), channel_id=1, source_target_pairs={{0,4},{4,8},{8,12},{12,16},{16,20},{20,24},{24,28},{28,32},{32,36}... | collective-permute-start | bytes 49160 | tf_op jit(solution)/shard_map/border_rows/ppermute | solution.py:27
  14.0 6.8 %collective-permute-start.5 = (bf16[64,128]{1,0:T(8,128)(2,1)S(1)}, bf16[64,128]{1,0:T(8,128)(2,1)S(1)}, u32[]{:S(2)}, u32[]{:S(2)}) collective-permute-start(bf16[64,128]{1,0:T(8,128)(2,1)S(1)} %get-tuple-element.46), channel_id=1, source_target_pairs={{0,128},{4,132},{8,136},{12,140},{16,144},{20,148},{24,152},{28,15... | collective-permute-start | bytes 49160 | tf_op jit(solution)/shard_map/border_rows/ppermute | solution.py:27
  16.9 4.7 %collective-permute-start.4 = (bf16[64,128]{1,0:T(8,128)(2,1)S(1)}, bf16[64,128]{1,0:T(8,128)(2,1)S(1)}, u32[]{:S(2)}, u32[]{:S(2)}) collective-permute-start(bf16[64,128]{1,0:T(8,128)(2,1)S(1)} %get-tuple-element.47), channel_id=1, source_target_pairs={{0,252},{4,0},{8,4},{12,8},{16,12},{20,16},{24,20},{28,24},{32,28}... | collective-permute-start | bytes 49160 | tf_op jit(solution)/shard_map/border_rows/ppermute | solution.py:27
  21.6 7.7 %copy-start.2 = (s32[9,4096]{1,0:T(8,128)S(1)}, s32[9,4096]{1,0:T(8,128)}, u32[]{:S(2)}) copy-start(s32[9,4096]{1,0:T(8,128)} %neighbors.1) | copy-start | bytes 442372
  57.8 19.9 %all-to-all-start.1 = ((bf16[32,32,256]{2,1,0:T(8,128)(2,1)}), bf16[32,32,256]{2,1,0:T(8,128)(2,1)S(1)}, u32[]{:S(2)}, u32[]{:S(2)}) async-start(bf16[32,32,256]{2,1,0:T(8,128)(2,1)} %bitcast.2), calls=%async_computation.1 | async-start | bytes 1048576 | tf_op jit(solution)/shard_map/weight_sums/all_to_all | solution.py:441
  66.0 13.3 %collective-permute-start.6 = (bf16[64,1536]{1,0:T(8,128)(2,1)S(1)}, bf16[64,1536]{1,0:T(8,128)(2,1)S(1)}, u32[]{:S(2)}, u32[]{:S(2)}) collective-permute-start(bf16[64,1536]{1,0:T(8,128)(2,1)S(1)} %get-tuple-element.29), channel_id=1, source_target_pairs={{0,1},{1,2},{2,3},{3,0},{4,5},{5,6},{6,7},{7,4},{8,9},{9,10},{10,1... | collective-permute-start | bytes 589832 | tf_op jit(solution)/shard_map/return/ppermute | solution.py:27
  67.5 16.3 %collective-permute-start.7 = (bf16[64,1536]{1,0:T(8,128)(2,1)S(1)}, bf16[64,1536]{1,0:T(8,128)(2,1)S(1)}, u32[]{:S(2)}, u32[]{:S(2)}) collective-permute-start(bf16[64,1536]{1,0:T(8,128)(2,1)S(1)} %get-tuple-element.30), channel_id=1, source_target_pairs={{0,2},{1,3},{2,0},{3,1},{4,6},{5,7},{6,4},{7,5},{8,10},{9,11},{10,... | collective-permute-start | bytes 589832 | tf_op jit(solution)/shard_map/return/ppermute | solution.py:27
  69.9 13.9 %collective-permute-start.8 = (bf16[64,1536]{1,0:T(8,128)(2,1)S(1)}, bf16[64,1536]{1,0:T(8,128)(2,1)S(1)}, u32[]{:S(2)}, u32[]{:S(2)}) collective-permute-start(bf16[64,1536]{1,0:T(8,128)(2,1)S(1)} %get-tuple-element.31), channel_id=1, source_target_pairs={{0,3},{1,0},{2,1},{3,2},{4,7},{5,4},{6,5},{7,6},{8,11},{9,8},{10,9... | collective-permute-start | bytes 589832 | tf_op jit(solution)/shard_map/return/ppermute | solution.py:27
  84.5 16.0 %all-to-all-start.2 = ((bf16[8,32,256]{2,1,0:T(8,128)(2,1)}), bf16[8,32,256]{2,1,0:T(8,128)(2,1)S(1)}, u32[]{:S(2)}, u32[]{:S(2)}) async-start(bf16[8,32,256]{2,1,0:T(8,128)(2,1)} %broadcast_in_dim.7), calls=%async_computation.2 | async-start | bytes 262144 | tf_op jit(solution)/shard_map/weight_sums/all_to_all | solution.py:31
  92.7 7.9 %collective-permute-start.9 = (bf16[64,128]{1,0:T(8,128)(2,1)S(1)}, bf16[64,128]{1,0:T(8,128)(2,1)S(1)}, u32[]{:S(2)}, u32[]{:S(2)}) collective-permute-start(bf16[64,128]{1,0:T(8,128)(2,1)S(1)} %get-tuple-element.37), channel_id=1, source_target_pairs={{0,252},{4,0},{8,4},{12,8},{16,12},{20,16},{24,20},{28,24},{32,28}... | collective-permute-start | bytes 49160 | tf_op jit(solution)/shard_map/return/ppermute | solution.py:27
  93.9 6.6 %collective-permute-start.10 = (bf16[64,128]{1,0:T(8,128)(2,1)S(1)}, bf16[64,128]{1,0:T(8,128)(2,1)S(1)}, u32[]{:S(2)}, u32[]{:S(2)}) collective-permute-start(bf16[64,128]{1,0:T(8,128)(2,1)S(1)} %get-tuple-element.38), channel_id=1, source_target_pairs={{0,4},{4,8},{8,12},{12,16},{16,20},{20,24},{24,28},{28,32},{32,36}... | collective-permute-start | bytes 49160 | tf_op jit(solution)/shard_map/return/ppermute | solution.py:27
  95.6 4.9 %collective-permute-start.11 = (bf16[64,128]{1,0:T(8,128)(2,1)S(1)}, bf16[64,128]{1,0:T(8,128)(2,1)S(1)}, u32[]{:S(2)}, u32[]{:S(2)}) collective-permute-start(bf16[64,128]{1,0:T(8,128)(2,1)S(1)} %get-tuple-element.39), channel_id=1, source_target_pairs={{0,128},{4,132},{8,136},{12,140},{16,144},{20,148},{24,152},{28,15... | collective-permute-start | bytes 49160 | tf_op jit(solution)/shard_map/return/ppermute | solution.py:27
  101.3 13.7 %all-to-all-start.3 = ((f32[8,32,256]{2,1,0:T(8,128)}), f32[8,32,256]{2,1,0:T(8,128)S(1)}, u32[]{:S(2)}, u32[]{:S(2)}) async-start(f32[8,32,256]{2,1,0:T(8,128)} %broadcast_in_dim.8), calls=%async_computation.3 | async-start | bytes 524288 | tf_op jit(solution)/shard_map/weight_sums/all_to_all | solution.py:31

commit v5 on v4

--- a/solution.py
+++ b/solution.py
@@ -124,7 +124,7 @@
 
 def attend(
     place, c0, c1, c2, c3, far, neighbors, o0, o1, o2, o3, sums,
-    bias, xe, dy, wq, wkv, wo, qs, ds, kvt, kv, dkv, da, dkvt, grads, summed,
+    bias, xe, dy, wq, wkv, wo, qs, ds, kvt, kv, dkv, dq, att, wflat, dkvt, grads, summed,
     products0, products1, weights0, weights1, means0, means1, qt, dt,
 ):
     head = place[0]
@@ -143,6 +143,7 @@
         xe[pl.ds(row, 64), :ext] = chunk[:, :ext]
         dy[pl.ds(row, 64), :] = chunk[:, ext : ext + own]
         base = ext + own
+        wflat[pl.ds(row, 64), :] = chunk[:, base : base + C]
         for k in range(2):
             dest = pl.multiple_of(source * 128 + 64 * k, 64)
             part = slice(32 * k, 32 * k + 32)
@@ -165,7 +166,7 @@
         ds[cols, :] = block.T
         qt[:, cols] = qs[start + SIDE : start + SIDE + 256, :].T
     dkv[...] = jnp.zeros_like(dkv)
-    da[:, own:] = jnp.zeros((2 * C, 2 * SIDE), F32)
+    dq[:, own:] = jnp.zeros((C, 2 * SIDE), F32)
     lane_head = lax.broadcasted_iota(jnp.int32, (BLOCK, C), 1) // 64
 
     zero = jnp.zeros((BLOCK, C), BF16)
@@ -218,8 +219,9 @@
         )
         result = nn(pair, weights[:, C * hh : C * hh + C])
         grad_query = result[:32, :BLOCK] - result[:32, BLOCK:] * means[hh : hh + 1, :]
-        da[top : top + 32, pl.ds(first, BLOCK)] = grad_query * scale
-        da[top + 32 : top + 64, pl.ds(first, BLOCK)] = result[32:, BLOCK:]
+        low = 128 * g + 32 * hh
+        dq[low : low + 32, pl.ds(first, BLOCK)] = grad_query * scale
+        att[low : low + 32, pl.ds(first, BLOCK)] = result[32:, BLOCK:].astype(BF16)
 
     def spread(b, g, hh, weights, means):
         first = pl.multiple_of(b * BLOCK, BLOCK)
@@ -282,22 +284,22 @@
     for start in range(0, full, 128):
         cols = slice(start, start + 128)
         dkvt[:, cols] = (dkv[:, cols] * row_scale).astype(BF16)
-    own_grads = pltpu.roll(da[...], SIDE, 1).astype(BF16)
-    summed[:, :ext] = (tn(wkv[...], dkvt[:, :ext]) + tn(wq[...], own_grads)).astype(BF16)
+    own_grads = pltpu.roll(dq[...], SIDE, 1).astype(BF16)
+    summed[:, :ext] = (tn(wkv[...], dkvt[:, :ext]) + tn(wflat[...], own_grads)).astype(BF16)
     summed[:, ext:] = tn(wkv[...], dkvt[:, ext:]).astype(BF16)
-    grads[0] = nt(own_grads, xe[:, :ext]).astype(BF16)
-    grads[1] = nt(dkvt[...], xe[...]).astype(BF16)
-    grads[2] = nt(da[:, :own].astype(BF16), dy[...]).astype(BF16)
+    grad_query = nt(own_grads, xe[:, :ext]).astype(BF16)
+    grads[...] = nt(dkvt[...], xe[...]).astype(BF16)
+    grad_out = nt(att[...], dy[...]).astype(BF16)
+    for target in range(4):
+        sums[target, :64, :] = grad_query[64 * target : 64 * target + 64, :]
+        sums[target, 192:, :] = grad_out[64 * target : 64 * target + 64, :]
+        for k in range(2):
+            top = 128 * target + 64 * k
+            sums[target, 64 + 32 * k : 96 + 32 * k, :] = grads[top : top + 32, :]
+            sums[target, 128 + 32 * k : 160 + 32 * k, :] = grads[top + 32 : top + 64, :]
     for step_out, out in enumerate((o0, o1, o2, o3)):
         target = (head + step_out) & 3
         out[...] = summed[pl.ds(pl.multiple_of(target * 64, 64), 64), :]
-    for target in range(4):
-        for k in range(2):
-            top = 128 * target + 64 * k
-            for kind, (which, low) in enumerate(((0, 0), (1, 0), (1, 32), (2, 32))):
-                sums[target, 64 * kind + 32 * k : 64 * kind + 32 * k + 32, :] = grads[
-                    which, top + low : top + low + 32, :
-                ]
 
 
 def add_up(r0, r1, r2, r3, b0, b1, b2):
@@ -369,9 +371,11 @@
             pltpu.VMEM((2 * C, full), BF16),
             pltpu.VMEM((full, 2 * C), BF16),
             pltpu.VMEM((2 * C, full), F32),
-            pltpu.VMEM((2 * C, ext), F32),
+            pltpu.VMEM((C, ext), F32),
+            pltpu.VMEM((C, own), BF16),
+            pltpu.VMEM((C, C), BF16),
             pltpu.VMEM((2 * C, full), BF16),
-            pltpu.VMEM((3, 2 * C, C), BF16),
+            pltpu.VMEM((2 * C, C), BF16),
             pltpu.VMEM((C, full), BF16),
             pltpu.VMEM((cand, 4 * C), F32),
             pltpu.VMEM((cand, 4 * C), F32),

time: 117 us -> 116 us (level)
  no operation moved by 1% of the time
where the time goes in v5:
time: 116 us
  starting transfers between devices  49.9 us (43%)
  Pallas kernels  32.2 us (28%)
  waiting for transfers between devices  19.7 us (17%)
  blocking collectives  7.68 us (7%)
  local copies, waits for them, and re-layouts  5.35 us (5%)
    pallas_call x5, Pallas kernels, kernel_call(): pl.pallas_call(body, out_shape=out_shape, in_specs=specs, out_specs=outs,...  32.2 us
    ppermute x12, starting transfers between devices, passed_along(): return lax.ppermute(value, axis, pairs)  26.3 us
    all_to_all x2, starting transfers between devices, grouped(): return lax.all_to_all(value, 'tile', 0, 0, axis_index_groups=groups)  15.4 us
    all_to_all x1, starting transfers between devices, local(): lax.all_to_all(sums.reshape(32, C // 8, C), ('tile', 'head'), 0, 0, axis_...  8.2 us
    all_to_all x1, blocking collectives, local(): lax.all_to_all(jnp.broadcast_to(mine[None], (4, 64, 3 * border)), 'head',...  7.68 us
    ppermute x12, waiting for transfers between devices, passed_along(): return lax.ppermute(value, axis, pairs)  6.83 us
    all_to_all x1, waiting for transfers between devices, local(): lax.all_to_all(sums.reshape(32, C // 8, C), ('tile', 'head'), 0, 0, axis_...  6.7 us
    all_to_all x2, waiting for transfers between devices, grouped(): return lax.all_to_all(value, 'tile', 0, 0, axis_index_groups=groups)  6.22 us
  transfers between devices with their start and end apart: 15, of which 6 were waited for; matrix products, arithmetic and copies ran while one was open for 0% of the time, Pallas kernels for 2%

profile of v5, /device:TPU:1, one launch (start us, length us, event | category | flops | bytes accessed | tf_op | source)
XLA Modules:
  0.0 115.8 jit_solution(4508864436782469118)
XLA Ops:
  0.6 0.0 copy-start.5
  0.6 0.7 copy-done.5
  1.3 0.0 copy-start
  1.3 1.0 copy-done
  2.4 0.0 copy-start.1
  2.4 0.0 copy-start.4
  2.4 1.2 %border_rows.1.halo = bf16[64,384]{1,0:T(8,128)(2,1)S(1)} custom-call(bf16[64,4096]{1,0:T(8,128)(2,1)S(1)} %copy-done, s32[1,384]{1,0:T(1,128)S(1)} %bitcast.5), custom_call_target="tpu_custom_call" | custom-call | tf_op jit(solution)/shard_map/border_rows/pallas_call | solution.py:342
  3.6 0.0 copy-done.1
  3.6 0.0 copy-done.4
  3.6 0.0 copy-start.3
  3.6 0.9 copy-done.3
  4.5 0.7 prepare.1
  5.1 2.1 %collective-permute-start = (bf16[64,3200]{1,0:T(8,128)(2,1)S(1)}, bf16[64,3200]{1,0:T(8,128)(2,1)S(1)}, u32[]{:S(2)}, u32[]{:S(2)}) collective-permute-start(bf16[64,3200]{1,0:T(8,128)(2,1)S(1)} %get-tuple-element.25), channel_id=1, source_target_pairs={{0,1},{1,2},{2,3},{3,0},{4,5},{5,6},{6,7},{7,4},{8,9},{9,10},{10,1... | collective-permute-start | bytes 1228808 | tf_op jit(solution)/shard_map/exchange/ppermute | solution.py:27
  7.3 2.5 %collective-permute-start.1 = (bf16[64,3200]{1,0:T(8,128)(2,1)S(1)}, bf16[64,3200]{1,0:T(8,128)(2,1)S(1)}, u32[]{:S(2)}, u32[]{:S(2)}) collective-permute-start(bf16[64,3200]{1,0:T(8,128)(2,1)S(1)} %get-tuple-element.26), channel_id=1, source_target_pairs={{0,2},{1,3},{2,0},{3,1},{4,6},{5,7},{6,4},{7,5},{8,10},{9,11},{10,... | collective-permute-start | bytes 1228808 | tf_op jit(solution)/shard_map/exchange/ppermute | solution.py:27
  9.7 1.1 collective-permute-start.2
  10.9 3.1 %collective-permute-start.3 = (bf16[64,128]{1,0:T(8,128)(2,1)S(1)}, bf16[64,128]{1,0:T(8,128)(2,1)S(1)}, u32[]{:S(2)}, u32[]{:S(2)}) collective-permute-start(bf16[64,128]{1,0:T(8,128)(2,1)S(1)} %get-tuple-element.45), channel_id=1, source_target_pairs={{0,4},{4,8},{8,12},{12,16},{16,20},{20,24},{24,28},{28,32},{32,36}... | collective-permute-start | bytes 49160 | tf_op jit(solution)/shard_map/border_rows/ppermute | solution.py:27
  14.0 2.9 %collective-permute-start.5 = (bf16[64,128]{1,0:T(8,128)(2,1)S(1)}, bf16[64,128]{1,0:T(8,128)(2,1)S(1)}, u32[]{:S(2)}, u32[]{:S(2)}) collective-permute-start(bf16[64,128]{1,0:T(8,128)(2,1)S(1)} %get-tuple-element.46), channel_id=1, source_target_pairs={{0,128},{4,132},{8,136},{12,140},{16,144},{20,148},{24,152},{28,15... | collective-permute-start | bytes 49160 | tf_op jit(solution)/shard_map/border_rows/ppermute | solution.py:27
  16.9 0.0 collective-permute-done.3
  16.9 3.9 %collective-permute-start.4 = (bf16[64,128]{1,0:T(8,128)(2,1)S(1)}, bf16[64,128]{1,0:T(8,128)(2,1)S(1)}, u32[]{:S(2)}, u32[]{:S(2)}) collective-permute-start(bf16[64,128]{1,0:T(8,128)(2,1)S(1)} %get-tuple-element.47), channel_id=1, source_target_pairs={{0,252},{4,0},{8,4},{12,8},{16,12},{20,16},{24,20},{28,24},{32,28}... | collective-permute-start | bytes 49160 | tf_op jit(solution)/shard_map/border_rows/ppermute | solution.py:27
  20.8 0.0 collective-permute-done.5
  20.8 0.8 collective-permute-done.4
  21.6 0.0 copy-start.2
  21.7 7.7 %all_to_all.20.far = bf16[4,64,384]{2,1,0:T(8,128)(2,1)S(1)} all-to-all(bf16[4,64,384]{2,1,0:T(8,128)(2,1)S(1)} %broadcast_in_dim.6), channel_id=1, replica_groups=mesh['tile'=64,'head'=4] {'head'}, dimensions={0} | all-to-all | bytes 393216 | tf_op jit(solution)/shard_map/border_rows/all_to_all | solution.py:435
  29.4 0.0 collective-permute-done.c1
  29.4 0.0 collective-permute-done.1.c2
  29.4 0.0 collective-permute-done.2.c3
  29.4 0.0 copy-done.2
  29.4 27.8 %attention.1 = (bf16[64,1536]{1,0:T(8,128)(2,1)S(1)}, bf16[64,1536]{1,0:T(8,128)(2,1)S(1)}, bf16[64,1536]{1,0:T(8,128)(2,1)S(1)}, bf16[64,1536]{1,0:T(8,128)(2,1)S(1)}, bf16[4,256,256]{2,1,0:T(8,128)(2,1)}) custom-call(s32[1]{0:T(128)} %bitcast.place, bf16[64,3200]{1,0:T(8,128)(2,1)S(1)} %get-tuple-element.24.c0, ...), custom_call_target="tpu_custom_call" | custom-call | tf_op jit(solution)/shard_map/attention/pallas_call | solution.py:342
  57.2 8.2 %all-to-all-start.1 = ((bf16[32,32,256]{2,1,0:T(8,128)(2,1)}), bf16[32,32,256]{2,1,0:T(8,128)(2,1)S(1)}, u32[]{:S(2)}, u32[]{:S(2)}) async-start(bf16[32,32,256]{2,1,0:T(8,128)(2,1)} %bitcast.2), calls=%async_computation.1 | async-start | bytes 1048576 | tf_op jit(solution)/shard_map/weight_sums/all_to_all | solution.py:445
  65.4 1.5 %collective-permute-start.6 = (bf16[64,1536]{1,0:T(8,128)(2,1)S(1)}, bf16[64,1536]{1,0:T(8,128)(2,1)S(1)}, u32[]{:S(2)}, u32[]{:S(2)}) collective-permute-start(bf16[64,1536]{1,0:T(8,128)(2,1)S(1)} %get-tuple-element.29), channel_id=1, source_target_pairs={{0,1},{1,2},{2,3},{3,0},{4,5},{5,6},{6,7},{7,4},{8,9},{9,10},{10,1... | collective-permute-start | bytes 589832 | tf_op jit(solution)/shard_map/return/ppermute | solution.py:27
  66.9 2.4 %collective-permute-start.7 = (bf16[64,1536]{1,0:T(8,128)(2,1)S(1)}, bf16[64,1536]{1,0:T(8,128)(2,1)S(1)}, u32[]{:S(2)}, u32[]{:S(2)}) collective-permute-start(bf16[64,1536]{1,0:T(8,128)(2,1)S(1)} %get-tuple-element.30), channel_id=1, source_target_pairs={{0,2},{1,3},{2,0},{3,1},{4,6},{5,7},{6,4},{7,5},{8,10},{9,11},{10,... | collective-permute-start | bytes 589832 | tf_op jit(solution)/shard_map/return/ppermute | solution.py:27
  69.3 1.1 collective-permute-start.8
  70.5 6.7 %all-to-all-done.1 = bf16[32,32,256]{2,1,0:T(8,128)(2,1)S(1)} async-done(((bf16[32,32,256]{2,1,0:T(8,128)(2,1)}), bf16[32,32,256]{2,1,0:T(8,128)(2,1)S(1)}, u32[]{:S(2)}, u32[]{:S(2)}) %all-to-all-start.1) | async-done | bytes 524320 | tf_op jit(solution)/shard_map/weight_sums/all_to_all | solution.py:445
  77.2 0.1 reduce_sum.21
  77.3 1.5 %collective-permute-done.6.r1 = bf16[64,1536]{1,0:T(8,128)(2,1)S(1)} collective-permute-done((bf16[64,1536]{1,0:T(8,128)(2,1)S(1)}, bf16[64,1536]{1,0:T(8,128)(2,1)S(1)}, u32[]{:S(2)}, u32[]{:S(2)}) %collective-permute-start.6) | collective-permute-done | bytes 196640 | tf_op jit(solution)/shard_map/return/ppermute | solution.py:27
  78.8 4.5 %collective-permute-done.7.r2 = bf16[64,1536]{1,0:T(8,128)(2,1)S(1)} collective-permute-done((bf16[64,1536]{1,0:T(8,128)(2,1)S(1)}, bf16[64,1536]{1,0:T(8,128)(2,1)S(1)}, u32[]{:S(2)}, u32[]{:S(2)}) %collective-permute-start.7) | collective-permute-done | bytes 196640 | tf_op jit(solution)/shard_map/return/ppermute | solution.py:27
  83.2 0.0 collective-permute-done.8.r3
  83.2 0.7 broadcast_in_dim.7
  83.9 8.2 %all-to-all-start.2 = ((bf16[8,32,256]{2,1,0:T(8,128)(2,1)}), bf16[8,32,256]{2,1,0:T(8,128)(2,1)S(1)}, u32[]{:S(2)}, u32[]{:S(2)}) async-start(bf16[8,32,256]{2,1,0:T(8,128)(2,1)} %broadcast_in_dim.7), calls=%async_computation.2 | async-start | bytes 262144 | tf_op jit(solution)/shard_map/weight_sums/all_to_all | solution.py:31
  92.1 1.2 %collective-permute-start.9 = (bf16[64,128]{1,0:T(8,128)(2,1)S(1)}, bf16[64,128]{1,0:T(8,128)(2,1)S(1)}, u32[]{:S(2)}, u32[]{:S(2)}) collective-permute-start(bf16[64,128]{1,0:T(8,128)(2,1)S(1)} %get-tuple-element.37), channel_id=1, source_target_pairs={{0,252},{4,0},{8,4},{12,8},{16,12},{20,16},{24,20},{28,24},{32,28}... | collective-permute-start | bytes 49160 | tf_op jit(solution)/shard_map/return/ppermute | solution.py:27
  93.4 1.7 %collective-permute-start.10 = (bf16[64,128]{1,0:T(8,128)(2,1)S(1)}, bf16[64,128]{1,0:T(8,128)(2,1)S(1)}, u32[]{:S(2)}, u32[]{:S(2)}) collective-permute-start(bf16[64,128]{1,0:T(8,128)(2,1)S(1)} %get-tuple-element.38), channel_id=1, source_target_pairs={{0,4},{4,8},{8,12},{12,16},{16,20},{20,24},{24,28},{28,32},{32,36}... | collective-permute-start | bytes 49160 | tf_op jit(solution)/shard_map/return/ppermute | solution.py:27
  95.1 2.7 %collective-permute-start.11 = (bf16[64,128]{1,0:T(8,128)(2,1)S(1)}, bf16[64,128]{1,0:T(8,128)(2,1)S(1)}, u32[]{:S(2)}, u32[]{:S(2)}) collective-permute-start(bf16[64,128]{1,0:T(8,128)(2,1)S(1)} %get-tuple-element.39), channel_id=1, source_target_pairs={{0,128},{4,132},{8,136},{12,140},{16,144},{20,148},{24,152},{28,15... | collective-permute-start | bytes 49160 | tf_op jit(solution)/shard_map/return/ppermute | solution.py:27
  97.8 2.2 %all-to-all-done.2 = bf16[8,32,256]{2,1,0:T(8,128)(2,1)S(1)} async-done(((bf16[8,32,256]{2,1,0:T(8,128)(2,1)}), bf16[8,32,256]{2,1,0:T(8,128)(2,1)S(1)}, u32[]{:S(2)}, u32[]{:S(2)}) %all-to-all-start.2) | async-done | bytes 131104 | tf_op jit(solution)/shard_map/weight_sums/all_to_all | solution.py:31
  100.0 0.0 collective-permute-done.9.b0
  100.0 0.0 collective-permute-done.10.b1
  100.0 0.0 collective-permute-done.11.b2
  100.0 0.7 broadcast_in_dim.8
  100.8 7.2 %all-to-all-start.3 = ((f32[8,32,256]{2,1,0:T(8,128)}), f32[8,32,256]{2,1,0:T(8,128)S(1)}, u32[]{:S(2)}, u32[]{:S(2)}) async-start(f32[8,32,256]{2,1,0:T(8,128)} %broadcast_in_dim.8), calls=%async_computation.3 | async-start | bytes 524288 | tf_op jit(solution)/shard_map/weight_sums/all_to_all | solution.py:31
  107.9 2.5 %return.3 = f32[64,4096]{1,0:T(8,128)} custom-call(s32[1]{0:T(128)} %bitcast.place, bf16[64,1536]{1,0:T(8,128)(2,1)S(1)} %get-tuple-element.33.r0, bf16[64,1536]{1,0:T(8,128)(2,1)S(1)} %collective-permute-done.6.r1, bf16[64,1536]{1,0:T(8,128)(2,1)S(1)} %collective-permute-done.7.r2, bf16[64,1536]{1,0:T(8,128)(2,1)S(1)} %collective-permute-done.8.r3, ...), custom_call_target="tpu_custom_call" | custom-call | tf_op jit(solution)/shard_map/return/pallas_call | solution.py:342
  110.4 4.0 %all-to-all-done.3 = f32[8,32,256]{2,1,0:T(8,128)S(1)} async-done(((f32[8,32,256]{2,1,0:T(8,128)}), f32[8,32,256]{2,1,0:T(8,128)S(1)}, u32[]{:S(2)}, u32[]{:S(2)}) %all-to-all-start.3) | async-done | bytes 262176 | tf_op jit(solution)/shard_map/weight_sums/all_to_all | solution.py:31
  114.5 0.6 slice.29
  115.1 0.7 slice.28
  (6 shorter events, 0.1 us)
Async XLA Ops:
  0.6 0.7 copy-start.5
  1.3 1.0 copy-start
  2.4 1.2 %copy-start.1 = (bf16[64,4096]{1,0:T(8,128)(2,1)S(1)}, bf16[64,4096]{1,0:T(8,128)(2,1)}, u32[]{:S(2)}) copy-start(bf16[64,4096]{1,0:T(8,128)(2,1)} %grad_in.3) | copy-start | bytes 1572868
  2.4 1.2 %copy-start.4 = (bf16[64,256]{1,0:T(8,128)(2,1)S(1)}, bf16[64,256]{1,0:T(8,128)(2,1)}, u32[]{:S(2)}) copy-start(bf16[64,256]{1,0:T(8,128)(2,1)} %w_out.1) | copy-start | bytes 98308
  3.6 0.9 copy-start.3
  5.1 24.2 %collective-permute-start = (bf16[64,3200]{1,0:T(8,128)(2,1)S(1)}, bf16[64,3200]{1,0:T(8,128)(2,1)S(1)}, u32[]{:S(2)}, u32[]{:S(2)}) collective-permute-start(bf16[64,3200]{1,0:T(8,128)(2,1)S(1)} %get-tuple-element.25), channel_id=1, source_target_pairs={{0,1},{1,2},{2,3},{3,0},{4,5},{5,6},{6,7},{7,4},{8,9},{9,10},{10,1... | collective-permute-start | bytes 1228808 | tf_op jit(solution)/shard_map/exchange/ppermute | solution.py:27
  7.3 22.1 %collective-permute-start.1 = (bf16[64,3200]{1,0:T(8,128)(2,1)S(1)}, bf16[64,3200]{1,0:T(8,128)(2,1)S(1)}, u32[]{:S(2)}, u32[]{:S(2)}) collective-permute-start(bf16[64,3200]{1,0:T(8,128)(2,1)S(1)} %get-tuple-element.26), channel_id=1, source_target_pairs={{0,2},{1,3},{2,0},{3,1},{4,6},{5,7},{6,4},{7,5},{8,10},{9,11},{10,... | collective-permute-start | bytes 1228808 | tf_op jit(solution)/shard_map/exchange/ppermute | solution.py:27
  9.7 19.7 %collective-permute-start.2 = (bf16[64,3200]{1,0:T(8,128)(2,1)S(1)}, bf16[64,3200]{1,0:T(8,128)(2,1)S(1)}, u32[]{:S(2)}, u32[]{:S(2)}) collective-permute-start(bf16[64,3200]{1,0:T(8,128)(2,1)S(1)} %get-tuple-element.27), channel_id=1, source_target_pairs={{0,3},{1,0},{2,1},{3,2},{4,7},{5,4},{6,5},{7,6},{8,11},{9,8},{10,9... | collective-permute-start | bytes 1228808 | tf_op jit(solution)/shard_map/exchange/ppermute | solution.py:27
  10.9 6.0 %collective-permute-start.3 = (bf16[64,128]{1,0:T(8,128)(2,1)S(1)}, bf16[64,128]{1,0:T(8,128)(2,1)S(1)}, u32[]{:S(2)}, u32[]{:S(2)}) collective-permute-start(bf16[64,128]{1,0:T(8,128)(2,1)S(1)} %get-tuple-element.45), channel_id=1, source_target_pairs={{0,4},{4,8},{8,12},{12,16},{16,20},{20,24},{24,28},{28,32},{32,36}... | collective-permute-start | bytes 49160 | tf_op jit(solution)/shard_map/border_rows/ppermute | solution.py:27
  14.0 6.8 %collective-permute-start.5 = (bf16[64,128]{1,0:T(8,128)(2,1)S(1)}, bf16[64,128]{1,0:T(8,128)(2,1)S(1)}, u32[]{:S(2)}, u32[]{:S(2)}) collective-permute-start(bf16[64,128]{1,0:T(8,128)(2,1)S(1)} %get-tuple-element.46), channel_id=1, source_target_pairs={{0,128},{4,132},{8,136},{12,140},{16,144},{20,148},{24,152},{28,15... | collective-permute-start | bytes 49160 | tf_op jit(solution)/shard_map/border_rows/ppermute | solution.py:27
  16.9 4.7 %collective-permute-start.4 = (bf16[64,128]{1,0:T(8,128)(2,1)S(1)}, bf16[64,128]{1,0:T(8,128)(2,1)S(1)}, u32[]{:S(2)}, u32[]{:S(2)}) collective-permute-start(bf16[64,128]{1,0:T(8,128)(2,1)S(1)} %get-tuple-element.47), channel_id=1, source_target_pairs={{0,252},{4,0},{8,4},{12,8},{16,12},{20,16},{24,20},{28,24},{32,28}... | collective-permute-start | bytes 49160 | tf_op jit(solution)/shard_map/border_rows/ppermute | solution.py:27
  21.6 7.7 %copy-start.2 = (s32[9,4096]{1,0:T(8,128)S(1)}, s32[9,4096]{1,0:T(8,128)}, u32[]{:S(2)}) copy-start(s32[9,4096]{1,0:T(8,128)} %neighbors.1) | copy-start | bytes 442372
  57.2 20.0 %all-to-all-start.1 = ((bf16[32,32,256]{2,1,0:T(8,128)(2,1)}), bf16[32,32,256]{2,1,0:T(8,128)(2,1)S(1)}, u32[]{:S(2)}, u32[]{:S(2)}) async-start(bf16[32,32,256]{2,1,0:T(8,128)(2,1)} %bitcast.2), calls=%async_computation.1 | async-start | bytes 1048576 | tf_op jit(solution)/shard_map/weight_sums/all_to_all | solution.py:445
  65.4 13.3 %collective-permute-start.6 = (bf16[64,1536]{1,0:T(8,128)(2,1)S(1)}, bf16[64,1536]{1,0:T(8,128)(2,1)S(1)}, u32[]{:S(2)}, u32[]{:S(2)}) collective-permute-start(bf16[64,1536]{1,0:T(8,128)(2,1)S(1)} %get-tuple-element.29), channel_id=1, source_target_pairs={{0,1},{1,2},{2,3},{3,0},{4,5},{5,6},{6,7},{7,4},{8,9},{9,10},{10,1... | collective-permute-start | bytes 589832 | tf_op jit(solution)/shard_map/return/ppermute | solution.py:27
  66.9 16.3 %collective-permute-start.7 = (bf16[64,1536]{1,0:T(8,128)(2,1)S(1)}, bf16[64,1536]{1,0:T(8,128)(2,1)S(1)}, u32[]{:S(2)}, u32[]{:S(2)}) collective-permute-start(bf16[64,1536]{1,0:T(8,128)(2,1)S(1)} %get-tuple-element.30), channel_id=1, source_target_pairs={{0,2},{1,3},{2,0},{3,1},{4,6},{5,7},{6,4},{7,5},{8,10},{9,11},{10,... | collective-permute-start | bytes 589832 | tf_op jit(solution)/shard_map/return/ppermute | solution.py:27
  69.3 13.9 %collective-permute-start.8 = (bf16[64,1536]{1,0:T(8,128)(2,1)S(1)}, bf16[64,1536]{1,0:T(8,128)(2,1)S(1)}, u32[]{:S(2)}, u32[]{:S(2)}) collective-permute-start(bf16[64,1536]{1,0:T(8,128)(2,1)S(1)} %get-tuple-element.31), channel_id=1, source_target_pairs={{0,3},{1,0},{2,1},{3,2},{4,7},{5,4},{6,5},{7,6},{8,11},{9,8},{10,9... | collective-permute-start | bytes 589832 | tf_op jit(solution)/shard_map/return/ppermute | solution.py:27
  83.9 16.1 %all-to-all-start.2 = ((bf16[8,32,256]{2,1,0:T(8,128)(2,1)}), bf16[8,32,256]{2,1,0:T(8,128)(2,1)S(1)}, u32[]{:S(2)}, u32[]{:S(2)}) async-start(bf16[8,32,256]{2,1,0:T(8,128)(2,1)} %broadcast_in_dim.7), calls=%async_computation.2 | async-start | bytes 262144 | tf_op jit(solution)/shard_map/weight_sums/all_to_all | solution.py:31
  92.1 7.9 %collective-permute-start.9 = (bf16[64,128]{1,0:T(8,128)(2,1)S(1)}, bf16[64,128]{1,0:T(8,128)(2,1)S(1)}, u32[]{:S(2)}, u32[]{:S(2)}) collective-permute-start(bf16[64,128]{1,0:T(8,128)(2,1)S(1)} %get-tuple-element.37), channel_id=1, source_target_pairs={{0,252},{4,0},{8,4},{12,8},{16,12},{20,16},{24,20},{28,24},{32,28}... | collective-permute-start | bytes 49160 | tf_op jit(solution)/shard_map/return/ppermute | solution.py:27
  93.4 6.6 %collective-permute-start.10 = (bf16[64,128]{1,0:T(8,128)(2,1)S(1)}, bf16[64,128]{1,0:T(8,128)(2,1)S(1)}, u32[]{:S(2)}, u32[]{:S(2)}) collective-permute-start(bf16[64,128]{1,0:T(8,128)(2,1)S(1)} %get-tuple-element.38), channel_id=1, source_target_pairs={{0,4},{4,8},{8,12},{12,16},{16,20},{20,24},{24,28},{28,32},{32,36}... | collective-permute-start | bytes 49160 | tf_op jit(solution)/shard_map/return/ppermute | solution.py:27
  95.1 4.9 %collective-permute-start.11 = (bf16[64,128]{1,0:T(8,128)(2,1)S(1)}, bf16[64,128]{1,0:T(8,128)(2,1)S(1)}, u32[]{:S(2)}, u32[]{:S(2)}) collective-permute-start(bf16[64,128]{1,0:T(8,128)(2,1)S(1)} %get-tuple-element.39), channel_id=1, source_target_pairs={{0,128},{4,132},{8,136},{12,140},{16,144},{20,148},{24,152},{28,15... | collective-permute-start | bytes 49160 | tf_op jit(solution)/shard_map/return/ppermute | solution.py:27
  100.8 13.7 %all-to-all-start.3 = ((f32[8,32,256]{2,1,0:T(8,128)}), f32[8,32,256]{2,1,0:T(8,128)S(1)}, u32[]{:S(2)}, u32[]{:S(2)}) async-start(f32[8,32,256]{2,1,0:T(8,128)} %broadcast_in_dim.8), calls=%async_computation.3 | async-start | bytes 524288 | tf_op jit(solution)/shard_map/weight_sums/all_to_all | solution.py:31

commit v6 on v5

--- a/solution.py
+++ b/solution.py
@@ -446,22 +446,21 @@
             sums.reshape(32, C // 8, C), ("tile", "head"), 0, 0, axis_index_groups=plates(4)
         )
         value = value.astype(F32).sum(0).astype(BF16)
+    with jax.named_scope("weight_sums"):
+        line = [[16 * y + 2 * z + c for z in range(8)] for y in range(4) for c in range(2)]
+        piece = (8, C // 8, C)
+        value = grouped(jnp.broadcast_to(value[None], piece), line)
+        grad_scale = 1.0 / math.sqrt(rows * groups)
+        value = value.astype(F32).sum(0) * grad_scale
         *parts, value = lax.optimization_barrier((*parts, value))
+        value = grouped(jnp.broadcast_to(value[None], piece), plates(1))
+        value = value.reshape(4, 64, C)
     with jax.named_scope("return"):
         back = kernel_call(add_up, [sds((64, border), BF16)] * 3, tuple(parts))
         back = [
             passed_along(back[peer], "tile", (groups - offsets[peer]) % groups)
             for peer in range(3)
         ]
-    with jax.named_scope("weight_sums"):
-        line = [[16 * y + 2 * z + c for z in range(8)] for y in range(4) for c in range(2)]
-        piece = (8, C // 8, C)
-        value = grouped(jnp.broadcast_to(value[None], piece), line)
-        grad_scale = 1.0 / math.sqrt(rows * groups)
-        value = value.astype(F32).sum(0) * grad_scale
-        *back, value = lax.optimization_barrier((*back, value))
-        value = grouped(jnp.broadcast_to(value[None], piece), plates(1))
-        value = value.reshape(4, 64, C)
     with jax.named_scope("return"):
         d_tokens = kernel_call(
             finish,

time: 116 us -> 117 us (level)
  the two profiles are of different devices: /device:TPU:1 before, /device:TPU:6 now
where the time goes in v6:
time: 117 us
  Pallas kernels  31.4 us (27%)
  starting transfers between devices  28.2 us (24%)
  blocking collectives  26.8 us (23%)
  waiting for transfers between devices  23.9 us (20%)
  local copies, waits for them, and re-layouts  5.36 us (5%)
    pallas_call x5, Pallas kernels, kernel_call(): pl.pallas_call(body, out_shape=out_shape, in_specs=specs, out_specs=outs,...  31.4 us
    ppermute x12, waiting for transfers between devices, passed_along(): return lax.ppermute(value, axis, pairs)  17.4 us
    all_to_all x1, blocking collectives, local(): lax.all_to_all(sums.reshape(32, C // 8, C), ('tile', 'head'), 0, 0, axis_...  16.7 us
    ppermute x12, starting transfers between devices, passed_along(): return lax.ppermute(value, axis, pairs)  16.3 us
    all_to_all x2, starting transfers between devices, grouped(): return lax.all_to_all(value, 'tile', 0, 0, axis_index_groups=groups)  11.9 us
    all_to_all x1, blocking collectives, local(): lax.all_to_all(jnp.broadcast_to(mine[None], (4, 64, 3 * border)), 'head',...  10.2 us
    all_to_all x2, waiting for transfers between devices, grouped(): return lax.all_to_all(value, 'tile', 0, 0, axis_index_groups=groups)  6.48 us
    unnamed x12, local copies, waits for them, and re-layouts  2.61 us
  transfers between devices with their start and end apart: 14, of which 8 were waited for; matrix products, arithmetic and copies ran while one was open for 0% of the time, Pallas kernels for 2%

profile of v6, /device:TPU:6, one launch (start us, length us, event | category | flops | bytes accessed | tf_op | source)
XLA Modules:
  0.0 116.6 jit_solution(5981740861010681494)
XLA Ops:
  0.6 0.0 copy-start.5
  0.6 0.7 copy-done.5
  1.3 0.0 copy-start
  1.3 1.0 copy-done
  2.4 0.0 copy-start.1
  2.4 0.0 copy-start.4
  2.4 1.2 %border_rows.1.halo = bf16[64,384]{1,0:T(8,128)(2,1)S(1)} custom-call(bf16[64,4096]{1,0:T(8,128)(2,1)S(1)} %copy-done, s32[1,384]{1,0:T(1,128)S(1)} %bitcast.6), custom_call_target="tpu_custom_call" | custom-call | tf_op jit(solution)/shard_map/border_rows/pallas_call | solution.py:342
  3.6 0.0 copy-done.1
  3.6 0.0 copy-done.4
  3.6 0.0 copy-start.3
  3.6 0.9 copy-done.3
  4.5 0.7 prepare.1
  5.1 2.3 %collective-permute-start = (bf16[64,3200]{1,0:T(8,128)(2,1)S(1)}, bf16[64,3200]{1,0:T(8,128)(2,1)S(1)}, u32[]{:S(2)}, u32[]{:S(2)}) collective-permute-start(bf16[64,3200]{1,0:T(8,128)(2,1)S(1)} %get-tuple-element.21), channel_id=1, source_target_pairs={{0,1},{1,2},{2,3},{3,0},{4,5},{5,6},{6,7},{7,4},{8,9},{9,10},{10,1... | collective-permute-start | bytes 1228808 | tf_op jit(solution)/shard_map/exchange/ppermute | solution.py:27
  7.4 0.7 collective-permute-start.1
  8.1 0.3 collective-permute-start.2
  8.4 0.1 collective-permute-start.3
  8.5 3.0 %collective-permute-start.5 = (bf16[64,128]{1,0:T(8,128)(2,1)S(1)}, bf16[64,128]{1,0:T(8,128)(2,1)S(1)}, u32[]{:S(2)}, u32[]{:S(2)}) collective-permute-start(bf16[64,128]{1,0:T(8,128)(2,1)S(1)} %get-tuple-element.38), channel_id=1, source_target_pairs={{0,128},{4,132},{8,136},{12,140},{16,144},{20,148},{24,152},{28,15... | collective-permute-start | bytes 49160 | tf_op jit(solution)/shard_map/border_rows/ppermute | solution.py:27
  11.5 5.3 %collective-permute-done.3 = bf16[64,128]{1,0:T(8,128)(2,1)S(1)} collective-permute-done((bf16[64,128]{1,0:T(8,128)(2,1)S(1)}, bf16[64,128]{1,0:T(8,128)(2,1)S(1)}, u32[]{:S(2)}, u32[]{:S(2)}) %collective-permute-start.3) | collective-permute-done | bytes 16416 | tf_op jit(solution)/shard_map/border_rows/ppermute | solution.py:27
  16.8 0.5 collective-permute-start.4
  17.3 0.0 collective-permute-done.5
  17.3 1.4 %collective-permute-done.4 = bf16[64,128]{1,0:T(8,128)(2,1)S(1)} collective-permute-done((bf16[64,128]{1,0:T(8,128)(2,1)S(1)}, bf16[64,128]{1,0:T(8,128)(2,1)S(1)}, u32[]{:S(2)}, u32[]{:S(2)}) %collective-permute-start.4) | collective-permute-done | bytes 16416 | tf_op jit(solution)/shard_map/border_rows/ppermute | solution.py:27
  18.8 0.0 copy-start.2
  18.8 10.2 %all_to_all.20.far = bf16[4,64,384]{2,1,0:T(8,128)(2,1)S(1)} all-to-all(bf16[4,64,384]{2,1,0:T(8,128)(2,1)S(1)} %broadcast_in_dim.6), channel_id=1, replica_groups=mesh['tile'=64,'head'=4] {'head'}, dimensions={0} | all-to-all | bytes 393216 | tf_op jit(solution)/shard_map/border_rows/all_to_all | solution.py:435
  29.0 0.0 collective-permute-done.c1
  29.0 0.0 collective-permute-done.1.c2
  29.0 0.0 collective-permute-done.2.c3
  29.0 0.0 copy-done.2
  29.0 27.0 %attention.1 = (bf16[64,1536]{1,0:T(8,128)(2,1)S(1)}, bf16[64,1536]{1,0:T(8,128)(2,1)S(1)}, bf16[64,1536]{1,0:T(8,128)(2,1)S(1)}, bf16[64,1536]{1,0:T(8,128)(2,1)S(1)}, bf16[4,256,256]{2,1,0:T(8,128)(2,1)S(1)}) custom-call(s32[1]{0:T(128)} %bitcast.place, bf16[64,3200]{1,0:T(8,128)(2,1)S(1)} %get-tuple-element.20.c0, ...), custom_call_target="tpu_custom_call" | custom-call | tf_op jit(solution)/shard_map/attention/pallas_call | solution.py:342
  56.0 16.7 %all_to_all.21 = bf16[32,32,256]{2,1,0:T(8,128)(2,1)S(1)} all-to-all(bf16[32,32,256]{2,1,0:T(8,128)(2,1)S(1)} %bitcast.5), channel_id=1, replica_groups={{0,4,64,68,128,132,192,196,1,5,65,69,129,133,193,197,2,6,66,70,130,134,..., dimensions={0} | all-to-all | bytes 1048576 | tf_op jit(solution)/shard_map/weight_sums/all_to_all | solution.py:445
  72.7 0.1 reduce_sum.21
  72.8 0.7 broadcast_in_dim.7
  73.5 8.5 %all-to-all-start.2 = ((bf16[8,32,256]{2,1,0:T(8,128)(2,1)}), bf16[8,32,256]{2,1,0:T(8,128)(2,1)S(1)}, u32[]{:S(2)}, u32[]{:S(2)}) async-start(bf16[8,32,256]{2,1,0:T(8,128)(2,1)} %broadcast_in_dim.7), calls=%async_computation.2 | async-start | bytes 262144 | tf_op jit(solution)/shard_map/weight_sums/all_to_all | solution.py:31
  82.0 2.1 %collective-permute-start.6 = (bf16[64,1536]{1,0:T(8,128)(2,1)S(1)}, bf16[64,1536]{1,0:T(8,128)(2,1)S(1)}, u32[]{:S(2)}, u32[]{:S(2)}) collective-permute-start(bf16[64,1536]{1,0:T(8,128)(2,1)S(1)} %get-tuple-element.25), channel_id=1, source_target_pairs={{0,1},{1,2},{2,3},{3,0},{4,5},{5,6},{6,7},{7,4},{8,9},{9,10},{10,1... | collective-permute-start | bytes 589832 | tf_op jit(solution)/shard_map/return/ppermute | solution.py:27
  84.0 1.1 collective-permute-start.7
  85.1 0.1 collective-permute-start.8
  85.2 6.5 %all-to-all-done.2 = bf16[8,32,256]{2,1,0:T(8,128)(2,1)S(1)} async-done(((bf16[8,32,256]{2,1,0:T(8,128)(2,1)}), bf16[8,32,256]{2,1,0:T(8,128)(2,1)S(1)}, u32[]{:S(2)}, u32[]{:S(2)}) %all-to-all-start.2) | async-done | bytes 131104 | tf_op jit(solution)/shard_map/weight_sums/all_to_all | solution.py:31
  91.7 1.3 %collective-permute-done.6.r1 = bf16[64,1536]{1,0:T(8,128)(2,1)S(1)} collective-permute-done((bf16[64,1536]{1,0:T(8,128)(2,1)S(1)}, bf16[64,1536]{1,0:T(8,128)(2,1)S(1)}, u32[]{:S(2)}, u32[]{:S(2)}) %collective-permute-start.6) | collective-permute-done | bytes 196640 | tf_op jit(solution)/shard_map/return/ppermute | solution.py:27
  93.1 0.3 collective-permute-done.7.r2
  93.3 3.4 %collective-permute-done.8.r3 = bf16[64,1536]{1,0:T(8,128)(2,1)S(1)} collective-permute-done((bf16[64,1536]{1,0:T(8,128)(2,1)S(1)}, bf16[64,1536]{1,0:T(8,128)(2,1)S(1)}, u32[]{:S(2)}, u32[]{:S(2)}) %collective-permute-start.8) | collective-permute-done | bytes 196640 | tf_op jit(solution)/shard_map/return/ppermute | solution.py:27
  96.7 0.7 broadcast_in_dim.8
  97.5 3.4 %all-to-all-start.3 = ((f32[8,32,256]{2,1,0:T(8,128)}), f32[8,32,256]{2,1,0:T(8,128)S(1)}, u32[]{:S(2)}, u32[]{:S(2)}) async-start(f32[8,32,256]{2,1,0:T(8,128)} %broadcast_in_dim.8), calls=%async_computation.3 | async-start | bytes 524288 | tf_op jit(solution)/shard_map/weight_sums/all_to_all | solution.py:31
  100.9 5.4 %collective-permute-start.9 = (bf16[64,128]{1,0:T(8,128)(2,1)S(1)}, bf16[64,128]{1,0:T(8,128)(2,1)S(1)}, u32[]{:S(2)}, u32[]{:S(2)}) collective-permute-start(bf16[64,128]{1,0:T(8,128)(2,1)S(1)} %get-tuple-element.33), channel_id=1, source_target_pairs={{0,252},{4,0},{8,4},{12,8},{16,12},{20,16},{24,20},{28,24},{32,28}... | collective-permute-start | bytes 49160 | tf_op jit(solution)/shard_map/return/ppermute | solution.py:27
  106.3 0.0 collective-permute-start.10
  106.3 0.8 collective-permute-start.11
  107.1 0.6 collective-permute-done.9.b0
  107.7 5.0 %collective-permute-done.10.b1 = bf16[64,128]{1,0:T(8,128)(2,1)S(1)} collective-permute-done((bf16[64,128]{1,0:T(8,128)(2,1)S(1)}, bf16[64,128]{1,0:T(8,128)(2,1)S(1)}, u32[]{:S(2)}, u32[]{:S(2)}) %collective-permute-start.10) | collective-permute-done | bytes 16416 | tf_op jit(solution)/shard_map/return/ppermute | solution.py:27
  112.8 0.0 collective-permute-done.11.b2
  112.8 2.5 %return.3 = f32[64,4096]{1,0:T(8,128)} custom-call(s32[1]{0:T(128)} %bitcast.place, bf16[64,1536]{1,0:T(8,128)(2,1)S(1)} %get-tuple-element.29.r0, bf16[64,1536]{1,0:T(8,128)(2,1)S(1)} %collective-permute-done.6.r1, bf16[64,1536]{1,0:T(8,128)(2,1)S(1)} %collective-permute-done.7.r2, bf16[64,1536]{1,0:T(8,128)(2,1)S(1)} %collective-permute-done.8.r3, ...), custom_call_target="tpu_custom_call" | custom-call | tf_op jit(solution)/shard_map/return/pallas_call | solution.py:342
  115.3 0.0 all-to-all-done.3
  115.3 0.6 slice.29
  115.9 0.7 slice.28
  (6 shorter events, 0.1 us)
Async XLA Ops:
  0.6 0.7 copy-start.5
  1.3 1.0 copy-start
  2.4 1.2 %copy-start.1 = (bf16[64,4096]{1,0:T(8,128)(2,1)S(1)}, bf16[64,4096]{1,0:T(8,128)(2,1)}, u32[]{:S(2)}) copy-start(bf16[64,4096]{1,0:T(8,128)(2,1)} %grad_in.3) | copy-start | bytes 1572868
  2.4 1.2 %copy-start.4 = (bf16[64,256]{1,0:T(8,128)(2,1)S(1)}, bf16[64,256]{1,0:T(8,128)(2,1)}, u32[]{:S(2)}) copy-start(bf16[64,256]{1,0:T(8,128)(2,1)} %w_out.1) | copy-start | bytes 98308
  3.6 0.9 copy-start.3
  5.1 23.8 %collective-permute-start = (bf16[64,3200]{1,0:T(8,128)(2,1)S(1)}, bf16[64,3200]{1,0:T(8,128)(2,1)S(1)}, u32[]{:S(2)}, u32[]{:S(2)}) collective-permute-start(bf16[64,3200]{1,0:T(8,128)(2,1)S(1)} %get-tuple-element.21), channel_id=1, source_target_pairs={{0,1},{1,2},{2,3},{3,0},{4,5},{5,6},{6,7},{7,4},{8,9},{9,10},{10,1... | collective-permute-start | bytes 1228808 | tf_op jit(solution)/shard_map/exchange/ppermute | solution.py:27
  7.4 21.5 %collective-permute-start.1 = (bf16[64,3200]{1,0:T(8,128)(2,1)S(1)}, bf16[64,3200]{1,0:T(8,128)(2,1)S(1)}, u32[]{:S(2)}, u32[]{:S(2)}) collective-permute-start(bf16[64,3200]{1,0:T(8,128)(2,1)S(1)} %get-tuple-element.22), channel_id=1, source_target_pairs={{0,2},{1,3},{2,0},{3,1},{4,6},{5,7},{6,4},{7,5},{8,10},{9,11},{10,... | collective-permute-start | bytes 1228808 | tf_op jit(solution)/shard_map/exchange/ppermute | solution.py:27
  8.1 20.9 %collective-permute-start.2 = (bf16[64,3200]{1,0:T(8,128)(2,1)S(1)}, bf16[64,3200]{1,0:T(8,128)(2,1)S(1)}, u32[]{:S(2)}, u32[]{:S(2)}) collective-permute-start(bf16[64,3200]{1,0:T(8,128)(2,1)S(1)} %get-tuple-element.23), channel_id=1, source_target_pairs={{0,3},{1,0},{2,1},{3,2},{4,7},{5,4},{6,5},{7,6},{8,11},{9,8},{10,9... | collective-permute-start | bytes 1228808 | tf_op jit(solution)/shard_map/exchange/ppermute | solution.py:27
  8.4 8.4 %collective-permute-start.3 = (bf16[64,128]{1,0:T(8,128)(2,1)S(1)}, bf16[64,128]{1,0:T(8,128)(2,1)S(1)}, u32[]{:S(2)}, u32[]{:S(2)}) collective-permute-start(bf16[64,128]{1,0:T(8,128)(2,1)S(1)} %get-tuple-element.37), channel_id=1, source_target_pairs={{0,4},{4,8},{8,12},{12,16},{16,20},{20,24},{24,28},{28,32},{32,36}... | collective-permute-start | bytes 49160 | tf_op jit(solution)/shard_map/border_rows/ppermute | solution.py:27
  8.5 8.8 %collective-permute-start.5 = (bf16[64,128]{1,0:T(8,128)(2,1)S(1)}, bf16[64,128]{1,0:T(8,128)(2,1)S(1)}, u32[]{:S(2)}, u32[]{:S(2)}) collective-permute-start(bf16[64,128]{1,0:T(8,128)(2,1)S(1)} %get-tuple-element.38), channel_id=1, source_target_pairs={{0,128},{4,132},{8,136},{12,140},{16,144},{20,148},{24,152},{28,15... | collective-permute-start | bytes 49160 | tf_op jit(solution)/shard_map/border_rows/ppermute | solution.py:27
  16.8 1.9 %collective-permute-start.4 = (bf16[64,128]{1,0:T(8,128)(2,1)S(1)}, bf16[64,128]{1,0:T(8,128)(2,1)S(1)}, u32[]{:S(2)}, u32[]{:S(2)}) collective-permute-start(bf16[64,128]{1,0:T(8,128)(2,1)S(1)} %get-tuple-element.39), channel_id=1, source_target_pairs={{0,252},{4,0},{8,4},{12,8},{16,12},{20,16},{24,20},{28,24},{32,28}... | collective-permute-start | bytes 49160 | tf_op jit(solution)/shard_map/border_rows/ppermute | solution.py:27
  18.8 10.2 %copy-start.2 = (s32[9,4096]{1,0:T(8,128)S(1)}, s32[9,4096]{1,0:T(8,128)}, u32[]{:S(2)}) copy-start(s32[9,4096]{1,0:T(8,128)} %neighbors.1) | copy-start | bytes 442372
  73.5 18.2 %all-to-all-start.2 = ((bf16[8,32,256]{2,1,0:T(8,128)(2,1)}), bf16[8,32,256]{2,1,0:T(8,128)(2,1)S(1)}, u32[]{:S(2)}, u32[]{:S(2)}) async-start(bf16[8,32,256]{2,1,0:T(8,128)(2,1)} %broadcast_in_dim.7), calls=%async_computation.2 | async-start | bytes 262144 | tf_op jit(solution)/shard_map/weight_sums/all_to_all | solution.py:31
  82.0 11.1 %collective-permute-start.6 = (bf16[64,1536]{1,0:T(8,128)(2,1)S(1)}, bf16[64,1536]{1,0:T(8,128)(2,1)S(1)}, u32[]{:S(2)}, u32[]{:S(2)}) collective-permute-start(bf16[64,1536]{1,0:T(8,128)(2,1)S(1)} %get-tuple-element.25), channel_id=1, source_target_pairs={{0,1},{1,2},{2,3},{3,0},{4,5},{5,6},{6,7},{7,4},{8,9},{9,10},{10,1... | collective-permute-start | bytes 589832 | tf_op jit(solution)/shard_map/return/ppermute | solution.py:27
  84.0 9.3 %collective-permute-start.7 = (bf16[64,1536]{1,0:T(8,128)(2,1)S(1)}, bf16[64,1536]{1,0:T(8,128)(2,1)S(1)}, u32[]{:S(2)}, u32[]{:S(2)}) collective-permute-start(bf16[64,1536]{1,0:T(8,128)(2,1)S(1)} %get-tuple-element.26), channel_id=1, source_target_pairs={{0,2},{1,3},{2,0},{3,1},{4,6},{5,7},{6,4},{7,5},{8,10},{9,11},{10,... | collective-permute-start | bytes 589832 | tf_op jit(solution)/shard_map/return/ppermute | solution.py:27
  85.1 11.6 %collective-permute-start.8 = (bf16[64,1536]{1,0:T(8,128)(2,1)S(1)}, bf16[64,1536]{1,0:T(8,128)(2,1)S(1)}, u32[]{:S(2)}, u32[]{:S(2)}) collective-permute-start(bf16[64,1536]{1,0:T(8,128)(2,1)S(1)} %get-tuple-element.27), channel_id=1, source_target_pairs={{0,3},{1,0},{2,1},{3,2},{4,7},{5,4},{6,5},{7,6},{8,11},{9,8},{10,9... | collective-permute-start | bytes 589832 | tf_op jit(solution)/shard_map/return/ppermute | solution.py:27
  97.5 17.8 %all-to-all-start.3 = ((f32[8,32,256]{2,1,0:T(8,128)}), f32[8,32,256]{2,1,0:T(8,128)S(1)}, u32[]{:S(2)}, u32[]{:S(2)}) async-start(f32[8,32,256]{2,1,0:T(8,128)} %broadcast_in_dim.8), calls=%async_computation.3 | async-start | bytes 524288 | tf_op jit(solution)/shard_map/weight_sums/all_to_all | solution.py:31
  100.9 6.8 %collective-permute-start.9 = (bf16[64,128]{1,0:T(8,128)(2,1)S(1)}, bf16[64,128]{1,0:T(8,128)(2,1)S(1)}, u32[]{:S(2)}, u32[]{:S(2)}) collective-permute-start(bf16[64,128]{1,0:T(8,128)(2,1)S(1)} %get-tuple-element.33), channel_id=1, source_target_pairs={{0,252},{4,0},{8,4},{12,8},{16,12},{20,16},{24,20},{28,24},{32,28}... | collective-permute-start | bytes 49160 | tf_op jit(solution)/shard_map/return/ppermute | solution.py:27
  106.3 6.5 %collective-permute-start.10 = (bf16[64,128]{1,0:T(8,128)(2,1)S(1)}, bf16[64,128]{1,0:T(8,128)(2,1)S(1)}, u32[]{:S(2)}, u32[]{:S(2)}) collective-permute-start(bf16[64,128]{1,0:T(8,128)(2,1)S(1)} %get-tuple-element.34), channel_id=1, source_target_pairs={{0,4},{4,8},{8,12},{12,16},{16,20},{20,24},{24,28},{28,32},{32,36}... | collective-permute-start | bytes 49160 | tf_op jit(solution)/shard_map/return/ppermute | solution.py:27
  106.3 6.5 %collective-permute-start.11 = (bf16[64,128]{1,0:T(8,128)(2,1)S(1)}, bf16[64,128]{1,0:T(8,128)(2,1)S(1)}, u32[]{:S(2)}, u32[]{:S(2)}) collective-permute-start(bf16[64,128]{1,0:T(8,128)(2,1)S(1)} %get-tuple-element.35), channel_id=1, source_target_pairs={{0,128},{4,132},{8,136},{12,140},{16,144},{20,148},{24,152},{28,15... | collective-permute-start | bytes 49160 | tf_op jit(solution)/shard_map/return/ppermute | solution.py:27
